TPU v7x, 32 devices: a whole 2x2x4 slice. The times are simulated.
32 devices in a mesh: runs: 2 (over y), area: 16 (over z, x, core).
Axes of the slice: x: 2, y: 2, z: 4, core: 2. Of those that a mesh axis runs over, the one named last changes fastest.
Arguments:
- spikes: int32 [8, 10, 6144], P('runs', None, 'area'), parts along dimension 0, may hold values 0 or 1
- weights: bfloat16 [1536, 384, 128], P('area'), may hold values from -0.625 to 0.625
- destination: int32 [1536, 1], P('area'), may hold values from 0 to 15; in each aligned block of 96 rows (0 to 95, 96 to 191, ...) at most 6 rows name the same one
- target_block: int32 [1536], P('area'), may hold values from 0 to 2
- delay_slot: int32 [1536], P('area'), may hold values from 0 to 3
- population: int32 [6144], P('area'), may hold values from 0 to 3
- leak_rate: float32 [6144], P('area'), may hold values from 0.3 to 0.95
- membrane_start: float32 [8, 6144], P('runs', 'area'), parts along dimension 0, may hold values from -6 to 6
- cycle_start: float32 [8, 4, 6144], P('runs', None, 'area'), parts along dimension 0, may hold values from -3 to 3
- history: float32 [64, 2, 8, 256], P('area', None, 'runs'), parts along dimension 2, may hold values from -1.2 to 1.2
- lfp_kernel: bfloat16 [384, 64, 2, 256], P(None, 'area'), may hold values from -0.375 to 0.375
Outputs:
- membrane: float32 [8, 6144], P('runs', 'area'), parts along dimension 0
- cycle_out: float32 [8, 4, 6144], P('runs', None, 'area'), parts along dimension 0
- lfp: float32 [384, 80], P('area', 'runs'), parts along dimension 1
There are 2 independent parts, one for each index of `runs`. A program takes and returns all parts, laid end to end along the dimension named above; an argument that names none is the same for every part. Nothing has to cross between parts.
Inputs may be any that keep to these rules, and one draw needn't show every extreme that they name: Of the 96 units of one device at most 6 have the same destination; in every draw some device sends exactly 6 units to one destination.
All inputs are finite; a program needn't handle non-finite values. No bound on the sum of `spikes` on one device may be relied on, other than what follows from the above.
Results may differ from a plain program's by a relative error of at most 0.0029.
Values may be sent and summed in bfloat16 or wider, within the bound.
No kernel may reach another device: no remote copies, remote signals or barrier semaphores. Data moves between devices by JAX's collectives and lax.ppermute only.
A program may use at most 64 MiB of HBM per device.

v0:
```python
import jax
import jax.numpy as jnp
from jax import lax
from jax.sharding import PartitionSpec as P


def arrivals_from(blocks_acc, cycle_start, step_count):
    delays = cycle_start.shape[1]
    trials = cycle_start.shape[0]
    total = jnp.zeros((blocks_acc.shape[0], trials, step_count + delays, 128), jnp.float32)
    for delay_index in range(delays):
        piece = blocks_acc[:, delay_index]
        total = total + jnp.pad(
            piece, ((0, 0), (0, 0), (delay_index + 1, delays - 1 - delay_index), (0, 0))
        )
    total = jnp.transpose(total, (1, 2, 0, 3)).reshape(trials, step_count + delays, -1)
    return total + jnp.pad(cycle_start, ((0, 0), (0, step_count), (0, 0)))


def build_lags(series, step_count, taps):
    windows = [series[..., step : step + taps][..., ::-1] for step in range(step_count)]
    stacked = jnp.stack(windows, axis=-1)
    lead = series.shape[:-2]
    order = tuple(range(len(lead))) + (len(lead) + 1, len(lead), len(lead) + 2)
    stacked = jnp.transpose(stacked, order)
    return stacked.reshape(-1, series.shape[-2] * step_count)


def body(
    spikes,
    weights,
    destination,
    target_block,
    delay_slot,
    population,
    leak_rate,
    membrane_start,
    cycle_start,
    history,
    lfp_kernel,
):
    area_count = lax.axis_size("area")
    unit_count = weights.shape[0]
    neurons_here = weights.shape[1]
    blocks = neurons_here // 128
    trials = spikes.shape[0]
    step_count = spikes.shape[1]
    row_count = trials * step_count
    delays = cycle_start.shape[1]
    channels = lfp_kernel.shape[0]
    pop_count = history.shape[0]
    taps = history.shape[3]
    capacity = max(2, (unit_count + area_count - 1) // area_count)
    spike_f = spikes.astype(jnp.float32)
    spike_rows = spikes.reshape(row_count, neurons_here).astype(jnp.bfloat16)
    payload = jnp.einsum(
        "rk,ukn->urn", spike_rows, weights, preferred_element_type=jnp.float32
    ).astype(jnp.bfloat16)
    target_dev = destination[:, 0]
    matching = target_dev[:, None] == target_dev[None, :]
    earlier = lax.broadcasted_iota(jnp.int32, (unit_count, unit_count), 0) > lax.broadcasted_iota(
        jnp.int32, (unit_count, unit_count), 1
    )
    position = jnp.sum(jnp.logical_and(matching, earlier).astype(jnp.int32), axis=1)
    send_slot = target_dev * capacity + position
    slot_code = target_block * delays + delay_slot + 1
    outgoing = jnp.zeros((area_count * capacity, trials, step_count, 128), jnp.bfloat16)
    outgoing = outgoing.at[send_slot].set(payload.reshape(unit_count, trials, step_count, 128))
    outgoing = outgoing.reshape(area_count, capacity, trials, step_count, 128)
    codes = jnp.zeros((area_count * capacity,), jnp.int32).at[send_slot].set(slot_code)
    codes = codes.reshape(area_count, capacity)
    pop_table = (population[:, None] == jnp.arange(pop_count, dtype=jnp.int32)[None, :]).astype(
        jnp.float32
    )
    pop_size = neurons_here / pop_count

    def signal(values):
        summed = jnp.dot(
            values.reshape(row_count, neurons_here),
            pop_table,
            precision=lax.Precision.HIGHEST,
            preferred_element_type=jnp.float32,
        )
        return (summed / pop_size).T.reshape(pop_count, trials, step_count)

    rate_fresh = signal(spike_f)
    incoming, codes_in = (
        lax.all_to_all(outgoing, "area", split_axis=0, concat_axis=0, tiled=True),
        lax.all_to_all(codes, "area", split_axis=0, concat_axis=0, tiled=True),
    )
    senders = incoming.shape[0] * incoming.shape[1]
    items = incoming.shape[2]
    flat = incoming.reshape(senders, items * step_count * 128)
    onehot = (
        codes_in.reshape(senders)[:, None]
        == jnp.arange(1, blocks * delays + 1, dtype=jnp.int32)[None, :]
    ).astype(jnp.bfloat16)
    summed = lax.dot_general(
        onehot, flat, (((0,), (0,)), ((), ())), preferred_element_type=jnp.float32
    )
    gathered = summed.reshape(blocks * delays, items, step_count, 128)
    blocks_acc = gathered.reshape(blocks, delays, trials, step_count, 128)
    arrivals = arrivals_from(blocks_acc, cycle_start, step_count)
    current = arrivals[:, :step_count]
    cycle_out = arrivals[:, step_count:]
    membrane = membrane_start
    for step in range(step_count):
        membrane = (leak_rate * membrane + current[:, step]) * (1.0 - spike_f[:, step])
    current_fresh = signal(current)
    fresh = jnp.stack([rate_fresh, current_fresh], axis=1)
    series = jnp.concatenate([history, fresh], axis=-1).astype(jnp.bfloat16)
    lagged = build_lags(series, step_count, taps)
    kernel_flat = lfp_kernel.reshape(channels, pop_count * 2 * taps)
    lfp = lax.psum_scatter(
        jnp.dot(kernel_flat, lagged, preferred_element_type=jnp.float32),
        "area",
        scatter_dimension=0,
        tiled=True,
    )
    return (membrane, cycle_out, lfp)


def solution(mesh):
    return jax.shard_map(
        body,
        mesh=mesh,
        in_specs=(
            P("runs", None, "area"),
            P("area", None, None),
            P("area", None),
            P("area"),
            P("area"),
            P("area"),
            P("area"),
            P("runs", "area"),
            P("runs", None, "area"),
            P("area", None, "runs", None),
            P(None, "area", None, None),
        ),
        out_specs=(P("runs", "area"), P("runs", None, "area"), P("area", "runs")),
        check_vma=False,
    )
```

profile of v0, /device:TPU:0, one launch (start us, length us, event | category | flops | bytes accessed | tf_op | source)
XLA Modules:
  0.0 134.4 jit_solution(2087363473931373412)
XLA Ops:
  0.6 0.9 convert_reduce_fusion
  1.5 0.7 fusion.53
  2.2 0.7 add_add_fusion.1
  2.9 0.9 scatter_custom_fusion
  3.8 0.7 all_to_all.9
  4.5 7.4 %all-to-all-start = ((s32[16,1,6]{2,1,0:T(1,128)}), s32[16,1,6]{2,1,0:T(1,128)S(1)}, u32[]{:S(2)}, u32[]{:S(2)}) async-start(s32[16,1,6]{2,1,0:T(1,128)} %bitcast.3), calls=%async_computation | async-start | bytes 16384 | tf_op jit(solution)/shard_map/all_to_all | solution.py:89
  11.8 0.9 fusion.57
  12.8 5.3 %fusion = bf16[96,40,128]{2,1,0:T(8,128)(2,1)S(1)} fusion(bf16[96,384,128]{2,1,0:T(8,128)(2,1)} %param.12, bf16[40,384,1]{1,0,2:T(8,128)(2,1)S(1)} %reshape.105), kind=kOutput, calls=%fused_computation.3 | convolution fusion | flops 377978880 | bytes 10450944 | tf_op jit(solution)/shard_map/rk,ukn->urn/dot_general | solution.py:56
  18.1 0.1 copy.131
  18.2 0.8 copy.132
  19.0 1.3 broadcast_in_dim.2
  20.2 11.8 %scatter_fusion = bf16[96,4,10,128]{3,1,2,0:T(4,128)(2,1)} fusion(bf16[96,4,10,128]{3,1,2,0:T(4,128)(2,1)} %broadcast_in_dim.2, s32[96]{0:T(128)S(1)} %fusion.53, bf16[96,4,10,128]{3,1,2,0:T(4,128)(2,1)S(1)} %copy.132), kind=kCustom, calls=%fused_computation.1 | custom fusion | bytes 2949504 | tf_op jit(solution)/shard_map/scatter | solution.py:68
  32.0 6.2 %all-to-all-start.1 = ((bf16[16,6,4,10,128]{4,2,3,1,0:T(4,128)(2,1)}), bf16[16,6,4,10,128]{4,2,3,1,0:T(4,128)(2,1)}, u32[]{:S(2)}, u32[]{:S(2)}) async-start(bf16[16,6,4,10,128]{4,2,3,1,0:T(4,128)(2,1)} %bitcast.8), calls=%async_computation.1 | async-start | bytes 1966080 | tf_op jit(solution)/shard_map/all_to_all | solution.py:88
  38.3 0.3 fusion.1
  38.6 0.1 stack_reshape.8
  38.8 0.2 rev.30
  39.0 1.2 reshape.88
  40.3 0.6 dynamic-slice
  41.5 0.5 broadcast.87
  42.1 0.7 reduce.3
  42.7 0.1 eq.53
  42.8 17.3 %all-to-all-done.1 = bf16[16,6,4,10,128]{4,2,3,1,0:T(4,128)(2,1)} async-done(((bf16[16,6,4,10,128]{4,2,3,1,0:T(4,128)(2,1)}), bf16[16,6,4,10,128]{4,2,3,1,0:T(4,128)(2,1)}, u32[]{:S(2)}, u32[]{:S(2)}) %all-to-all-start.1) | async-done | bytes 983072 | tf_op jit(solution)/shard_map/all_to_all | solution.py:88
  60.2 1.6 %copy.133 = bf16[16,6,4,10,128]{4,3,2,1,0:T(8,128)(2,1)S(1)} copy(bf16[16,6,4,10,128]{4,2,3,1,0:T(4,128)(2,1)} %all-to-all-done.1) | data formatting | bytes 1966080 | tf_op jit(solution)/shard_map/all_to_all | solution.py:88
  61.8 1.4 %reshape.83 = bf16[96,5120]{1,0:T(8,128)(2,1)} reshape(bf16[16,6,4,10,128]{4,3,2,1,0:T(8,128)(2,1)S(1)} %copy.133) | data formatting | bytes 1966080 | tf_op jit(solution)/shard_map/reshape | solution.py:93
  63.2 1.7 %copy.134 = bf16[5120,96]{1,0:T(8,128)(2,1)S(1)} copy(bf16[5120,96]{0,1:T(8,128)(2,1)} %bitcast.210) | data formatting | bytes 1966080 | tf_op jit(solution)/shard_map/dot_general | solution.py:98
  64.9 0.5 fusion.48
  65.4 0.2 fusion.56
  65.8 0.3 fusion.2
  66.1 0.1 stack_reshape.9
  66.2 0.1 maximum_maximum_fusion
  66.3 0.2 fusion.58
  66.4 0.2 rev.31
  66.7 0.2 rev.32
  66.9 0.2 rev.33
  67.2 0.2 rev.34
  67.4 0.2 rev.35
  67.7 0.2 rev.36
  67.9 0.2 rev.37
  68.2 0.2 rev.38
  68.4 0.2 rev.39
  68.9 0.1 copy.146
  69.0 0.1 reshape.87
  69.1 0.6 convolution_bitcast_fusion
  69.7 62.7 %all-reduce.5 = f32[384,40]{0,1:T(8,128)S(1)} all-reduce(f32[384,40]{0,1:T(8,128)S(1)} %convolution_bitcast_fusion), channel_id=2, replica_groups=mesh['runs'=2,'area'=16] {'area'}, use_global_device_ids=true, to_apply=%region_3.4.clone | all-reduce | flops 15360 | bytes 122880
  132.4 0.1 constant_dynamic-slice_fusion
  132.4 0.7 copy.148
  133.1 0.6 copy.147
  133.7 0.6 fusion.10
  (39 shorter events, 0.4 us)
Async XLA Ops:
  4.5 27.6 %all-to-all-start = ((s32[16,1,6]{2,1,0:T(1,128)}), s32[16,1,6]{2,1,0:T(1,128)S(1)}, u32[]{:S(2)}, u32[]{:S(2)}) async-start(s32[16,1,6]{2,1,0:T(1,128)} %bitcast.3), calls=%async_computation | async-start | bytes 16384 | tf_op jit(solution)/shard_map/all_to_all | solution.py:89
  32.0 6.2 %copy-start.2 = (f32[4,4,384]{2,1,0:T(4,128)S(1)}, f32[4,4,384]{2,1,0:T(4,128)}, u32[]{:S(2)}) copy-start(f32[4,4,384]{2,1,0:T(4,128)} %param.19) | copy-start | bytes 73732
  32.0 6.3 %copy-start.5 = (s32[384]{0:T(512)S(1)}, s32[384]{0:T(512)}, u32[]{:S(2)}) copy-start(s32[384]{0:T(512)} %param.16) | copy-start | bytes 4612
  32.0 6.7 %copy-start.1 = (f32[4,2,4,256]{3,2,1,0:T(4,128)S(1)}, f32[4,2,4,256]{3,2,1,0:T(4,128)}, u32[]{:S(2)}) copy-start(f32[4,2,4,256]{3,2,1,0:T(4,128)} %param.20) | copy-start | bytes 98308
  32.0 7.0 %copy-start = (bf16[384,4,2,256]{3,2,1,0:T(2,128)(2,1)S(1)}, bf16[384,4,2,256]{3,2,1,0:T(2,128)(2,1)}, u32[]{:S(2)}) copy-start(bf16[384,4,2,256]{3,2,1,0:T(2,128)(2,1)} %param.21) | copy-start | bytes 4718596
  32.0 28.1 %all-to-all-start.1 = ((bf16[16,6,4,10,128]{4,2,3,1,0:T(4,128)(2,1)}), bf16[16,6,4,10,128]{4,2,3,1,0:T(4,128)(2,1)}, u32[]{:S(2)}, u32[]{:S(2)}) async-start(bf16[16,6,4,10,128]{4,2,3,1,0:T(4,128)(2,1)} %bitcast.8), calls=%async_computation.1 | async-start | bytes 1966080 | tf_op jit(solution)/shard_map/all_to_all | solution.py:88
  39.0 1.3 copy-start.6
  67.7 66.1 %copy-start.3 = (f32[4,384]{1,0:T(4,128)S(1)}, f32[4,384]{1,0:T(4,128)}, u32[]{:S(2)}) copy-start(f32[4,384]{1,0:T(4,128)} %param.18) | copy-start | bytes 18436
  67.7 66.0 %copy-start.4 = (f32[384]{0:T(512)S(1)}, f32[384]{0:T(512)}, u32[]{:S(2)}) copy-start(f32[384]{0:T(512)} %param.17) | copy-start | bytes 4612
where the time goes:
time: 135 us; the launch traced here: 134 us
  blocking collectives  62.7 us (46%)
  local copies, waits for them, and re-layouts  27.5 us (20%)
  waiting for transfers between devices  17.3 us (13%)
  starting transfers between devices  13.5 us (10%)
  matrix products  6.9 us (5%)
  other arithmetic  4.66 us (3%)
  between operations  1.73 us (1%)
    unnamed x1, blocking collectives  62.7 us
    all_to_all x1, waiting for transfers between devices, body(): lax.all_to_all(outgoing, 'area', split_axis=0, concat_axis=0, tiled=True)  17.3 us
    scatter x1, local copies, waits for them, and re-layouts, body(): outgoing.at[send_slot]  11.8 us
    all_to_all x1, starting transfers between devices, body(): lax.all_to_all(codes, 'area', split_axis=0, concat_axis=0, tiled=True)  7.36 us
    all_to_all x1, starting transfers between devices, body(): lax.all_to_all(outgoing, 'area', split_axis=0, concat_axis=0, tiled=True)  6.18 us
    dot_general x1, matrix products, body(): jnp.einsum('rk,ukn->urn', spike_rows, weights, preferred_element_type=jnp...  5.26 us
  transfers between devices with their start and end apart: 2, of which 1 were waited for; matrix products, arithmetic and copies ran while one was open for 18% of the time, Pallas kernels for 0%

commit v1 on v0

v1 whole, which is shorter than its diff:
```python
import functools

import jax
import jax.numpy as jnp
from jax import lax
from jax.experimental import pallas as pl
from jax.experimental.pallas import tpu as pltpu
from jax.sharding import PartitionSpec as P

BF16, F32 = jnp.bfloat16, jnp.float32


def chunk_of(unit_count):
    for size in (8, 6, 4, 3, 2):
        if unit_count % size == 0:
            return size
    return 1


def payload_kernel(
    destination, target_block, delay_slot, spikes, weights, keep, send, held, lagged, plain, sems
):
    trials, steps, neurons = spikes.shape
    unit_count = weights.shape[0]
    delays = lagged.shape[0]
    blocks = neurons // 128
    rows = keep.shape[1]
    chunk = held.shape[0] // sems.shape[0]
    chunks = unit_count // chunk

    def copy(index):
        part = pl.ds(index * chunk, chunk)
        return pltpu.make_async_copy(weights.at[part], held.at[part], sems.at[index])

    for index in range(chunks):
        copy(index).start()
    keep[...] = jnp.zeros_like(keep)
    send[...] = jnp.zeros_like(send)
    plain[...] = jnp.zeros_like(plain)
    front = trials * delays
    for trial in range(trials):
        for step in range(steps):
            plain[front + step * trials + trial, :] = spikes[trial, step, :].astype(F32)
    lagged[...] = jnp.zeros_like(lagged)
    for delay in range(delays):
        start = front - trials * (delay + 1)
        lagged[delay, 0:rows, :] = plain[start : start + rows, :].astype(BF16)
    me = lax.axis_index("area")

    def some(index, _):
        copy(index).wait()
        for inner in range(chunk):
            unit = index * chunk + inner
            device = lax.bitwise_xor(destination[unit, 0], me)
            place = (device // 2) * blocks + target_block[unit]
            value = jnp.dot(lagged[delay_slot[unit]], held[unit], preferred_element_type=F32)
            value = value[0:rows].astype(BF16).astype(F32)

            @pl.when(device % 2 == 0)
            def _():
                keep[place] += value

            @pl.when(device % 2 == 1)
            def _():
                send[place] += value

        return 0

    lax.fori_loop(0, chunks, some, 0)


def payload_sums(spikes, weights, destination, target_block, delay_slot, area_count, delays):
    trials, steps, neurons = spikes.shape
    unit_count = weights.shape[0]
    blocks = neurons // 128
    rows = trials * (steps + delays)
    padded = -(-rows // 16) * 16
    chunk = chunk_of(unit_count)
    half = jax.ShapeDtypeStruct((area_count // 2 * blocks, rows, 128), F32)
    smem = pl.BlockSpec(memory_space=pltpu.SMEM)
    vmem = pl.BlockSpec(memory_space=pltpu.VMEM)
    front = trials * delays
    return pl.pallas_call(
        payload_kernel,
        out_shape=(half, half),
        in_specs=[smem, smem, smem, vmem, pl.BlockSpec(memory_space=pl.ANY)],
        out_specs=(vmem, vmem),
        scratch_shapes=[
            pltpu.VMEM(weights.shape, BF16),
            pltpu.VMEM((delays, padded, neurons), BF16),
            pltpu.VMEM((front + rows, neurons), F32),
            pltpu.SemaphoreType.DMA((unit_count // chunk,)),
        ],
        compiler_params=pltpu.CompilerParams(vmem_limit_bytes=40 * 2**20),
        cost_estimate=pl.CostEstimate(
            flops=2 * unit_count * rows * neurons * 128,
            bytes_accessed=unit_count * neurons * 256,
            transcendentals=0,
        ),
        name="payload",
    )(destination, target_block, delay_slot, spikes, weights)


def swap(values, bit, area_count):
    return lax.ppermute(values, "area", [(i, i ^ bit) for i in range(area_count)])


def halve(values, bit_dim, narrow):
    keep = lax.index_in_dim(values, 0, bit_dim, keepdims=False)
    send = lax.index_in_dim(values, 1, bit_dim, keepdims=False)
    return keep, send.astype(BF16) if narrow else send


def scatter_sum(values, bits, direct, area_count, narrow):
    lead = values.shape[1:]
    for bit in bits:
        count = values.shape[0]
        keep, send = halve(values.reshape((count // 2, 2) + lead), 1, narrow)
        values = keep + swap(send, bit, area_count).astype(F32)
    total = values[0]
    for index, bit in enumerate(direct, 1):
        send = values[index]
        send = send.astype(BF16) if narrow else send
        total = total + swap(send, bit, area_count).astype(F32)
    return total


def lag_rows(series, step_count, taps):
    windows = [series[..., step : step + taps][..., ::-1] for step in range(step_count)]
    stacked = jnp.stack(windows, axis=-1)
    lead = series.shape[:-2]
    order = tuple(range(len(lead))) + (len(lead) + 1, len(lead), len(lead) + 2)
    stacked = jnp.transpose(stacked, order)
    return stacked.reshape(-1, series.shape[-2] * step_count)


def body(
    spikes,
    weights,
    destination,
    target_block,
    delay_slot,
    population,
    leak_rate,
    membrane_start,
    cycle_start,
    history,
    lfp_kernel,
):
    area_count = lax.axis_size("area")
    neurons_here = weights.shape[1]
    blocks = neurons_here // 128
    trials, step_count = spikes.shape[:2]
    row_count = trials * step_count
    delays = cycle_start.shape[1]
    channels = lfp_kernel.shape[0]
    pop_count = history.shape[0]
    taps = history.shape[3]
    me = lax.axis_index("area")
    span = step_count + delays

    keep, send = payload_sums(
        spikes, weights, destination, target_block, delay_slot, area_count, delays
    )

    spike_f = spikes.astype(F32)
    pop_table = (population[:, None] == jnp.arange(pop_count, dtype=jnp.int32)[None, :]).astype(F32)
    pop_size = neurons_here / pop_count

    def signal(values):
        summed = jnp.dot(
            values.reshape(-1, neurons_here),
            pop_table,
            precision=lax.Precision.HIGHEST,
            preferred_element_type=F32,
        )
        return (summed / pop_size).T.reshape(pop_count, trials, -1)

    rate_fresh = signal(spike_f)
    fresh = jnp.stack([rate_fresh, jnp.zeros_like(rate_fresh)], axis=1)
    series = jnp.concatenate([history, fresh], axis=-1).astype(BF16)
    known = jnp.dot(
        lfp_kernel.reshape(channels, -1),
        lag_rows(series, step_count, taps),
        preferred_element_type=F32,
    )
    recent = lfp_kernel[:, :, 1, : step_count - 1].reshape(channels, -1)

    high = [1 << index for index in range(1, area_count.bit_length() - 1)]
    bits, last = high[:-2], high[-2:]
    direct = [last[0], last[1], last[0] + last[1]]
    summed = keep + swap(send, 1, area_count)
    summed = summed.reshape((area_count // 2, blocks, span * trials, 128))
    summed = scatter_sum(summed, bits, direct, area_count, True)

    arrivals = jnp.transpose(summed.reshape(blocks, span, trials, 128), (2, 1, 0, 3))
    arrivals = arrivals.reshape(trials, span, neurons_here)
    arrivals = arrivals + jnp.pad(cycle_start, ((0, 0), (0, step_count), (0, 0)))
    current = arrivals[:, :step_count]
    cycle_out = arrivals[:, step_count:]
    membrane = membrane_start
    for step in range(step_count):
        membrane = (leak_rate * membrane + current[:, step]) * (1.0 - spike_f[:, step])

    current_fresh = signal(current[:, : step_count - 1]).astype(BF16)
    padded = jnp.pad(current_fresh, ((0, 0), (0, 0), (step_count - 1, 0)))
    partial = known + jnp.dot(
        recent, lag_rows(padded, step_count, step_count - 1), preferred_element_type=F32
    )

    share = channels // area_count
    partial = partial.reshape(area_count, share, row_count)
    partial = partial[jnp.bitwise_xor(jnp.arange(area_count), me)]
    lfp = scatter_sum(partial, [1] + bits, direct, area_count, False)
    return (membrane, cycle_out, lfp)


def solution(mesh):
    return jax.shard_map(
        body,
        mesh=mesh,
        in_specs=(
            P("runs", None, "area"),
            P("area", None, None),
            P("area", None),
            P("area"),
            P("area"),
            P("area"),
            P("area"),
            P("runs", "area"),
            P("runs", None, "area"),
            P("area", None, "runs", None),
            P(None, "area", None, None),
        ),
        out_specs=(P("runs", "area"), P("runs", None, "area"), P("area", "runs")),
        check_vma=False,
    )
```

time: 135 us -> 67.3 us (0.50)
  blocking collectives: 62.7 us -> 0 us
  Pallas kernels: 0 us -> 16.9 us
  local copies, waits for them, and re-layouts: 27.5 us -> 16.9 us
  matrix products: 6.9 us -> 1.35 us
  waiting for transfers between devices: 17.3 us -> 14.3 us
  other arithmetic: 4.66 us -> 2.74 us
    unnamed x1 -> x0, blocking collectives: 62.7 us -> none
    all_to_all x2 -> x0, waiting for transfers between devices: 17.3 us -> none  [the longest x1 17.3 us: body(): lax.all_to_all(outgoing, 'area', split_axis=0, concat_axis=0, tiled=True)]
    pallas_call x0 -> x1, Pallas kernels: none -> 16.9 us  [payload_sums(): pl.pallas_call(payload_kernel, out_shape=(half, half), in_specs=[smem, sm...]
    ppermute x0 -> x10, waiting for transfers between devices: none -> 14.3 us  [swap(): lax.ppermute(values, 'area', [(i, i ^ bit) for i in range(area_count)])]
    ppermute x0 -> x10, starting transfers between devices: none -> 13.7 us  [swap(): lax.ppermute(values, 'area', [(i, i ^ bit) for i in range(area_count)])]
    all_to_all x2 -> x0, starting transfers between devices: 13.5 us -> none  [the longest x1 7.36 us: body(): lax.all_to_all(codes, 'area', split_axis=0, concat_axis=0, tiled=True)]
    scatter x2 -> x0, local copies, waits for them, and re-layouts: 12.7 us -> none  [the longest x1 11.8 us: body(): outgoing.at[send_slot]]
    dot_general x5 -> x4, matrix products: 6.9 us -> 1.35 us  [the longest x2 0.59 us: signal(): jnp.dot(values.reshape(-1, neurons_here), pop_table, precision=lax.Precis...]
  transfers between devices with their start and end apart: 2 -> 10, of which waited for: 1 -> 6; matrix products, arithmetic and copies ran while one was open for 18% -> 14% of each run, Pallas kernels for 0% -> 0%
where the time goes in v1:
time: 67.3 us; the launch traced here: 66.9 us
  local copies, waits for them, and re-layouts  16.9 us (25%)
  Pallas kernels  16.9 us (25%)
  waiting for transfers between devices  14.3 us (21%)
  starting transfers between devices  13.7 us (20%)
  other arithmetic  2.74 us (4%)
  matrix products  1.35 us (2%)
  between operations  1.14 us (2%)
    pallas_call x1, Pallas kernels, payload_sums(): pl.pallas_call(payload_kernel, out_shape=(half, half), in_specs=[smem, sm...  16.9 us
    ppermute x10, waiting for transfers between devices, swap(): lax.ppermute(values, 'area', [(i, i ^ bit) for i in range(area_count)])  14.3 us
    ppermute x10, starting transfers between devices, swap(): lax.ppermute(values, 'area', [(i, i ^ bit) for i in range(area_count)])  13.7 us
    unnamed x42, local copies, waits for them, and re-layouts  7.47 us
    rev x19, local copies, waits for them, and re-layouts, lag_rows(): series[..., step:step + taps][..., ::-1]  3.28 us
    reshape x1, local copies, waits for them, and re-layouts, body(): lfp_kernel.reshape(channels, -1)  2.87 us
  transfers between devices with their start and end apart: 10, of which 6 were waited for; matrix products, arithmetic and copies ran while one was open for 14% of the time, Pallas kernels for 0%

profile of v1, /device:TPU:0, one launch (start us, length us, event | category | flops | bytes accessed | tf_op | source)
XLA Modules:
  0.0 66.9 jit_solution(5628060421329272065)
XLA Ops:
  0.6 0.8 %copy.54.spikes = s32[4,10,384]{2,1,0:T(8,128)S(1)} copy(s32[4,10,384]{2,0,1:T(4,128)} %param.11) | data formatting | bytes 122880 | tf_op args[0]
  1.5 0.8 %copy.53.destination = s32[96,1]{1,0:T(8,128)S(1)} copy(s32[96,1]{0,1:T(1,128)} %param.13) | data formatting | bytes 768 | tf_op args[2]
  2.2 3.7 %copy-done = bf16[96,384,128]{2,1,0:T(8,128)(2,1)S(1)} copy-done((bf16[96,384,128]{2,1,0:T(8,128)(2,1)S(1)}, bf16[96,384,128]{2,1,0:T(8,128)(2,1)}, u32[]{:S(2)}) %copy-start) | copy-done | bytes 9437208
  5.9 0.7 copy-done.1
  6.6 0.7 copy-done.2
  7.2 16.9 %payload.1 = (f32[24,56,128]{2,1,0:T(8,128)S(1)}, f32[24,56,128]{2,1,0:T(8,128)S(1)}) custom-call(s32[96,1]{1,0:T(8,128)S(1)} %copy.53.destination, s32[96]{0:T(128)S(1)} %copy-done.1, s32[96]{0:T(128)S(1)} %copy-done.2, s32[4,10,384]{2,1,0:T(8,128)S(1)} %copy.54.spikes, bf16[96,384,128]{2,1,0:T(8,128)(2,1)S(1)} %copy-done), custom_call_target="tpu_custom_call" | custom-call | flops 528482304 | bytes 9437184 | tf_op jit(solution)/shard_map/payload/pallas_call | solution.py:83
  24.1 0.5 collective-permute-start
  24.7 0.3 fusion.1
  25.2 0.2 rev.58
  25.4 0.2 fusion.62
  25.6 0.2 rev.59
  25.9 0.2 rev.60
  26.1 0.2 rev.61
  26.3 0.2 rev.62
  26.6 0.2 rev.63
  26.8 0.2 rev.64
  27.1 0.2 rev.65
  27.3 0.2 rev.66
  27.6 0.2 rev.67
  28.0 0.1 copy.60
  28.1 0.1 reshape.83
  28.2 2.9 %reshape.84 = bf16[384,2048]{1,0:T(8,128)(2,1)S(1)} reshape(bf16[384,4,2,256]{3,2,1,0:T(2,128)(2,1)} %param.21) | data formatting | bytes 3145728 | tf_op jit(solution)/shard_map/reshape | solution.py:183
  31.1 0.6 fusion.63
  31.7 1.3 %add.85 = f32[24,56,128]{2,1,0:T(8,128)S(1)} add(f32[24,56,128]{2,1,0:T(8,128)S(1)} %get-tuple-element.5, f32[24,56,128]{2,1,0:T(8,128)} %collective-permute-done) | non-fusion elementwise | flops 172032 | bytes 2064384 | tf_op jit(solution)/shard_map/add | solution.py:192
  33.1 2.6 %collective-permute-start.1 = (bf16[4,3,56,128]{3,2,1,0:T(8,128)(2,1)S(1)}, bf16[4,3,56,128]{3,2,1,0:T(8,128)(2,1)S(1)}, u32[]{:S(2)}, u32[]{:S(2)}) collective-permute-start(bf16[4,3,56,128]{3,2,1,0:T(8,128)(2,1)S(1)} %fusion.5), channel_id=1, source_target_pairs={{0,2},{1,3},{2,0},{3,1},{4,6},{5,7},{6,4},{7,5},{8,10},{9,11},{10,... | collective-permute-start | bytes 516104 | tf_op jit(solution)/shard_map/ppermute | solution.py:105
  35.6 5.0 %collective-permute-done.1 = bf16[4,3,56,128]{3,2,1,0:T(8,128)(2,1)S(1)} collective-permute-done((bf16[4,3,56,128]{3,2,1,0:T(8,128)(2,1)S(1)}, bf16[4,3,56,128]{3,2,1,0:T(8,128)(2,1)S(1)}, u32[]{:S(2)}, u32[]{:S(2)}) %collective-permute-start.1) | collective-permute-done | bytes 172064 | tf_op jit(solution)/shard_map/ppermute | solution.py:105
  40.7 1.9 %collective-permute-start.2 = (bf16[3,56,128]{2,1,0:T(8,128)(2,1)S(1)}, bf16[3,56,128]{2,1,0:T(8,128)(2,1)S(1)}, u32[]{:S(2)}, u32[]{:S(2)}) collective-permute-start(bf16[3,56,128]{2,1,0:T(8,128)(2,1)S(1)} %get-tuple-element.15), channel_id=1, source_target_pairs={{0,4},{1,5},{2,6},{3,7},{4,0},{5,1},{6,2},{7,3},{8,12},{9,13},{10,... | collective-permute-start | bytes 129032 | tf_op jit(solution)/shard_map/ppermute | solution.py:105
  42.6 2.6 %collective-permute-start.3 = (bf16[3,56,128]{2,1,0:T(8,128)(2,1)S(1)}, bf16[3,56,128]{2,1,0:T(8,128)(2,1)S(1)}, u32[]{:S(2)}, u32[]{:S(2)}) collective-permute-start(bf16[3,56,128]{2,1,0:T(8,128)(2,1)S(1)} %get-tuple-element.17), channel_id=1, source_target_pairs={{0,8},{1,9},{2,10},{3,11},{4,12},{5,13},{6,14},{7,15},{8,0},{9,1},... | collective-permute-start | bytes 129032 | tf_op jit(solution)/shard_map/ppermute | solution.py:105
  45.2 0.8 %slice.229 = bf16[384,4,1,9]{3,2,1,0:T(2,128)(2,1)S(1)} slice(bf16[384,4,2,256]{3,2,1,0:T(2,128)(2,1)S(1)} %copy-done.3), slice={[0:384], [0:4], [1:2], [0:9]} | slice | bytes 55296 | tf_op jit(solution)/shard_map/slice | solution.py:187
  46.1 0.5 copy.63
  46.6 1.6 %collective-permute-done.3 = bf16[3,56,128]{2,1,0:T(8,128)(2,1)S(1)} collective-permute-done((bf16[3,56,128]{2,1,0:T(8,128)(2,1)S(1)}, bf16[3,56,128]{2,1,0:T(8,128)(2,1)S(1)}, u32[]{:S(2)}, u32[]{:S(2)}) %collective-permute-start.3) | collective-permute-done | bytes 43040 | tf_op jit(solution)/shard_map/ppermute | solution.py:105
  48.2 2.8 %collective-permute-done.4 = bf16[3,56,128]{2,1,0:T(8,128)(2,1)S(1)} collective-permute-done((bf16[3,56,128]{2,1,0:T(8,128)(2,1)S(1)}, bf16[3,56,128]{2,1,0:T(8,128)(2,1)S(1)}, u32[]{:S(2)}, u32[]{:S(2)}) %collective-permute-start.4) | collective-permute-done | bytes 43040 | tf_op jit(solution)/shard_map/ppermute | solution.py:105
  51.3 0.3 fusion.2
  51.7 0.1 pad_slice_fusion
  51.8 0.1 rev.76
  52.8 0.2 copy.62
  53.2 0.2 fusion
  53.3 0.1 copy.64
  53.5 0.6 gather_fusion
  54.1 1.3 %collective-permute-done.5 = f32[8,24,40]{2,1,0:T(8,128)S(1)} collective-permute-done((f32[8,24,40]{2,1,0:T(8,128)S(1)}, f32[8,24,40]{2,1,0:T(8,128)S(1)}, u32[]{:S(2)}, u32[]{:S(2)}) %collective-permute-start.5) | collective-permute-done | bytes 30752 | tf_op jit(solution)/shard_map/ppermute | solution.py:105
  55.5 1.6 %collective-permute-start.6 = (f32[4,24,40]{2,1,0:T(8,128)S(1)}, f32[4,24,40]{2,1,0:T(8,128)S(1)}, u32[]{:S(2)}, u32[]{:S(2)}) collective-permute-start(f32[4,24,40]{2,1,0:T(8,128)S(1)} %slice_bitcast_fusion.4), channel_id=1, source_target_pairs={{0,2},{1,3},{2,0},{3,1},{4,6},{5,7},{6,4},{7,5},{8,10},{9,11},{10,... | collective-permute-start | bytes 46088 | tf_op jit(solution)/shard_map/ppermute | solution.py:105
  57.0 2.6 %collective-permute-done.6 = f32[4,24,40]{2,1,0:T(8,128)S(1)} collective-permute-done((f32[4,24,40]{2,1,0:T(8,128)S(1)}, f32[4,24,40]{2,1,0:T(8,128)S(1)}, u32[]{:S(2)}, u32[]{:S(2)}) %collective-permute-start.6) | collective-permute-done | bytes 15392 | tf_op jit(solution)/shard_map/ppermute | solution.py:105
  59.7 1.1 %collective-permute-start.8 = (f32[24,40]{1,0:T(8,128)S(1)}, f32[24,40]{1,0:T(8,128)S(1)}, u32[]{:S(2)}, u32[]{:S(2)}) collective-permute-start(f32[24,40]{1,0:T(8,128)S(1)} %get-tuple-element.20), channel_id=1, source_target_pairs={{0,8},{1,9},{2,10},{3,11},{4,12},{5,13},{6,14},{7,15},{8,0},{9,1},... | collective-permute-start | bytes 11528 | tf_op jit(solution)/shard_map/ppermute | solution.py:105
  60.8 3.3 %collective-permute-start.9 = (f32[24,40]{1,0:T(8,128)S(1)}, f32[24,40]{1,0:T(8,128)S(1)}, u32[]{:S(2)}, u32[]{:S(2)}) collective-permute-start(f32[24,40]{1,0:T(8,128)S(1)} %get-tuple-element.19), channel_id=1, source_target_pairs={{0,12},{1,13},{2,14},{3,15},{4,8},{5,9},{6,10},{7,11},{8,4},{9,5},... | collective-permute-start | bytes 11528 | tf_op jit(solution)/shard_map/ppermute | solution.py:105
  64.1 0.6 fusion.21
  64.7 0.6 copy.68
  65.4 1.0 %collective-permute-done.9 = f32[24,40]{1,0:T(8,128)S(1)} collective-permute-done((f32[24,40]{1,0:T(8,128)S(1)}, f32[24,40]{1,0:T(8,128)S(1)}, u32[]{:S(2)}, u32[]{:S(2)}) %collective-permute-start.9) | collective-permute-done | bytes 3872 | tf_op jit(solution)/shard_map/ppermute | solution.py:105
  66.3 0.6 fusion.19
  (80 shorter events, 1.9 us)
Async XLA Ops:
  2.2 3.7 %copy-start = (bf16[96,384,128]{2,1,0:T(8,128)(2,1)S(1)}, bf16[96,384,128]{2,1,0:T(8,128)(2,1)}, u32[]{:S(2)}) copy-start(bf16[96,384,128]{2,1,0:T(8,128)(2,1)} %weights.1) | copy-start | bytes 28311556
  5.9 0.7 copy-start.1
  6.6 0.7 copy-start.2
  7.2 17.4 %copy-start.4 = (s32[4,10,384]{2,0,1:T(4,128)S(1)}, s32[4,10,384]{2,0,1:T(4,128)}, u32[]{:S(2)}) copy-start(s32[4,10,384]{2,0,1:T(4,128)} %param.11) | copy-start | bytes 184324
  7.2 17.5 %copy-start.9 = (s32[384]{0:T(512)S(1)}, s32[384]{0:T(512)}, u32[]{:S(2)}) copy-start(s32[384]{0:T(512)} %param.16) | copy-start | bytes 4612
  7.2 17.9 %copy-start.5 = (f32[4,2,4,256]{3,2,1,0:T(4,128)S(1)}, f32[4,2,4,256]{3,2,1,0:T(4,128)}, u32[]{:S(2)}) copy-start(f32[4,2,4,256]{3,2,1,0:T(4,128)} %param.20) | copy-start | bytes 98308
  24.1 7.6 %collective-permute-start = (f32[24,56,128]{2,1,0:T(8,128)S(1)}, f32[24,56,128]{2,1,0:T(8,128)}, u32[]{:S(2)}, u32[]{:S(2)}) collective-permute-start(f32[24,56,128]{2,1,0:T(8,128)S(1)} %get-tuple-element.6), channel_id=1, source_target_pairs={{0,1},{1,0},{2,3},{3,2},{4,5},{5,4},{6,7},{7,6},{8,9},{9,8},{10,11... | collective-permute-start | bytes 2064392 | tf_op jit(solution)/shard_map/ppermute | solution.py:105
  31.7 13.5 %copy-start.3 = (bf16[384,4,2,256]{3,2,1,0:T(2,128)(2,1)S(1)}, bf16[384,4,2,256]{3,2,1,0:T(2,128)(2,1)}, u32[]{:S(2)}) copy-start(bf16[384,4,2,256]{3,2,1,0:T(2,128)(2,1)} %param.21) | copy-start | bytes 4718596
  33.0 13.1 %copy-start.6 = (f32[4,4,384]{2,1,0:T(4,128)S(1)}, f32[4,4,384]{2,1,0:T(4,128)}, u32[]{:S(2)}) copy-start(f32[4,4,384]{2,1,0:T(4,128)} %param.19) | copy-start | bytes 73732
  33.1 7.6 %collective-permute-start.1 = (bf16[4,3,56,128]{3,2,1,0:T(8,128)(2,1)S(1)}, bf16[4,3,56,128]{3,2,1,0:T(8,128)(2,1)S(1)}, u32[]{:S(2)}, u32[]{:S(2)}) collective-permute-start(bf16[4,3,56,128]{3,2,1,0:T(8,128)(2,1)S(1)} %fusion.5), channel_id=1, source_target_pairs={{0,2},{1,3},{2,0},{3,1},{4,6},{5,7},{6,4},{7,5},{8,10},{9,11},{10,... | collective-permute-start | bytes 516104 | tf_op jit(solution)/shard_map/ppermute | solution.py:105
  40.7 5.9 %collective-permute-start.2 = (bf16[3,56,128]{2,1,0:T(8,128)(2,1)S(1)}, bf16[3,56,128]{2,1,0:T(8,128)(2,1)S(1)}, u32[]{:S(2)}, u32[]{:S(2)}) collective-permute-start(bf16[3,56,128]{2,1,0:T(8,128)(2,1)S(1)} %get-tuple-element.15), channel_id=1, source_target_pairs={{0,4},{1,5},{2,6},{3,7},{4,0},{5,1},{6,2},{7,3},{8,12},{9,13},{10,... | collective-permute-start | bytes 129032 | tf_op jit(solution)/shard_map/ppermute | solution.py:105
  42.6 5.6 %collective-permute-start.3 = (bf16[3,56,128]{2,1,0:T(8,128)(2,1)S(1)}, bf16[3,56,128]{2,1,0:T(8,128)(2,1)S(1)}, u32[]{:S(2)}, u32[]{:S(2)}) collective-permute-start(bf16[3,56,128]{2,1,0:T(8,128)(2,1)S(1)} %get-tuple-element.17), channel_id=1, source_target_pairs={{0,8},{1,9},{2,10},{3,11},{4,12},{5,13},{6,14},{7,15},{8,0},{9,1},... | collective-permute-start | bytes 129032 | tf_op jit(solution)/shard_map/ppermute | solution.py:105
  45.2 5.8 %collective-permute-start.4 = (bf16[3,56,128]{2,1,0:T(8,128)(2,1)S(1)}, bf16[3,56,128]{2,1,0:T(8,128)(2,1)S(1)}, u32[]{:S(2)}, u32[]{:S(2)}) collective-permute-start(bf16[3,56,128]{2,1,0:T(8,128)(2,1)S(1)} %get-tuple-element.16), channel_id=1, source_target_pairs={{0,12},{1,13},{2,14},{3,15},{4,8},{5,9},{6,10},{7,11},{8,4},{9,5},... | collective-permute-start | bytes 129032 | tf_op jit(solution)/shard_map/ppermute | solution.py:105
  51.1 13.0 %copy-start.7 = (f32[4,384]{1,0:T(4,128)S(1)}, f32[4,384]{1,0:T(4,128)}, u32[]{:S(2)}) copy-start(f32[4,384]{1,0:T(4,128)} %param.18) | copy-start | bytes 18436
  51.1 13.0 %copy-start.8 = (f32[384]{0:T(512)S(1)}, f32[384]{0:T(512)}, u32[]{:S(2)}) copy-start(f32[384]{0:T(512)} %param.17) | copy-start | bytes 4612
  54.1 1.4 %collective-permute-start.5 = (f32[8,24,40]{2,1,0:T(8,128)S(1)}, f32[8,24,40]{2,1,0:T(8,128)S(1)}, u32[]{:S(2)}, u32[]{:S(2)}) collective-permute-start(f32[8,24,40]{2,1,0:T(8,128)S(1)} %slice_bitcast_fusion.1), channel_id=1, source_target_pairs={{0,1},{1,0},{2,3},{3,2},{4,5},{5,4},{6,7},{7,6},{8,9},{9,8},{10,11... | collective-permute-start | bytes 92168 | tf_op jit(solution)/shard_map/ppermute | solution.py:105
  55.5 4.2 %collective-permute-start.6 = (f32[4,24,40]{2,1,0:T(8,128)S(1)}, f32[4,24,40]{2,1,0:T(8,128)S(1)}, u32[]{:S(2)}, u32[]{:S(2)}) collective-permute-start(f32[4,24,40]{2,1,0:T(8,128)S(1)} %slice_bitcast_fusion.4), channel_id=1, source_target_pairs={{0,2},{1,3},{2,0},{3,1},{4,6},{5,7},{6,4},{7,5},{8,10},{9,11},{10,... | collective-permute-start | bytes 46088 | tf_op jit(solution)/shard_map/ppermute | solution.py:105
  59.6 5.7 %collective-permute-start.7 = (f32[24,40]{1,0:T(8,128)S(1)}, f32[24,40]{1,0:T(8,128)S(1)}, u32[]{:S(2)}, u32[]{:S(2)}) collective-permute-start(f32[24,40]{1,0:T(8,128)S(1)} %get-tuple-element.18), channel_id=1, source_target_pairs={{0,4},{1,5},{2,6},{3,7},{4,0},{5,1},{6,2},{7,3},{8,12},{9,13},{10,... | collective-permute-start | bytes 11528 | tf_op jit(solution)/shard_map/ppermute | solution.py:105
  59.7 5.6 %collective-permute-start.8 = (f32[24,40]{1,0:T(8,128)S(1)}, f32[24,40]{1,0:T(8,128)S(1)}, u32[]{:S(2)}, u32[]{:S(2)}) collective-permute-start(f32[24,40]{1,0:T(8,128)S(1)} %get-tuple-element.20), channel_id=1, source_target_pairs={{0,8},{1,9},{2,10},{3,11},{4,12},{5,13},{6,14},{7,15},{8,0},{9,1},... | collective-permute-start | bytes 11528 | tf_op jit(solution)/shard_map/ppermute | solution.py:105
  60.8 5.5 %collective-permute-start.9 = (f32[24,40]{1,0:T(8,128)S(1)}, f32[24,40]{1,0:T(8,128)S(1)}, u32[]{:S(2)}, u32[]{:S(2)}) collective-permute-start(f32[24,40]{1,0:T(8,128)S(1)} %get-tuple-element.19), channel_id=1, source_target_pairs={{0,12},{1,13},{2,14},{3,15},{4,8},{5,9},{6,10},{7,11},{8,4},{9,5},... | collective-permute-start | bytes 11528 | tf_op jit(solution)/shard_map/ppermute | solution.py:105

commit v2 on v0

v2 whole, which is shorter than its diff:
```python
import functools

import jax
import jax.numpy as jnp
from jax import lax
from jax.experimental import pallas as pl
from jax.experimental.pallas import tpu as pltpu
from jax.sharding import PartitionSpec as P

BF16, F32 = jnp.bfloat16, jnp.float32
VMEM = pl.BlockSpec(memory_space=pltpu.VMEM)
HBM = pl.BlockSpec(memory_space=pltpu.HBM)
NT = (((1,), (1,)), ((), ()))


def up(value, unit):
    return -(-value // unit) * unit


def dot(left, right, dims=None):
    if dims is None:
        return jnp.dot(left, right, preferred_element_type=F32)
    return lax.dot_general(left, right, dims, preferred_element_type=F32)


def both(values):
    high = values.astype(BF16)
    return high, (values - high.astype(F32)).astype(BF16)


def payload_kernel(
    destination, target_block, delay_slot, spikes, weights, total,
    codes, given, held, plain, lagged, sems, part_sems,
):
    steps, trials, neurons = spikes.shape
    unit_count = weights.shape[0]
    delays = lagged.shape[0]
    blocks = neurons // 128
    rows = total.shape[1]
    chunk = held.shape[0] // part_sems.shape[0]
    chunks = unit_count // chunk
    small = [
        pltpu.make_async_copy(destination, codes.at[0], sems.at[0]),
        pltpu.make_async_copy(target_block, codes.at[1], sems.at[1]),
        pltpu.make_async_copy(delay_slot, codes.at[2], sems.at[2]),
        pltpu.make_async_copy(spikes, given, sems.at[3]),
    ]
    for copy in small:
        copy.start()

    def part(index):
        where = pl.ds(index * chunk, chunk)
        return pltpu.make_async_copy(weights.at[where], held.at[where], part_sems.at[index])

    for index in range(chunks):
        part(index).start()
    total[...] = jnp.zeros_like(total)
    plain[...] = jnp.zeros_like(plain)
    lagged[...] = jnp.zeros_like(lagged)
    for copy in small:
        copy.wait()
    front = trials * delays
    for step in range(steps):
        start = front + step * trials
        plain[start : start + trials, :] = given[step].astype(F32)
    for delay in range(delays):
        start = front - trials * (delay + 1)
        lagged[delay, 0:rows, :] = plain[start : start + rows, :].astype(BF16)
    me = lax.axis_index("area")

    def some(index, _):
        part(index).wait()
        units = [index * chunk + inner for inner in range(chunk)]
        values = [
            dot(lagged[codes[2, unit]], held[unit])[0:rows].astype(BF16).astype(F32)
            for unit in units
        ]
        for unit, value in zip(units, values):
            place = lax.bitwise_xor(codes[0, unit], me) * blocks + codes[1, unit]
            total[place] += value
        return 0

    lax.fori_loop(0, chunks, some, 0)


def payload_sums(spikes, weights, destination, target_block, delay_slot, area_count, delays):
    steps, trials, neurons = spikes.shape
    unit_count = weights.shape[0]
    blocks = neurons // 128
    rows = trials * (steps + delays)
    chunk = next(size for size in (16, 12, 8, 6, 4, 3, 2, 1) if unit_count % size == 0)
    return pl.pallas_call(
        payload_kernel,
        out_shape=jax.ShapeDtypeStruct((area_count * blocks, rows, 128), F32),
        in_specs=[HBM, HBM, HBM, HBM, HBM],
        out_specs=VMEM,
        scratch_shapes=[
            pltpu.SMEM((3, unit_count), jnp.int32),
            pltpu.VMEM(spikes.shape, jnp.int32),
            pltpu.VMEM(weights.shape, BF16),
            pltpu.VMEM((trials * delays + rows, neurons), F32),
            pltpu.VMEM((delays, up(rows, 16), neurons), BF16),
            pltpu.SemaphoreType.DMA((4,)),
            pltpu.SemaphoreType.DMA((unit_count // chunk,)),
        ],
        compiler_params=pltpu.CompilerParams(vmem_limit_bytes=32 * 2**20),
        name="payload",
    )(destination, target_block, delay_slot, spikes, weights)


def known_kernel(spikes, population, history, kernel, out, series, fresh, lags):
    steps, trials, neurons = spikes.shape
    pops, kinds, _, taps = history.shape
    group = kinds * trials
    lane = lax.broadcasted_iota(jnp.int32, (pops * group, taps), 1)
    for pop in range(pops):
        for kind in range(kinds):
            start = pop * group + kind * trials
            series[start : start + trials, :] = history[pop, kind]
    flip = lax.broadcasted_iota(jnp.int32, (taps, taps), 0) + lax.broadcasted_iota(
        jnp.int32, (taps, taps), 1
    )
    flip = (flip == taps - 1).astype(F32).astype(BF16)
    back = dot(series[...].astype(BF16), flip)

    which = lax.broadcasted_iota(jnp.int32, (8, neurons), 0)
    member = (which == population[...]).astype(F32).astype(BF16)
    rows = spikes[...].reshape(steps * trials, neurons).astype(F32).astype(BF16)
    rates = (dot(member, rows, NT) / (neurons / pops)).astype(BF16)
    fresh[...] = jnp.zeros_like(fresh)
    row = lax.broadcasted_iota(jnp.int32, (steps * trials, taps), 0)
    column = lax.broadcasted_iota(jnp.int32, (steps * trials, taps), 1)
    for trial in range(trials):
        place = (row == (taps - 1 - column) * trials + trial).astype(F32).astype(BF16)
        placed = dot(rates, place)
        for pop in range(pops):
            fresh[pop * group + trial : pop * group + trial + 1, :] = placed[pop : pop + 1, :]
    lags[...] = jnp.zeros_like(lags)
    recent = fresh[...]
    for step in range(steps):
        shifted = jnp.where(lane >= taps - step, recent, back)
        if step:
            shifted = pltpu.roll(shifted, step, 1)
        for part in range(pops * kinds):
            lags[part, step * trials : (step + 1) * trials, :] = shifted[
                part * trials : (part + 1) * trials, :
            ]
    total = dot(kernel[:, 0:taps], lags[0].astype(BF16), NT)
    for part in range(1, pops * kinds):
        total += dot(kernel[:, part * taps : (part + 1) * taps], lags[part].astype(BF16), NT)
    out[...] = total


def known_lfp(spikes, population, history, kernel):
    pops, kinds, trials, taps = history.shape
    channels = kernel.shape[0]
    return pl.pallas_call(
        known_kernel,
        out_shape=jax.ShapeDtypeStruct((channels, 128), F32),
        in_specs=[VMEM] * 4,
        out_specs=VMEM,
        scratch_shapes=[
            pltpu.VMEM((pops * kinds * trials, taps), F32),
            pltpu.VMEM((pops * kinds * trials, taps), F32),
            pltpu.VMEM((pops * kinds, 128, taps), F32),
        ],
        compiler_params=pltpu.CompilerParams(vmem_limit_bytes=16 * 2**20),
        name="known_lfp",
    )(spikes, population, history, kernel)


class Plan:
    def __init__(self, area_count, trials, steps, delays, neurons, pops, channels):
        self.area_count, self.trials, self.steps, self.delays = area_count, trials, steps, delays
        self.blocks, self.pops = neurons // 128, pops
        self.pop_size = neurons / pops
        self.each = trials * (1 + delays)
        self.main = up(self.blocks * self.each, 16)
        self.share = channels // area_count
        self.groups = up(self.share, 8) // 8
        self.width = trials * steps
        self.slot = self.main + 8
        self.narrow_slot = self.main + 16
        self.signal_rows = up(trials * (steps - 1), 8)
        self.signal_lanes = pops * area_count
        self.parts = up(self.signal_lanes, 128) // 128
        self.wide_lanes = min(self.signal_lanes, 128)
        self.tail = self.parts * self.signal_rows
        self.narrow_tail = up(self.tail, 16) * (2 if 2 * self.wide_lanes > 128 else 1)

    def wide(self, slots):
        return jax.ShapeDtypeStruct((slots * self.slot + self.tail, 128), F32)

    def narrow(self, slots):
        return jax.ShapeDtypeStruct((slots * self.narrow_slot + self.narrow_tail, 128), BF16)


def compress_kernel(plan, total, given, cycle, start, known, keep, send, signal):
    trials, steps, delays, blocks = plan.trials, plan.steps, plan.delays, plan.blocks
    me = lax.axis_index("area")
    signal_rows, lanes = plan.signal_rows, plan.signal_lanes
    signal[...] = jnp.zeros_like(signal)
    owner = lax.broadcasted_iota(jnp.int32, (lanes, 128), 0).astype(F32)

    def pair(index, _):
        sums = jnp.zeros((2 * signal_rows, lanes), F32)
        for bit, out in enumerate((keep, send)):
            device = 2 * index + bit
            own = (device == 0).astype(F32)
            place = lax.bitwise_xor(device, me)
            first = (place * plan.pops).astype(F32)
            base = pl.multiple_of(index * plan.slot, 8)
            tops, members = [], []
            for block in range(blocks):
                arriving = total[device * blocks + block]
                early = arriving[0 : trials * delays] + own * cycle[block]
                arriving = jnp.concatenate([early, arriving[trials * delays :]], axis=0)
                facts = given[device, block * 8 : block * 8 + 8]
                last, leak = facts[0:trials], facts[trials : trials + 1]
                population = facts[trials + 1 : trials + 2]
                membrane = own * start[block]
                for step in range(steps):
                    current = arriving[step * trials : (step + 1) * trials]
                    membrane = jnp.where(last < step, leak * membrane + current, 0.0)
                spot = base + block * plan.each
                out[pl.ds(spot, trials)] = membrane
                out[pl.ds(spot + trials, trials * delays)] = arriving[trials * steps :]
                tops.append(arriving[0:signal_rows])
                members.append((owner == population + first).astype(F32).astype(BF16))
            out[pl.ds(base + blocks * plan.each, plan.main - blocks * plan.each)] = jnp.zeros(
                (plan.main - blocks * plan.each, 128), F32
            )
            top = jnp.concatenate(tops, axis=1)
            high, low = both(top)
            stacked = jnp.concatenate([high.astype(F32), low.astype(F32)], axis=0).astype(BF16)
            sums += dot(stacked, jnp.concatenate(members, axis=1), NT)
            mine = known[place]
            packed = mine[0:8]
            for group in range(1, plan.groups):
                packed += pltpu.roll(mine[group * 8 : group * 8 + 8], group * plan.width, 1)
            out[pl.ds(base + plan.main, 8)] = packed
        signal[...] += sums[:signal_rows] + sums[signal_rows:]
        return 0

    pairs = plan.area_count // 2
    lax.fori_loop(0, pairs, pair, 0, unroll=2)
    for part in range(plan.parts):
        values = signal[:, part * 128 : part * 128 + plan.wide_lanes]
        if plan.wide_lanes < 128:
            values = jnp.concatenate(
                [values, jnp.zeros((signal_rows, 128 - plan.wide_lanes), F32)], axis=1
            )
        spot = pairs * plan.slot + part * signal_rows
        keep[spot : spot + signal_rows] = values
        send[spot : spot + signal_rows] = values


def compress(plan, total, given, cycle, start, known):
    return pl.pallas_call(
        functools.partial(compress_kernel, plan),
        out_shape=(plan.wide(plan.area_count // 2),) * 2,
        in_specs=[VMEM] * 5,
        out_specs=(VMEM, VMEM),
        scratch_shapes=[pltpu.VMEM((plan.signal_rows, plan.signal_lanes), F32)],
        compiler_params=pltpu.CompilerParams(vmem_limit_bytes=32 * 2**20),
        name="compress",
    )(total, given, cycle, start, known)


def narrow_slot(plan, out, slot, main, channels):
    base = slot * plan.narrow_slot
    high, low = both(channels)
    out[base : base + plan.main] = main.astype(BF16)
    out[base + plan.main : base + plan.narrow_slot] = jnp.concatenate(
        [high.astype(F32), low.astype(F32)], axis=0
    ).astype(BF16)


def narrow_tail(plan, out, slots, values):
    base = slots * plan.narrow_slot
    high, low = both(values)
    high, low = high.astype(F32), low.astype(F32)
    if 2 * plan.wide_lanes <= 128:
        rows = high + pltpu.roll(low, plan.wide_lanes, 1)
        pad = plan.narrow_tail - plan.tail
        if pad:
            rows = jnp.concatenate([rows, jnp.zeros((pad, 128), F32)], axis=0)
        out[base : base + plan.narrow_tail] = rows.astype(BF16)
    else:
        half = plan.narrow_tail // 2
        for index, rows in enumerate((high, low)):
            if half > plan.tail:
                rows = jnp.concatenate([rows, jnp.zeros((half - plan.tail, 128), F32)], axis=0)
            out[base + index * half : base + (index + 1) * half] = rows.astype(BF16)


def wide_tail(plan, values):
    values = values.astype(F32)
    if 2 * plan.wide_lanes <= 128:
        lane = lax.broadcasted_iota(jnp.int32, values.shape, 1)
        values = jnp.where(
            lane < plan.wide_lanes, values + pltpu.roll(values, 128 - plan.wide_lanes, 1), 0.0
        )
        return values[: plan.tail]
    half = plan.narrow_tail // 2
    return (values[:half] + values[half:])[: plan.tail]


def received(plan, got, slots, slot):
    if got.dtype == F32:
        rows = got[slot * plan.slot : (slot + 1) * plan.slot]
        return rows[: plan.main], rows[plan.main :]
    rows = got[slot * plan.narrow_slot : (slot + 1) * plan.narrow_slot].astype(F32)
    return rows[: plan.main], rows[plan.main : plan.main + 8] + rows[plan.main + 8 :]


def received_tail(plan, got, slots):
    if got.dtype == F32:
        return got[slots * plan.slot : slots * plan.slot + plan.tail]
    base = slots * plan.narrow_slot
    return wide_tail(plan, got[base : base + plan.narrow_tail])


def fold_kernel(plan, slots, direct, held, got, keep, *sends):
    tail = held[slots * plan.slot : slots * plan.slot + plan.tail] + received_tail(plan, got, slots)
    left = 1 if direct else slots // 2
    for slot in range(slots):
        main, channels = received(plan, got, slots, slot)
        main = main + held[slot * plan.slot : slot * plan.slot + plan.main]
        channels = channels + held[slot * plan.slot + plan.main : (slot + 1) * plan.slot]
        if direct and slot:
            narrow_slot(plan, sends[slot - 1], 0, main, channels)
        elif slot % 2:
            narrow_slot(plan, sends[0], slot // 2, main, channels)
        else:
            base = slot // 2 * plan.slot
            keep[base : base + plan.main] = main
            keep[base + plan.main : base + plan.slot] = channels
    keep[left * plan.slot : left * plan.slot + plan.tail] = tail
    for out in sends:
        narrow_tail(plan, out, left, tail)


def fold(plan, slots, direct, held, got):
    left = 1 if direct else slots // 2
    count = slots - 1 if direct else 1
    return pl.pallas_call(
        functools.partial(fold_kernel, plan, slots, direct),
        out_shape=(plan.wide(left),) + (plan.narrow(left),) * count,
        in_specs=[VMEM] * 2,
        out_specs=(VMEM,) * (1 + count),
        compiler_params=pltpu.CompilerParams(vmem_limit_bytes=32 * 2**20),
        name="fold",
    )(held, got)


def final_kernel(plan, taps_in, held, *refs):
    gots, (membrane, cycle, lfp, late) = refs[:-4], refs[-4:]
    trials, steps, delays = plan.trials, plan.steps, plan.delays
    main, channels = held[0 : plan.main], held[plan.main : plan.slot]
    tail = held[plan.slot : plan.slot + plan.tail]
    for got in gots:
        more, few = received(plan, got, 1, 0)
        main, channels = main + more, channels + few
        tail = tail + received_tail(plan, got, 1)
    for block in range(plan.blocks):
        lanes = slice(block * 128, block * 128 + 128)
        base = block * plan.each
        membrane[:, lanes] = main[base : base + trials]
        for delay in range(delays):
            spot = base + trials * (1 + delay)
            cycle[:, delay, lanes] = main[spot : spot + trials]
    signal = (tail / plan.pop_size).astype(BF16)
    products = None
    for part in range(plan.parts):
        rows = part * 128
        one = dot(
            signal[part * plan.signal_rows : (part + 1) * plan.signal_rows, : plan.wide_lanes],
            taps_in[rows : rows + plan.wide_lanes].astype(BF16),
        )
        products = one if products is None else products + one
    late[...] = jnp.zeros_like(late)
    width = products.shape[1]
    for lag in range(1, steps):
        moved = products
        if lag > 1:
            moved = pltpu.roll(products, width - (lag - 1) * plan.share, 1)
        top = trials * lag
        late[top : plan.width] += moved[0 : plan.width - top, 0:128]
    fresh = jnp.transpose(late[...])
    pieces = [channels]
    for group in range(1, plan.groups):
        pieces.append(pltpu.roll(channels, 128 - group * plan.width, 1))
    known = jnp.concatenate(pieces, axis=0)
    lane = lax.broadcasted_iota(jnp.int32, known.shape, 1)
    value = jnp.where(lane < plan.width, known, 0.0) + fresh[0 : known.shape[0]]
    old = lax.broadcasted_iota(jnp.int32, (128, 128), 0)
    new = lax.broadcasted_iota(jnp.int32, (128, 128), 1)
    swap = (old == (new % steps) * trials + new // steps).astype(F32)
    value = lax.dot_general(
        value, swap, (((1,), (0,)), ((), ())),
        precision=lax.Precision.HIGHEST, preferred_element_type=F32,
    )
    lfp[...] = value[0 : plan.share, 0 : plan.width]


def final(plan, neurons, taps_in, held, gots):
    trials, delays = plan.trials, plan.delays
    return pl.pallas_call(
        functools.partial(final_kernel, plan),
        out_shape=(
            jax.ShapeDtypeStruct((trials, neurons), F32),
            jax.ShapeDtypeStruct((trials, delays, neurons), F32),
            jax.ShapeDtypeStruct((plan.share, plan.width), F32),
        ),
        in_specs=[VMEM] * (2 + len(gots)),
        out_specs=(VMEM,) * 3,
        scratch_shapes=[pltpu.VMEM((128, 128), F32)],
        compiler_params=pltpu.CompilerParams(vmem_limit_bytes=16 * 2**20),
        name="final",
    )(taps_in, held, *gots)


def swap(values, bit, area_count):
    return lax.ppermute(values, "area", [(i, i ^ bit) for i in range(area_count)])


def body(
    spikes,
    weights,
    destination,
    target_block,
    delay_slot,
    population,
    leak_rate,
    membrane_start,
    cycle_start,
    history,
    lfp_kernel,
):
    area_count = lax.axis_size("area")
    neurons = weights.shape[1]
    blocks = neurons // 128
    trials, steps = spikes.shape[:2]
    delays = cycle_start.shape[1]
    channels = lfp_kernel.shape[0]
    pops = history.shape[0]
    me = lax.axis_index("area")
    plan = Plan(area_count, trials, steps, delays, neurons, pops, channels)
    share = plan.share
    spikes = jnp.transpose(spikes, (1, 0, 2))

    order = lax.broadcasted_iota(jnp.int32, spikes.shape, 0)
    last = jnp.max(jnp.where(spikes > 0, order, -1), axis=0)
    facts = jnp.concatenate(
        [
            last.astype(F32),
            leak_rate[None],
            population.astype(F32)[None],
            jnp.zeros((6 - trials, neurons), F32),
        ]
    )
    facts = jnp.transpose(facts.reshape(8, blocks, 128), (1, 0, 2)).reshape(1, blocks * 8, 128)
    reach = steps - 1
    taps_in = lfp_kernel[:, :, 1, :reach].astype(F32).reshape(area_count, share, pops, reach)
    taps_in = jnp.transpose(taps_in, (0, 2, 3, 1)).reshape(area_count, pops, reach * share)
    lanes = up(reach * share, 128)
    taps_in = jnp.pad(taps_in, ((0, 0), (0, 0), (0, lanes - reach * share)))
    taps_in = taps_in.reshape(1, area_count, pops * lanes // 128, 128)
    for level in range(area_count.bit_length() - 2, -1, -1):
        bit = 1 << level
        upper = lax.bitwise_and(lax.shift_right_logical(me, level), 1)
        count, left, rows = taps_in.shape[:3]
        halves = taps_in.reshape(count, 2, left // 2, rows, 128)
        stays = lax.dynamic_index_in_dim(halves, upper, 1, keepdims=False)
        goes = lax.dynamic_index_in_dim(halves, 1 - upper, 1, keepdims=False)
        size = facts.shape[0] * facts.shape[1]
        message = jnp.concatenate([facts.reshape(-1, 128), goes.reshape(-1, 128)])
        message = swap(message, bit, area_count)
        facts = jnp.stack([facts, message[:size].reshape(facts.shape)], axis=1)
        facts = facts.reshape(-1, blocks * 8, 128)
        came = message[size:].reshape(stays.shape)
        taps_in = jnp.stack(
            [jnp.where(upper == 0, stays, came), jnp.where(upper == 0, came, stays)], axis=1
        ).reshape(count * 2, left // 2, rows, 128)
    taps_in = taps_in.reshape(area_count * pops, lanes)

    total = payload_sums(
        spikes, weights, destination[:, 0], target_block, delay_slot, area_count, delays
    )
    known = known_lfp(spikes, population[None], history, lfp_kernel.reshape(channels, -1))
    known = known.reshape(area_count, share, 128)
    known = jnp.pad(known, ((0, 0), (0, plan.groups * 8 - share), (0, 0)))
    cycle = jnp.transpose(cycle_start, (1, 0, 2)).reshape(delays * trials, blocks, 128)
    cycle = jnp.transpose(cycle, (1, 0, 2))
    start = jnp.transpose(membrane_start.reshape(trials, blocks, 128), (1, 0, 2))
    keep, send = compress(plan, total, facts, cycle, start, known)

    slots = area_count // 2
    got = swap(send, 1, area_count)
    bit = 2
    while slots > 4:
        keep, send = fold(plan, slots, False, keep, got)
        got = swap(send, bit, area_count)
        slots, bit = slots // 2, bit * 2
    keep, *sends = fold(plan, slots, True, keep, got)
    gots = [swap(send, bit * index, area_count) for index, send in enumerate(sends, 1)]
    return tuple(final(plan, neurons, taps_in, keep, gots))


def solution(mesh):
    return jax.shard_map(
        body,
        mesh=mesh,
        in_specs=(
            P("runs", None, "area"),
            P("area", None, None),
            P("area", None),
            P("area"),
            P("area"),
            P("area"),
            P("area"),
            P("runs", "area"),
            P("runs", None, "area"),
            P("area", None, "runs", None),
            P(None, "area", None, None),
        ),
        out_specs=(P("runs", "area"), P("runs", None, "area"), P("area", "runs")),
        check_vma=False,
    )
```

time: 135 us -> 50.6 us (0.37)
  blocking collectives: 62.7 us -> 0 us
  local copies, waits for them, and re-layouts: 27.5 us -> 9.06 us
  Pallas kernels: 0 us -> 7.19 us
  matrix products: 6.9 us -> 0 us
  other arithmetic: 4.66 us -> 0.92 us
    unnamed x1 -> x0, blocking collectives: 62.7 us -> none
    ppermute x0 -> x9, waiting for transfers between devices: none -> 18.2 us  [swap(): lax.ppermute(values, 'area', [(i, i ^ bit) for i in range(area_count)])]
    all_to_all x2 -> x0, waiting for transfers between devices: 17.3 us -> none  [the longest x1 17.3 us: body(): lax.all_to_all(outgoing, 'area', split_axis=0, concat_axis=0, tiled=True)]
    ppermute x0 -> x9, starting transfers between devices: none -> 14 us  [swap(): lax.ppermute(values, 'area', [(i, i ^ bit) for i in range(area_count)])]
    all_to_all x2 -> x0, starting transfers between devices: 13.5 us -> none  [the longest x1 7.36 us: body(): lax.all_to_all(codes, 'area', split_axis=0, concat_axis=0, tiled=True)]
    scatter x2 -> x0, local copies, waits for them, and re-layouts: 12.7 us -> none  [the longest x1 11.8 us: body(): outgoing.at[send_slot]]
    pallas_call x0 -> x6, Pallas kernels: none -> 7.19 us  [the longest x1 3.63 us: payload_sums(): pl.pallas_call(payload_kernel, out_shape=jax.ShapeDtypeStruct((area_count...]
    dot_general x5 -> x0, matrix products: 6.9 us -> none  [the longest x1 5.26 us: body(): jnp.einsum('rk,ukn->urn', spike_rows, weights, preferred_element_type=jnp...]
  transfers between devices with their start and end apart: 2 -> 9, of which waited for: 1 -> 7; matrix products, arithmetic and copies ran while one was open for 18% -> 4% of each run, Pallas kernels for 0% -> 9%
where the time goes in v2:
time: 50.6 us; the launch traced here: 50.4 us
  waiting for transfers between devices  18.2 us (36%)
  starting transfers between devices  14 us (28%)
  local copies, waits for them, and re-layouts  9.06 us (18%)
  Pallas kernels  7.19 us (14%)
  between operations  1.06 us (2%)
  other arithmetic  0.92 us (2%)
    ppermute x9, waiting for transfers between devices, swap(): lax.ppermute(values, 'area', [(i, i ^ bit) for i in range(area_count)])  18.2 us
    ppermute x9, starting transfers between devices, swap(): lax.ppermute(values, 'area', [(i, i ^ bit) for i in range(area_count)])  14 us
    unnamed x20, local copies, waits for them, and re-layouts  3.72 us
    pallas_call x1, Pallas kernels, payload_sums(): pl.pallas_call(payload_kernel, out_shape=jax.ShapeDtypeStruct((area_count...  3.63 us
    slice x2, local copies, waits for them, and re-layouts, body(): lfp_kernel[:, :, 1, :reach].astype(F32)  2.53 us
    reshape x1, local copies, waits for them, and re-layouts, body(): lfp_kernel.reshape(channels, -1)  1.22 us
    pallas_call x1, Pallas kernels, compress(): pl.pallas_call(functools.partial(compress_kernel, plan), out_shape=(plan....  1.19 us
    pallas_call x1, Pallas kernels, final(): pl.pallas_call(functools.partial(final_kernel, plan), out_shape=(jax.Shap...  1.15 us
  transfers between devices with their start and end apart: 9, of which 7 were waited for; matrix products, arithmetic and copies ran while one was open for 4% of the time, Pallas kernels for 9%

profile of v2, /device:TPU:0, one launch (start us, length us, event | category | flops | bytes accessed | tf_op | source)
XLA Modules:
  0.0 50.4 jit_solution(12106009672640999298)
XLA Ops:
  0.6 0.0 copy-start.1
  0.7 2.0 %slice.27 = bf16[384,4,1,9]{3,2,1,0:T(2,128)(2,1)S(1)} slice(bf16[384,4,2,256]{3,2,1,0:T(2,128)(2,1)} %param.21), slice={[0:384], [0:4], [1:2], [0:9]} | slice | bytes 55296 | tf_op jit(solution)/shard_map/slice | solution.py:465
  2.7 0.5 copy.31
  3.2 0.2 convert_element_type.17
  3.4 0.1 copy.32
  3.5 0.2 reshape.96
  3.8 0.0 copy-start.7
  3.9 0.0 copy-done.1
  3.9 0.0 copy-done.8
  4.0 0.1 pad.33.clone
  4.1 0.1 fusion.3
  4.2 4.0 %collective-permute-start = (f32[88,128]{1,0:T(8,128)S(1)}, f32[88,128]{1,0:T(8,128)S(1)}, u32[]{:S(2)}, u32[]{:S(2)}) collective-permute-start(f32[88,128]{1,0:T(8,128)S(1)} %pad_maximum_fusion.9), channel_id=1, source_target_pairs={{0,8},{1,9},{2,10},{3,11},{4,12},{5,13},{6,14},{7,15},{8,0},{9,1},... | collective-permute-start | bytes 135176 | tf_op jit(solution)/shard_map/ppermute | solution.py:425
  8.2 2.5 %collective-permute-done = f32[88,128]{1,0:T(8,128)S(1)} collective-permute-done((f32[88,128]{1,0:T(8,128)S(1)}, f32[88,128]{1,0:T(8,128)S(1)}, u32[]{:S(2)}, u32[]{:S(2)}) %collective-permute-start) | collective-permute-done | bytes 45088 | tf_op jit(solution)/shard_map/ppermute | solution.py:425
  10.8 1.5 %collective-permute-start.1 = (f32[112,128]{1,0:T(8,128)S(1)}, f32[112,128]{1,0:T(8,128)S(1)}, u32[]{:S(2)}, u32[]{:S(2)}) collective-permute-start(f32[112,128]{1,0:T(8,128)S(1)} %pad_maximum_fusion.7), channel_id=1, source_target_pairs={{0,4},{1,5},{2,6},{3,7},{4,0},{5,1},{6,2},{7,3},{8,12},{9,13},{10,... | collective-permute-start | bytes 172040 | tf_op jit(solution)/shard_map/ppermute | solution.py:425
  12.3 2.8 %collective-permute-done.1 = f32[112,128]{1,0:T(8,128)S(1)} collective-permute-done((f32[112,128]{1,0:T(8,128)S(1)}, f32[112,128]{1,0:T(8,128)S(1)}, u32[]{:S(2)}, u32[]{:S(2)}) %collective-permute-start.1) | collective-permute-done | bytes 57376 | tf_op jit(solution)/shard_map/ppermute | solution.py:425
  15.1 1.8 %collective-permute-start.2 = (f32[160,128]{1,0:T(8,128)S(1)}, f32[160,128]{1,0:T(8,128)S(1)}, u32[]{:S(2)}, u32[]{:S(2)}) collective-permute-start(f32[160,128]{1,0:T(8,128)S(1)} %pad_maximum_fusion.3), channel_id=1, source_target_pairs={{0,2},{1,3},{2,0},{3,1},{4,6},{5,7},{6,4},{7,5},{8,10},{9,11},{10,... | collective-permute-start | bytes 245768 | tf_op jit(solution)/shard_map/ppermute | solution.py:425
  16.9 2.7 %collective-permute-done.2 = f32[160,128]{1,0:T(8,128)S(1)} collective-permute-done((f32[160,128]{1,0:T(8,128)S(1)}, f32[160,128]{1,0:T(8,128)S(1)}, u32[]{:S(2)}, u32[]{:S(2)}) %collective-permute-start.2) | collective-permute-done | bytes 81952 | tf_op jit(solution)/shard_map/ppermute | solution.py:425
  19.7 0.7 %pad_maximum_fusion.1 = f32[256,128]{1,0:T(8,128)} fusion(f32[64,128]{1,0:T(8,128)S(1)} %dynamic-slice_bitcast_fusion, f32[192,128]{1,0:T(8,128)S(1)} %bitcast.80), kind=kLoop, calls=%fused_computation.1 | loop fusion | flops 32768 | bytes 262144 | tf_op jit(solution)/shard_map/concatenate | solution.py:478
  20.4 0.0 collective-permute-start.3
  20.4 1.2 %reshape.108.kernel = bf16[384,2048]{1,0:T(8,128)(2,1)S(1)} reshape(bf16[384,4,2,256]{3,2,1,0:T(2,128)(2,1)S(1)} %copy-done.7) | data formatting | bytes 3145728 | tf_op jit(solution)/shard_map/reshape | solution.py:491
  21.6 0.0 copy-start.4
  21.6 0.0 copy-start.5
  21.6 0.0 copy-start.6
  21.7 0.7 %copy.42 = f32[4,4,384]{2,1,0:T(4,128)S(1)} copy(f32[4,4,384]{2,0,1:T(4,128)} %bitcast.101) | data formatting | bytes 49152 | tf_op jit(solution)/shard_map/transpose | solution.py:494
  22.5 0.0 copy-done.2
  22.5 1.0 %known_lfp.1 = f32[384,128]{1,0:T(8,128)S(1)} custom-call(s32[10,4,384]{2,1,0:T(4,128)S(1)} %bitcast.75, s32[1,384]{1,0:T(1,128)S(1)} %broadcast_in_dim.14.population, f32[4,2,4,256]{3,2,1,0:T(4,128)S(1)} %copy-done.2, bf16[384,2048]{1,0:T(8,128)(2,1)S(1)} %reshape.108.kernel), custom_call_target="tpu_custom_call" | custom-call | tf_op jit(solution)/shard_map/known_lfp/pallas_call | solution.py:157
  23.4 0.0 copy-done.4
  23.5 0.0 copy-done.5
  23.5 0.0 copy-done.6
  23.5 0.0 copy-start
  23.5 3.7 %copy-done = bf16[96,384,128]{2,1,0:T(8,128)(2,1)S(1)} copy-done((bf16[96,384,128]{2,1,0:T(8,128)(2,1)S(1)}, bf16[96,384,128]{2,1,0:T(8,128)(2,1)}, u32[]{:S(2)}) %copy-start) | copy-done | bytes 9437208
  27.2 3.6 %payload.1.total = f32[48,56,128]{2,1,0:T(8,128)S(1)} custom-call(s32[96]{0:T(128)S(1)} %bitcast.79, s32[96]{0:T(128)S(1)} %copy-done.5, s32[96]{0:T(128)S(1)} %copy-done.6, s32[10,4,384]{2,1,0:T(4,128)S(1)} %bitcast.76, bf16[96,384,128]{2,1,0:T(8,128)(2,1)S(1)} %copy-done), custom_call_target="tpu_custom_call" | custom-call | tf_op jit(solution)/shard_map/payload/pallas_call | solution.py:92
  30.8 0.0 collective-permute-done.3
  30.9 0.0 copy-done.3
  30.9 1.2 %compress.1 = (f32[616,128]{1,0:T(8,128)S(1)}, f32[616,128]{1,0:T(8,128)S(1)}) custom-call(f32[48,56,128]{2,1,0:T(8,128)S(1)} %payload.1.total, f32[16,24,128]{2,1,0:T(8,128)S(1)} %bitcast.73, f32[3,16,128]{2,1,0:T(8,128)S(1)} %bitcast.77, f32[3,4,128]{2,1,0:T(4,128)S(1)} %bitcast.78, f32[16,24,128]{2,1,0:T(8,128)S(1)} %bitcast.74), custom_call_target="tpu_custom_call" | custom-call | tf_op jit(solution)/shard_map/compress/pallas_call | solution.py:259
  32.1 0.6 %collective-permute-start.4 = (f32[616,128]{1,0:T(8,128)S(1)}, f32[616,128]{1,0:T(8,128)S(1)}, u32[]{:S(2)}, u32[]{:S(2)}) collective-permute-start(f32[616,128]{1,0:T(8,128)S(1)} %get-tuple-element.12), channel_id=1, source_target_pairs={{0,1},{1,0},{2,3},{3,2},{4,5},{5,4},{6,7},{7,6},{8,9},{9,8},{10,11... | collective-permute-start | bytes 946184 | tf_op jit(solution)/shard_map/ppermute | solution.py:425
  32.6 1.2 %collective-permute-done.4.got = f32[616,128]{1,0:T(8,128)S(1)} collective-permute-done((f32[616,128]{1,0:T(8,128)S(1)}, f32[616,128]{1,0:T(8,128)S(1)}, u32[]{:S(2)}, u32[]{:S(2)}) %collective-permute-start.4) | collective-permute-done | bytes 315424 | tf_op jit(solution)/shard_map/ppermute | solution.py:425
  33.9 0.1 fold.2
  34.0 1.7 %collective-permute-start.5 = (bf16[368,128]{1,0:T(8,128)(2,1)S(1)}, bf16[368,128]{1,0:T(8,128)(2,1)S(1)}, u32[]{:S(2)}, u32[]{:S(2)}) collective-permute-start(bf16[368,128]{1,0:T(8,128)(2,1)S(1)} %get-tuple-element.14), channel_id=1, source_target_pairs={{0,2},{1,3},{2,0},{3,1},{4,6},{5,7},{6,4},{7,5},{8,10},{9,11},{10,... | collective-permute-start | bytes 282632 | tf_op jit(solution)/shard_map/ppermute | solution.py:425
  35.7 3.3 %collective-permute-done.5.got = bf16[368,128]{1,0:T(8,128)(2,1)S(1)} collective-permute-done((bf16[368,128]{1,0:T(8,128)(2,1)S(1)}, bf16[368,128]{1,0:T(8,128)(2,1)S(1)}, u32[]{:S(2)}, u32[]{:S(2)}) %collective-permute-start.5) | collective-permute-done | bytes 94240 | tf_op jit(solution)/shard_map/ppermute | solution.py:425
  39.0 0.2 fold.3
  39.1 1.4 %collective-permute-start.6 = (bf16[128,128]{1,0:T(8,128)(2,1)S(1)}, bf16[128,128]{1,0:T(8,128)(2,1)S(1)}, u32[]{:S(2)}, u32[]{:S(2)}) collective-permute-start(bf16[128,128]{1,0:T(8,128)(2,1)S(1)} %get-tuple-element.16), channel_id=1, source_target_pairs={{0,4},{1,5},{2,6},{3,7},{4,0},{5,1},{6,2},{7,3},{8,12},{9,13},{10,... | collective-permute-start | bytes 98312 | tf_op jit(solution)/shard_map/ppermute | solution.py:425
  40.6 3.0 %collective-permute-start.7 = (bf16[128,128]{1,0:T(8,128)(2,1)S(1)}, bf16[128,128]{1,0:T(8,128)(2,1)S(1)}, u32[]{:S(2)}, u32[]{:S(2)}) collective-permute-start(bf16[128,128]{1,0:T(8,128)(2,1)S(1)} %get-tuple-element.17), channel_id=1, source_target_pairs={{0,8},{1,9},{2,10},{3,11},{4,12},{5,13},{6,14},{7,15},{8,0},{9,1},... | collective-permute-start | bytes 98312 | tf_op jit(solution)/shard_map/ppermute | solution.py:425
  43.5 0.0 collective-permute-start.8
  43.6 0.0 collective-permute-done.6.refs_0_
  43.6 2.4 %collective-permute-done.7.refs_1_ = bf16[128,128]{1,0:T(8,128)(2,1)S(1)} collective-permute-done((bf16[128,128]{1,0:T(8,128)(2,1)S(1)}, bf16[128,128]{1,0:T(8,128)(2,1)S(1)}, u32[]{:S(2)}, u32[]{:S(2)}) %collective-permute-start.7) | collective-permute-done | bytes 32800 | tf_op jit(solution)/shard_map/ppermute | solution.py:425
  46.0 3.3 %collective-permute-done.8.refs_2_ = bf16[128,128]{1,0:T(8,128)(2,1)S(1)} collective-permute-done((bf16[128,128]{1,0:T(8,128)(2,1)S(1)}, bf16[128,128]{1,0:T(8,128)(2,1)S(1)}, u32[]{:S(2)}, u32[]{:S(2)}) %collective-permute-start.8) | collective-permute-done | bytes 32800 | tf_op jit(solution)/shard_map/ppermute | solution.py:425
  49.2 1.1 %final.1 = (f32[4,384]{1,0:T(4,128)}, f32[4,4,384]{2,1,0:T(4,128)}, f32[24,40]{1,0:T(8,128)}) custom-call(f32[64,256]{1,0:T(8,128)S(1)} %reshape_reshape.36.taps_in, f32[112,128]{1,0:T(8,128)S(1)} %get-tuple-element.15.held, bf16[128,128]{1,0:T(8,128)(2,1)S(1)} %collective-permute-done.6.refs_0_, bf16[128,128]{1,0:T(8,128)(2,1)S(1)} %collective-permute-done.7.refs_1_, ...), custom_call_target="tpu_custom_call" | custom-call | tf_op jit(solution)/shard_map/final/pallas_call | solution.py:409
  (46 shorter events, 0.5 us)
Async XLA Ops:
  0.6 3.2 %copy-start.1 = (s32[4,10,384]{2,0,1:T(4,128)S(1)}, s32[4,10,384]{2,0,1:T(4,128)}, u32[]{:S(2)}) copy-start(s32[4,10,384]{2,0,1:T(4,128)} %param.11) | copy-start | bytes 184324
  0.6 3.3 %copy-start.8 = (s32[384]{0:T(512)S(1)}, s32[384]{0:T(512)}, u32[]{:S(2)}) copy-start(s32[384]{0:T(512)} %param.16) | copy-start | bytes 4612
  0.7 3.3 %copy-start.9 = (f32[384]{0:T(512)S(1)}, f32[384]{0:T(512)}, u32[]{:S(2)}) copy-start(f32[384]{0:T(512)} %param.17) | copy-start | bytes 4612
  3.8 16.6 %copy-start.7 = (bf16[384,4,2,256]{3,2,1,0:T(2,128)(2,1)S(1)}, bf16[384,4,2,256]{3,2,1,0:T(2,128)(2,1)}, u32[]{:S(2)}) copy-start(bf16[384,4,2,256]{3,2,1,0:T(2,128)(2,1)} %param.21) | copy-start | bytes 4718596
  4.2 6.6 %collective-permute-start = (f32[88,128]{1,0:T(8,128)S(1)}, f32[88,128]{1,0:T(8,128)S(1)}, u32[]{:S(2)}, u32[]{:S(2)}) collective-permute-start(f32[88,128]{1,0:T(8,128)S(1)} %pad_maximum_fusion.9), channel_id=1, source_target_pairs={{0,8},{1,9},{2,10},{3,11},{4,12},{5,13},{6,14},{7,15},{8,0},{9,1},... | collective-permute-start | bytes 135176 | tf_op jit(solution)/shard_map/ppermute | solution.py:425
  10.8 4.2 %collective-permute-start.1 = (f32[112,128]{1,0:T(8,128)S(1)}, f32[112,128]{1,0:T(8,128)S(1)}, u32[]{:S(2)}, u32[]{:S(2)}) collective-permute-start(f32[112,128]{1,0:T(8,128)S(1)} %pad_maximum_fusion.7), channel_id=1, source_target_pairs={{0,4},{1,5},{2,6},{3,7},{4,0},{5,1},{6,2},{7,3},{8,12},{9,13},{10,... | collective-permute-start | bytes 172040 | tf_op jit(solution)/shard_map/ppermute | solution.py:425
  15.1 4.5 %collective-permute-start.2 = (f32[160,128]{1,0:T(8,128)S(1)}, f32[160,128]{1,0:T(8,128)S(1)}, u32[]{:S(2)}, u32[]{:S(2)}) collective-permute-start(f32[160,128]{1,0:T(8,128)S(1)} %pad_maximum_fusion.3), channel_id=1, source_target_pairs={{0,2},{1,3},{2,0},{3,1},{4,6},{5,7},{6,4},{7,5},{8,10},{9,11},{10,... | collective-permute-start | bytes 245768 | tf_op jit(solution)/shard_map/ppermute | solution.py:425
  20.4 2.1 %copy-start.2 = (f32[4,2,4,256]{3,2,1,0:T(4,128)S(1)}, f32[4,2,4,256]{3,2,1,0:T(4,128)}, u32[]{:S(2)}) copy-start(f32[4,2,4,256]{3,2,1,0:T(4,128)} %history.1) | copy-start | bytes 98308
  20.4 10.4 %collective-permute-start.3 = (f32[256,128]{1,0:T(8,128)}, f32[256,128]{1,0:T(8,128)S(1)}, u32[]{:S(2)}, u32[]{:S(2)}) collective-permute-start(f32[256,128]{1,0:T(8,128)} %pad_maximum_fusion.1), channel_id=1, source_target_pairs={{0,1},{1,0},{2,3},{3,2},{4,5},{5,4},{6,7},{7,6},{8,9},{9,8},{10,11... | collective-permute-start | bytes 393224 | tf_op jit(solution)/shard_map/ppermute | solution.py:425
  21.6 1.8 %copy-start.4 = (s32[96,1]{0,1:T(1,128)S(1)}, s32[96,1]{0,1:T(1,128)}, u32[]{:S(2)}) copy-start(s32[96,1]{0,1:T(1,128)} %param.13) | copy-start | bytes 1156
  21.6 1.8 %copy-start.5 = (s32[96]{0:T(128)S(1)}, s32[96]{0:T(128)}, u32[]{:S(2)}) copy-start(s32[96]{0:T(128)} %target_block.1) | copy-start | bytes 1156
  21.6 1.8 %copy-start.6 = (s32[96]{0:T(128)S(1)}, s32[96]{0:T(128)}, u32[]{:S(2)}) copy-start(s32[96]{0:T(128)} %delay_slot.1) | copy-start | bytes 1156
  23.5 3.7 %copy-start = (bf16[96,384,128]{2,1,0:T(8,128)(2,1)S(1)}, bf16[96,384,128]{2,1,0:T(8,128)(2,1)}, u32[]{:S(2)}) copy-start(bf16[96,384,128]{2,1,0:T(8,128)(2,1)} %weights.1) | copy-start | bytes 28311556
  27.2 3.7 %copy-start.3 = (f32[4,384]{1,0:T(4,128)S(1)}, f32[4,384]{1,0:T(4,128)}, u32[]{:S(2)}) copy-start(f32[4,384]{1,0:T(4,128)} %param.18) | copy-start | bytes 18436
  32.1 1.8 %collective-permute-start.4 = (f32[616,128]{1,0:T(8,128)S(1)}, f32[616,128]{1,0:T(8,128)S(1)}, u32[]{:S(2)}, u32[]{:S(2)}) collective-permute-start(f32[616,128]{1,0:T(8,128)S(1)} %get-tuple-element.12), channel_id=1, source_target_pairs={{0,1},{1,0},{2,3},{3,2},{4,5},{5,4},{6,7},{7,6},{8,9},{9,8},{10,11... | collective-permute-start | bytes 946184 | tf_op jit(solution)/shard_map/ppermute | solution.py:425
  34.0 5.0 %collective-permute-start.5 = (bf16[368,128]{1,0:T(8,128)(2,1)S(1)}, bf16[368,128]{1,0:T(8,128)(2,1)S(1)}, u32[]{:S(2)}, u32[]{:S(2)}) collective-permute-start(bf16[368,128]{1,0:T(8,128)(2,1)S(1)} %get-tuple-element.14), channel_id=1, source_target_pairs={{0,2},{1,3},{2,0},{3,1},{4,6},{5,7},{6,4},{7,5},{8,10},{9,11},{10,... | collective-permute-start | bytes 282632 | tf_op jit(solution)/shard_map/ppermute | solution.py:425
  39.1 4.4 %collective-permute-start.6 = (bf16[128,128]{1,0:T(8,128)(2,1)S(1)}, bf16[128,128]{1,0:T(8,128)(2,1)S(1)}, u32[]{:S(2)}, u32[]{:S(2)}) collective-permute-start(bf16[128,128]{1,0:T(8,128)(2,1)S(1)} %get-tuple-element.16), channel_id=1, source_target_pairs={{0,4},{1,5},{2,6},{3,7},{4,0},{5,1},{6,2},{7,3},{8,12},{9,13},{10,... | collective-permute-start | bytes 98312 | tf_op jit(solution)/shard_map/ppermute | solution.py:425
  40.6 5.4 %collective-permute-start.7 = (bf16[128,128]{1,0:T(8,128)(2,1)S(1)}, bf16[128,128]{1,0:T(8,128)(2,1)S(1)}, u32[]{:S(2)}, u32[]{:S(2)}) collective-permute-start(bf16[128,128]{1,0:T(8,128)(2,1)S(1)} %get-tuple-element.17), channel_id=1, source_target_pairs={{0,8},{1,9},{2,10},{3,11},{4,12},{5,13},{6,14},{7,15},{8,0},{9,1},... | collective-permute-start | bytes 98312 | tf_op jit(solution)/shard_map/ppermute | solution.py:425
  43.5 5.7 %collective-permute-start.8 = (bf16[128,128]{1,0:T(8,128)(2,1)S(1)}, bf16[128,128]{1,0:T(8,128)(2,1)S(1)}, u32[]{:S(2)}, u32[]{:S(2)}) collective-permute-start(bf16[128,128]{1,0:T(8,128)(2,1)S(1)} %get-tuple-element.18), channel_id=1, source_target_pairs={{0,12},{1,13},{2,14},{3,15},{4,8},{5,9},{6,10},{7,11},{8,4},{9,5},... | collective-permute-start | bytes 98312 | tf_op jit(solution)/shard_map/ppermute | solution.py:425

commit v3 on v2

v3 whole, which is shorter than its diff:
```python
import functools

import jax
import jax.numpy as jnp
from jax import lax
from jax.experimental import pallas as pl
from jax.experimental.pallas import tpu as pltpu
from jax.sharding import PartitionSpec as P

BF16, F32 = jnp.bfloat16, jnp.float32
VMEM = pl.BlockSpec(memory_space=pltpu.VMEM)
HBM = pl.BlockSpec(memory_space=pltpu.HBM)
NT = (((1,), (1,)), ((), ()))


def up(value, unit):
    return -(-value // unit) * unit


def dot(left, right, dims=None):
    if dims is None:
        return jnp.dot(left, right, preferred_element_type=F32)
    return lax.dot_general(left, right, dims, preferred_element_type=F32)


def both(values):
    high = values.astype(BF16).astype(F32)
    return high, (values - high).astype(BF16).astype(F32)


def params(megabytes):
    return pltpu.CompilerParams(vmem_limit_bytes=megabytes * 2**20)


def cost(flops, size):
    return pl.CostEstimate(flops=flops, bytes_accessed=size, transcendentals=0)


class Plan:
    def __init__(self, area_count, trials, steps, delays, neurons, pops, channels):
        self.area_count, self.trials, self.steps, self.delays = area_count, trials, steps, delays
        self.lanes = area_count // 2
        self.blocks, self.pops = neurons // 128, pops
        self.pop_size = neurons / pops
        self.arriving = trials * (steps + delays)
        self.each = trials * (1 + delays)
        self.main = self.blocks * self.each
        self.main_up = up(self.main, 16)
        self.share = channels // area_count
        self.groups = up(self.share, 8) // 8
        self.width = trials * steps
        self.taps_lanes = up((steps - 1) * self.share, 128)
        self.taps = up(self.taps_lanes // 128 * pops, 8)
        self.signal = up(trials * (steps - 1), 8)
        self.signal_lanes = pops * self.lanes
        self.tile = min(self.signal_lanes, 128)
        self.tiles = up(self.signal_lanes, 128) // 128
        self.compact = 4 * self.tile <= 128 and self.signal % 2 == 0
        self.packed = self.signal // 2 if self.compact else 2 * self.tiles * self.signal
        self.packed_up = up(self.packed, 16)
        self.held = self.main_up + 16
        self.last = up(self.main + self.packed, 16)

    def keep(self, slots):
        rows = slots * self.held + self.tiles * self.signal
        return jax.ShapeDtypeStruct((rows, 128), F32)

    def slot(self, stage):
        return self.held + (2 * self.taps << stage)

    def send(self, slots, stage):
        return jax.ShapeDtypeStruct((slots * self.slot(stage) + self.packed_up, 128), BF16)

    def direct(self):
        rows = self.last + 16 + self.lanes // 4 * 2 * self.taps
        return jax.ShapeDtypeStruct((rows, 128), BF16)

    def carried(self):
        return jax.ShapeDtypeStruct((self.lanes * 2 * self.taps, 128), BF16)


def payload_kernel(
    destination, target_block, delay_slot, spikes, weights, keep, send, token,
    codes, given, held, plain, lagged, total, sems, part_sems,
):
    steps, trials, neurons = spikes.shape
    unit_count = weights.shape[0]
    delays = lagged.shape[0]
    blocks = neurons // 128
    half, rows = keep.shape[:2]
    chunk = held.shape[0] // part_sems.shape[0]
    chunks = unit_count // chunk
    small = [
        pltpu.make_async_copy(destination, codes.at[0], sems.at[0]),
        pltpu.make_async_copy(target_block, codes.at[1], sems.at[1]),
        pltpu.make_async_copy(delay_slot, codes.at[2], sems.at[2]),
        pltpu.make_async_copy(spikes, given, sems.at[3]),
    ]
    for copy in small:
        copy.start()

    def part(index):
        where = pl.ds(index * chunk, chunk)
        return pltpu.make_async_copy(weights.at[where], held.at[where], part_sems.at[index])

    for index in range(chunks):
        part(index).start()
    total[...] = jnp.zeros_like(total)
    plain[...] = jnp.zeros_like(plain)
    lagged[...] = jnp.zeros_like(lagged)
    token[...] = jnp.zeros_like(token)
    for copy in small:
        copy.wait()
    front = trials * delays
    for step in range(steps):
        start = front + step * trials
        plain[start : start + trials, :] = given[step].astype(F32)
    for delay in range(delays):
        start = front - trials * (delay + 1)
        lagged[delay, 0:rows, :] = plain[start : start + rows, :].astype(BF16)
    me = lax.axis_index("area")

    def some(index, _):
        part(index).wait()
        units = [index * chunk + inner for inner in range(chunk)]
        values = [
            dot(lagged[codes[2, unit]], held[unit])[0:rows].astype(BF16).astype(F32)
            for unit in units
        ]
        for unit, value in zip(units, values):
            device = lax.bitwise_xor(codes[0, unit], me)
            lane = lax.shift_right_logical(device, 1)
            place = lax.bitwise_and(device, 1) * half + lane * blocks + codes[1, unit]
            total[place] += value
        return 0

    lax.fori_loop(0, chunks, some, 0)
    keep[...] = total[0:half]
    send[...] = total[half:]


def payload_sums(plan, spikes, weights, destination, target_block, delay_slot):
    steps, trials, neurons = spikes.shape
    unit_count = weights.shape[0]
    rows, delays = plan.arriving, plan.delays
    chunk = next(size for size in (16, 12, 8, 6, 4, 3, 2, 1) if unit_count % size == 0)
    half = jax.ShapeDtypeStruct((plan.lanes * plan.blocks, rows, 128), F32)
    return pl.pallas_call(
        payload_kernel,
        out_shape=(half, half, jax.ShapeDtypeStruct((8, 128), F32)),
        in_specs=[HBM, HBM, HBM, HBM, HBM],
        out_specs=(VMEM, VMEM, VMEM),
        scratch_shapes=[
            pltpu.SMEM((3, unit_count), jnp.int32),
            pltpu.VMEM(spikes.shape, jnp.int32),
            pltpu.VMEM(weights.shape, BF16),
            pltpu.VMEM((trials * delays + rows, neurons), F32),
            pltpu.VMEM((delays, up(rows, 16), neurons), BF16),
            pltpu.VMEM((2 * plan.lanes * plan.blocks, rows, 128), F32),
            pltpu.SemaphoreType.DMA((4,)),
            pltpu.SemaphoreType.DMA((unit_count // chunk,)),
        ],
        compiler_params=params(52),
        cost_estimate=cost(2 * unit_count * 256 * neurons * 128, 2 * unit_count * neurons * 128),
        name="payload",
    )(destination, target_block, delay_slot, spikes, weights)


def known_kernel(spikes, population, history, kernel, out, series, fresh, lags):
    steps, trials, neurons = spikes.shape
    pops, kinds, _, taps = history.shape
    group = kinds * trials
    lane = lax.broadcasted_iota(jnp.int32, (pops * group, taps), 1)
    for pop in range(pops):
        for kind in range(kinds):
            start = pop * group + kind * trials
            series[start : start + trials, :] = history[pop, kind]
    flip = lax.broadcasted_iota(jnp.int32, (taps, taps), 0) + lax.broadcasted_iota(
        jnp.int32, (taps, taps), 1
    )
    flip = (flip == taps - 1).astype(F32).astype(BF16)
    back = dot(series[...].astype(BF16), flip)

    which = lax.broadcasted_iota(jnp.int32, (8, neurons), 0)
    member = (which == population[...]).astype(F32).astype(BF16)
    rows = spikes[...].reshape(steps * trials, neurons).astype(F32).astype(BF16)
    rates = (dot(member, rows, NT) / (neurons / pops)).astype(BF16)
    fresh[...] = jnp.zeros_like(fresh)
    row = lax.broadcasted_iota(jnp.int32, (steps * trials, taps), 0)
    column = lax.broadcasted_iota(jnp.int32, (steps * trials, taps), 1)
    for trial in range(trials):
        place = (row == (taps - 1 - column) * trials + trial).astype(F32).astype(BF16)
        placed = dot(rates, place)
        for pop in range(pops):
            fresh[pop * group + trial : pop * group + trial + 1, :] = placed[pop : pop + 1, :]
    lags[...] = jnp.zeros_like(lags)
    recent = fresh[...]
    for step in range(steps):
        shifted = jnp.where(lane >= taps - step, recent, back)
        if step:
            shifted = pltpu.roll(shifted, step, 1)
        for part in range(pops * kinds):
            for trial in range(trials):
                row = part * trials + trial
                spot = trial * steps + step
                lags[part, spot : spot + 1, :] = shifted[row : row + 1, :]
    total = dot(kernel[:, 0:taps], lags[0].astype(BF16), NT)
    for part in range(1, pops * kinds):
        total += dot(kernel[:, part * taps : (part + 1) * taps], lags[part].astype(BF16), NT)
    out[...] = total


def known_lfp(spikes, population, history, kernel):
    pops, kinds, trials, taps = history.shape
    channels = kernel.shape[0]
    return pl.pallas_call(
        known_kernel,
        out_shape=jax.ShapeDtypeStruct((channels, 128), F32),
        in_specs=[VMEM] * 4,
        out_specs=VMEM,
        scratch_shapes=[
            pltpu.VMEM((pops * kinds * trials, taps), F32),
            pltpu.VMEM((pops * kinds * trials, taps), F32),
            pltpu.VMEM((pops * kinds, 128, taps), F32),
        ],
        compiler_params=params(16),
        cost_estimate=cost(2 * channels * 128 * pops * kinds * taps * 4, 2 * kernel.size),
        name="known_lfp",
    )(spikes, population, history, kernel)


def pack_signal(plan, values):
    high, low = both(values)
    if not plan.compact:
        return jnp.concatenate([high, low], axis=0)
    half = plan.signal // 2
    out = high[:half]
    for index, piece in enumerate((high[half:], low[:half], low[half:]), 1):
        out = out + pltpu.roll(piece, index * plan.tile, 1)
    return out


def unpack_signal(plan, rows):
    if not plan.compact:
        half = plan.packed // 2
        return rows[:half] + rows[half:]
    lane = lax.broadcasted_iota(jnp.int32, rows.shape, 1)
    pieces = [rows] + [pltpu.roll(rows, 128 - index * plan.tile, 1) for index in (1, 2, 3)]
    value = jnp.concatenate([pieces[0] + pieces[2], pieces[1] + pieces[3]], axis=0)
    lane = lax.broadcasted_iota(jnp.int32, value.shape, 1)
    return jnp.where(lane < plan.tile, value, 0.0)


def compress_kernel(
    plan, mine, got, given, cycle, start, known, taps, keep, send, carried, signal, room
):
    trials, steps, delays, blocks = plan.trials, plan.steps, plan.delays, plan.blocks
    me = lax.axis_index("area")
    signal[...] = jnp.zeros_like(signal)
    room[...] = jnp.zeros_like(room)
    owner = lax.broadcasted_iota(jnp.int32, (plan.signal_lanes, 128), 0).astype(F32)

    def pair(index, _):
        sums = jnp.zeros((2 * plan.signal, plan.signal_lanes), F32)
        for bit in range(2):
            lane = 2 * index + bit
            own = (lane == 0).astype(F32)
            place = lax.bitwise_xor(2 * lane, me)
            first = (lax.shift_right_logical(place, 1) * plan.pops).astype(F32)
            tops, members = [], []
            for block in range(blocks):
                arriving = mine[lane * blocks + block] + got[lane * blocks + block]
                early = arriving[0 : trials * delays] + own * cycle[block]
                arriving = jnp.concatenate([early, arriving[trials * delays :]], axis=0)
                facts = given[lane, block * 8 : block * 8 + 8]
                last = facts[0:trials]
                leak = facts[trials : trials + 1] + facts[trials + 1 : trials + 2]
                population = facts[trials + 2 : trials + 3]
                membrane = own * start[block]
                for step in range(steps):
                    current = arriving[step * trials : (step + 1) * trials]
                    membrane = jnp.where(last < step, leak * membrane + current, 0.0)
                spot = block * plan.each
                room[bit, spot : spot + trials] = membrane
                room[bit, spot + trials : spot + plan.each] = arriving[trials * steps :]
                tops.append(arriving[0 : plan.signal])
                members.append((owner == population + first).astype(F32).astype(BF16))
            high, low = both(jnp.concatenate(tops, axis=1))
            stacked = jnp.concatenate([high, low], axis=0).astype(BF16)
            sums += dot(stacked, jnp.concatenate(members, axis=1), NT)
            channels, reach = [], []
            for core in range(2):
                there = lax.bitwise_xor(place, core)
                rows = known[there]
                packed = rows[0:8]
                for group in range(1, plan.groups):
                    packed += pltpu.roll(rows[group * 8 : group * 8 + 8], group * plan.width, 1)
                channels.append(packed)
                reach.append(taps[there])
            reach = jnp.concatenate(reach, axis=0).astype(BF16)
            spot = pl.multiple_of(lane * 2 * plan.taps, 16)
            carried[pl.ds(spot, 2 * plan.taps)] = reach
            if bit:
                base = pl.multiple_of(index * plan.slot(0), 16)
                send[pl.ds(base, plan.main_up)] = room[bit].astype(BF16)
                spot = pl.multiple_of(base + plan.main_up, 16)
                send[pl.ds(spot, 16)] = jnp.concatenate(channels, axis=0).astype(BF16)
                spot = pl.multiple_of(base + plan.held, 16)
                send[pl.ds(spot, 2 * plan.taps)] = reach
            else:
                base = pl.multiple_of(index * plan.held, 8)
                keep[pl.ds(base, plan.main_up)] = room[bit]
                keep[pl.ds(base + plan.main_up, 8)] = channels[0]
                keep[pl.ds(base + plan.main_up + 8, 8)] = channels[1]
        signal[...] += sums[: plan.signal] + sums[plan.signal :]
        return 0

    pairs = plan.lanes // 2
    lax.fori_loop(0, pairs, pair, 0, unroll=min(pairs, 4))
    pieces = []
    for tile in range(plan.tiles):
        values = signal[:, tile * 128 : tile * 128 + plan.tile]
        if plan.tile < 128:
            blank = jnp.zeros((plan.signal, 128 - plan.tile), F32)
            values = jnp.concatenate([values, blank], axis=1)
        pieces.append(values)
    values = jnp.concatenate(pieces, axis=0) if plan.tiles > 1 else pieces[0]
    keep[pairs * plan.held :] = values
    put_signal(plan, send, pairs * plan.slot(0), values)


def put_signal(plan, out, base, values):
    rows = pack_signal(plan, values)
    if plan.packed_up > plan.packed:
        blank = jnp.zeros((plan.packed_up - plan.packed, 128), F32)
        rows = jnp.concatenate([rows, blank], axis=0)
    out[base:] = rows.astype(BF16)


def compress(plan, mine, got, given, cycle, start, known, taps):
    return pl.pallas_call(
        functools.partial(compress_kernel, plan),
        out_shape=(plan.keep(plan.lanes // 2), plan.send(plan.lanes // 2, 0), plan.carried()),
        in_specs=[VMEM] * 7,
        out_specs=(VMEM,) * 3,
        scratch_shapes=[
            pltpu.VMEM((plan.signal, plan.signal_lanes), F32),
            pltpu.VMEM((2, plan.main_up, 128), F32),
        ],
        compiler_params=params(32),
        name="compress",
    )(mine, got, given, cycle, start, known, taps)


def fold_kernel(plan, slots, stage, direct, held, got, carried, keep, *refs):
    taps = 2 * plan.taps
    if direct:
        sends, (now, room) = refs[:-2], refs[-2:]
    else:
        sends, (now,) = refs[:1], refs[1:]
    def spot_of(lane, stage):
        rest = lane & ((1 << stage) - 1)
        return (lane >> (stage + 1)) * plan.slot(stage) + plan.held + rest * taps

    for lane in range(plan.lanes):
        rows = slice(lane * taps, (lane + 1) * taps)
        if lane >> stage & 1:
            spot = spot_of(lane, stage)
            now[rows] = got[spot : spot + taps]
        else:
            now[rows] = carried[rows]
    size = plan.slot(stage)
    tail = got[slots * size : slots * size + plan.packed_up].astype(F32)[: plan.packed]
    tail = unpack_signal(plan, tail)
    tail = tail + held[slots * plan.held :]
    left = 1 if direct else slots // 2
    for slot in range(slots):
        rows = got[slot * size : slot * size + plan.held].astype(F32)
        rows = rows + held[slot * plan.held : (slot + 1) * plan.held]
        if direct and slot:
            out = sends[slot - 1]
            room[0 : plan.main] = rows[: plan.main]
            room[plan.main : plan.main + plan.packed] = pack_signal(plan, tail)
            out[0 : plan.last] = room[...].astype(BF16)
            out[plan.last : plan.last + 16] = rows[plan.main_up :].astype(BF16)
            span = plan.lanes // 4 * taps
            out[plan.last + 16 :] = now[slot * span : (slot + 1) * span]
        elif slot % 2:
            base = slot // 2 * plan.slot(stage + 1)
            sends[0][base : base + plan.held] = rows.astype(BF16)
        else:
            keep[slot // 2 * plan.held : (slot // 2 + 1) * plan.held] = rows
    keep[left * plan.held :] = tail
    if not direct:
        for lane in range(plan.lanes):
            if lane >> (stage + 1) & 1:
                spot = spot_of(lane, stage + 1)
                sends[0][spot : spot + taps] = now[lane * taps : (lane + 1) * taps]
        put_signal(plan, sends[0], left * plan.slot(stage + 1), tail)


def fold(plan, slots, stage, direct, held, got, carried):
    left = 1 if direct else slots // 2
    scratch = []
    sends = (plan.send(left, stage + 1),)
    if direct:
        sends = (plan.direct(),) * (slots - 1)
        scratch = [pltpu.VMEM((plan.last, 128), F32)]
    return pl.pallas_call(
        functools.partial(fold_kernel, plan, slots, stage, direct),
        out_shape=(plan.keep(left),) + sends + (plan.carried(),),
        in_specs=[VMEM] * 3,
        out_specs=(VMEM,) * (2 + len(sends)),
        scratch_shapes=scratch,
        compiler_params=params(32),
        name="fold",
    )(held, got, carried)


def finish_kernel(plan, held, carried, *refs):
    gots, (membrane, cycle, own, other, mixed, reach, late, parts) = refs[:3], refs[3:]
    trials, steps, delays = plan.trials, plan.steps, plan.delays
    taps = 2 * plan.taps
    rows = held[0 : plan.held]
    main, channels = rows[: plan.main_up], rows[plan.main_up :]
    tail = held[plan.held :]
    parts[0 : plan.main] = main[: plan.main]
    for got in gots:
        arrived = got[0 : plan.last].astype(F32)
        parts[0 : plan.main] += arrived[: plan.main]
        channels = channels + got[plan.last : plan.last + 16].astype(F32)
        tail = tail + unpack_signal(plan, arrived[plan.main : plan.main + plan.packed])
    for block in range(plan.blocks):
        lanes = slice(block * 128, block * 128 + 128)
        base = block * plan.each
        membrane[:, lanes] = parts[base : base + trials]
        for delay in range(delays):
            spot = base + trials * (1 + delay)
            cycle[:, delay, lanes] = parts[spot : spot + trials]

    me = lax.shift_right_logical(lax.axis_index("area"), 1)
    span = plan.lanes // 4
    pops, wide = plan.pops, plan.taps_lanes // 128
    for lane in range(plan.lanes):
        far, near = divmod(lane, span)
        if far:
            spot = plan.last + 16 + near * taps
            slot = gots[far - 1][spot : spot + taps]
        else:
            slot = carried[lane * taps : (lane + 1) * taps]
        slot = slot.astype(F32)
        spot = lax.bitwise_xor(me, lane)
        for core in range(2):
            for tile in range(wide):
                top = core * plan.taps + tile * pops
                mixed[core, spot, 0:pops, tile * 128 : tile * 128 + 128] = slot[top : top + pops]
    for core in range(2):
        for lane in range(plan.lanes):
            reach[core, lane * pops : (lane + 1) * pops] = mixed[core, lane, 0:pops]
    new = lax.broadcasted_iota(jnp.int32, (plan.width, plan.signal), 0)
    old = lax.broadcasted_iota(jnp.int32, (plan.width, plan.signal), 1)
    order = (old == (new % steps) * trials + new // steps).astype(F32).astype(BF16)
    signal = (tail / plan.pop_size).astype(BF16)
    signal = [
        dot(order, signal[tile * plan.signal : (tile + 1) * plan.signal]).astype(BF16)
        for tile in range(plan.tiles)
    ]
    step_of = lax.broadcasted_iota(jnp.int32, (plan.width, 128), 0) % steps
    late[...] = jnp.zeros_like(late)
    sums = []
    for core in range(2):
        products = None
        for tile in range(plan.tiles):
            right = reach[core, tile * 128 : tile * 128 + plan.tile].astype(BF16)
            one = dot(signal[tile][:, : plan.tile], right)
            products = one if products is None else products + one
        value = jnp.zeros((plan.width, 128), F32)
        width = products.shape[1]
        for lag in range(1, steps):
            moved = products
            if lag > 1:
                moved = pltpu.roll(products, width - (lag - 1) * plan.share, 1)
            moved = pltpu.roll(moved[:, 0:128], lag, 0)
            value = value + jnp.where(step_of >= lag, moved, 0.0)
        sums.append(value)
    lane = lax.broadcasted_iota(jnp.int32, (plan.width, 128), 1)
    late[0 : plan.width] = jnp.where(lane < 64, sums[0], pltpu.roll(sums[1], 64, 1))
    fresh = jnp.transpose(late[...])
    lane = lax.broadcasted_iota(jnp.int32, (8, 128), 1)
    row = lax.broadcasted_iota(jnp.int32, (8, 128), 0)
    for core, out in enumerate((own, other)):
        value = channels[core * 8 : core * 8 + 8]
        for group in range(plan.groups):
            piece = fresh[core * 64 + group * 8 : core * 64 + group * 8 + 8]
            piece = jnp.where(lane < plan.width, piece, 0.0)
            if group:
                piece = pltpu.roll(piece, group * plan.width, 1)
            value = value + piece
        out[...] = value


def finish(plan, neurons, held, carried, gots):
    trials, delays = plan.trials, plan.delays
    part = jax.ShapeDtypeStruct((8, 128), F32)
    return pl.pallas_call(
        functools.partial(finish_kernel, plan),
        out_shape=(
            jax.ShapeDtypeStruct((trials, neurons), F32),
            jax.ShapeDtypeStruct((trials, delays, neurons), F32),
            part,
            part,
        ),
        in_specs=[VMEM] * (2 + len(gots)),
        out_specs=(VMEM,) * 4,
        scratch_shapes=[
            pltpu.VMEM((2, plan.lanes, 8, plan.taps_lanes), F32),
            pltpu.VMEM((2, plan.signal_lanes, plan.taps_lanes), F32),
            pltpu.VMEM((128, 128), F32),
            pltpu.VMEM((plan.main_up, 128), F32),
        ],
        compiler_params=params(16),
        name="finish",
    )(held, carried, *gots)


def lfp_kernel_body(plan, own, got, out):
    value = own[...] + got[...]
    pieces = [value]
    for group in range(1, plan.groups):
        pieces.append(pltpu.roll(value, 128 - group * plan.width, 1))
    value = jnp.concatenate(pieces, axis=0) if plan.groups > 1 else value
    out[...] = value[0 : plan.share, 0 : plan.width]


def lfp_sum(plan, own, got):
    return pl.pallas_call(
        functools.partial(lfp_kernel_body, plan),
        out_shape=jax.ShapeDtypeStruct((plan.share, plan.width), F32),
        in_specs=[VMEM] * 2,
        out_specs=VMEM,
        name="lfp_sum",
    )(own, got)


def swap(values, bit, area_count):
    return lax.ppermute(values, "area", [(i, i ^ bit) for i in range(area_count)])


def body(
    spikes,
    weights,
    destination,
    target_block,
    delay_slot,
    population,
    leak_rate,
    membrane_start,
    cycle_start,
    history,
    lfp_kernel,
):
    area_count = lax.axis_size("area")
    neurons = weights.shape[1]
    blocks = neurons // 128
    trials, steps = spikes.shape[:2]
    delays = cycle_start.shape[1]
    channels = lfp_kernel.shape[0]
    pops, kinds, _, taps = history.shape
    plan = Plan(area_count, trials, steps, delays, neurons, pops, channels)
    share = plan.share
    spikes = jnp.transpose(spikes, (1, 0, 2))
    top = area_count // 4
    far = [top, 2 * top, 3 * top]

    order = lax.broadcasted_iota(jnp.int32, spikes.shape, 0)
    last = jnp.max(jnp.where(spikes > 0, order, -1), axis=0)
    leak = lax.reduce_precision(leak_rate, 8, 7)
    facts = jnp.concatenate(
        [
            last.astype(F32),
            leak[None],
            (leak_rate - leak)[None],
            population.astype(F32)[None],
            jnp.zeros((5 - trials, neurons), F32),
        ]
    ).astype(BF16)
    facts = jnp.transpose(facts.reshape(8, blocks, 128), (1, 0, 2)).reshape(blocks * 8, 128)
    facts = jnp.stack([facts] + [swap(facts, bit, area_count) for bit in far])

    mine, goes, token = payload_sums(
        plan, spikes, weights, destination[:, 0], target_block, delay_slot
    )
    facts = facts + token[0, 0].astype(BF16)
    got = swap(goes, 1, area_count)
    bit = top // 2
    while bit > 1:
        more = swap(facts.reshape(-1, 128), bit, area_count).reshape(facts.shape)
        facts = jnp.stack([facts, more], axis=1).reshape(-1, blocks * 8, 128)
        bit //= 2
    facts = facts.astype(F32)

    flat = lax.optimization_barrier(lfp_kernel.reshape(channels, -1))
    known = known_lfp(spikes, population[None], history, flat)
    known = known.reshape(area_count, share, 128)
    known = jnp.pad(known, ((0, 0), (0, plan.groups * 8 - share), (0, 0)))
    reach = steps - 1
    first = [flat[:, (pop * kinds + 1) * taps :][:, :reach] for pop in range(pops)]
    first = jnp.stack(first, axis=1).astype(F32).reshape(area_count, share, pops, reach)
    first = jnp.transpose(first, (0, 2, 3, 1)).reshape(area_count, pops, reach * share)
    first = jnp.pad(first, ((0, 0), (0, 0), (0, plan.taps_lanes - reach * share)))
    first = first.reshape(area_count, pops, plan.taps_lanes // 128, 128)
    first = jnp.transpose(first, (0, 2, 1, 3)).reshape(area_count, -1, 128)
    first = jnp.pad(first, ((0, 0), (0, plan.taps - first.shape[1]), (0, 0)))

    cycle = jnp.transpose(cycle_start, (1, 0, 2)).reshape(delays * trials, blocks, 128)
    cycle = jnp.transpose(cycle, (1, 0, 2))
    start = jnp.transpose(membrane_start.reshape(trials, blocks, 128), (1, 0, 2))
    keep, send, carried = compress(plan, mine, got, facts, cycle, start, known, first)

    slots, stage = plan.lanes // 2, 0
    got = swap(send, 2, area_count)
    while slots > 4:
        keep, send, carried = fold(plan, slots, stage, False, keep, got, carried)
        slots, stage = slots // 2, stage + 1
        got = swap(send, 2 << stage, area_count)
    keep, *sends, carried = fold(plan, slots, stage, True, keep, got, carried)
    gots = [swap(send, bit, area_count) for send, bit in zip(sends, far)]
    membrane, cycle_out, own, other = finish(plan, neurons, keep, carried, gots)
    lfp = lfp_sum(plan, own, swap(other, 1, area_count))
    return membrane, cycle_out, lfp


def solution(mesh):
    return jax.shard_map(
        body,
        mesh=mesh,
        in_specs=(
            P("runs", None, "area"),
            P("area", None, None),
            P("area", None),
            P("area"),
            P("area"),
            P("area"),
            P("area"),
            P("runs", "area"),
            P("runs", None, "area"),
            P("area", None, "runs", None),
            P(None, "area", None, None),
        ),
        out_specs=(P("runs", "area"), P("runs", None, "area"), P("area", "runs")),
        check_vma=False,
    )
```

time: 50.6 us -> 51.8 us (1.024)
  waiting for transfers between devices: 18.2 us -> 10.7 us
  other arithmetic: 0.92 us -> 6 us
  Pallas kernels: 7.19 us -> 9.66 us
  local copies, waits for them, and re-layouts: 9.06 us -> 10.4 us
    ppermute x9 -> x10, waiting for transfers between devices: 18.2 us -> 10.7 us  [swap(): lax.ppermute(values, 'area', [(i, i ^ bit) for i in range(area_count)])]
    pallas_call x4, Pallas kernels: 5.03 us -> 8.11 us  [the longest x1 5.26 us: payload_sums(): pl.pallas_call(payload_kernel, out_shape=(half, half, jax.ShapeDtypeStruc...]
    add x0 -> x2, other arithmetic: none -> 2.73 us  [body(): facts = facts + token[0, 0].astype(BF16)]
    another operation x7 -> x4, local copies, waits for them, and re-layouts: 0.13 us -> 2.59 us  [body(): jnp.stack(first, axis=1).astype(F32).reshape(area_count, share, pops, reach)]
    slice x7 -> x2, local copies, waits for them, and re-layouts: 2.56 us -> 0.58 us  [the longest x1 0.51 us: body(): facts = facts + token[0, 0].astype(BF16)]
    reshape x4, local copies, waits for them, and re-layouts: 1.43 us -> 3.14 us  [the longest x1 2.87 us: body(): flat = lax.optimization_barrier(lfp_kernel.reshape(channels, -1))]
    transpose x0 -> x1, other arithmetic: none -> 0.99 us  [body(): jnp.transpose(first, (0, 2, 3, 1)).reshape(area_count, pops, reach * share)]
    reduce_max x1, other arithmetic: 0.03 us -> 0.86 us  [body(): last = jnp.max(jnp.where(spikes > 0, order, -1), axis=0)]
  transfers between devices with their start and end apart: 9 -> 10, of which waited for: 7 -> 5; matrix products, arithmetic and copies ran while one was open for 4% -> 20% of each run, Pallas kernels for 9% -> 12%
where the time goes in v3:
time: 51.8 us; the launch traced here: 51.3 us
  starting transfers between devices  13.6 us (26%)
  waiting for transfers between devices  10.7 us (21%)
  local copies, waits for them, and re-layouts  10.4 us (20%)
  Pallas kernels  9.66 us (19%)
  other arithmetic  6 us (12%)
  between operations  0.88 us (2%)
    ppermute x10, starting transfers between devices, swap(): lax.ppermute(values, 'area', [(i, i ^ bit) for i in range(area_count)])  13.6 us
    ppermute x10, waiting for transfers between devices, swap(): lax.ppermute(values, 'area', [(i, i ^ bit) for i in range(area_count)])  10.7 us
    pallas_call x1, Pallas kernels, payload_sums(): pl.pallas_call(payload_kernel, out_shape=(half, half, jax.ShapeDtypeStruc...  5.26 us
    unnamed x22, local copies, waits for them, and re-layouts  4 us
    reshape x1, local copies, waits for them, and re-layouts, body(): flat = lax.optimization_barrier(lfp_kernel.reshape(channels, -1))  2.87 us
    add x2, other arithmetic, body(): facts = facts + token[0, 0].astype(BF16)  2.73 us
    another operation x4, local copies, waits for them, and re-layouts, body(): jnp.stack(first, axis=1).astype(F32).reshape(area_count, share, pops, reach)  2.59 us
    concatenate x2, other arithmetic, body(): jnp.concatenate([last.astype(F32), leak[None], (leak_rate - leak)[None],...  1.37 us
  transfers between devices with their start and end apart: 10, of which 5 were waited for; matrix products, arithmetic and copies ran while one was open for 20% of the time, Pallas kernels for 12%

profile of v3, /device:TPU:0, one launch (start us, length us, event | category | flops | bytes accessed | tf_op | source)
XLA Modules:
  0.0 51.3 jit_solution(10771643913429300334)
XLA Ops:
  0.6 0.7 %fusion.2 = bf16[1,3,128]{2,1,0:T(4,128)(2,1)S(1)} fusion(s32[384]{0:T(512)} %param.16), kind=kLoop, calls=%fused_computation.14 | loop fusion | flops 768 | bytes 2304 | tf_op jit(solution)/shard_map/concatenate | solution.py:578
  1.3 0.7 %fusion.3 = (bf16[1,3,128]{2,1,0:T(4,128)(2,1)S(1)}, bf16[1,3,128]{2,1,0:T(4,128)(2,1)S(1)}) fusion(f32[384]{0:T(512)} %param.17), kind=kLoop, calls=%fused_computation.15 | loop fusion | flops 1536 | bytes 3072 | tf_op jit(solution)/shard_map/concatenate | solution.py:578
  2.0 0.9 %select_reduce_fusion = s32[4,384]{1,0:T(4,128)S(1)} fusion(s32[4,10,384]{2,0,1:T(4,128)} %param.11), kind=kLoop, calls=%fused_computation.1 | loop fusion | flops 44544 | bytes 67584 | tf_op jit(solution)/shard_map/reduce_max | solution.py:576
  2.9 5.1 %collective-permute-start.3 = (bf16[24,128]{1,0:T(8,128)(2,1)S(1)}, bf16[24,128]{1,0:T(8,128)(2,1)S(1)}, u32[]{:S(2)}, u32[]{:S(2)}) collective-permute-start(bf16[24,128]{1,0:T(8,128)(2,1)S(1)} %bitcast.62), channel_id=1, source_target_pairs={{0,12},{1,13},{2,14},{3,15},{4,8},{5,9},{6,10},{7,11},{8,4},{9,5},... | collective-permute-start | bytes 18440 | tf_op jit(solution)/shard_map/ppermute | solution.py:546
  8.1 0.0 collective-permute-start.2
  8.1 0.6 %collective-permute-start.1 = (bf16[24,128]{1,0:T(8,128)(2,1)S(1)}, bf16[24,128]{1,0:T(8,128)(2,1)}, u32[]{:S(2)}, u32[]{:S(2)}) collective-permute-start(bf16[24,128]{1,0:T(8,128)(2,1)S(1)} %bitcast.64), channel_id=1, source_target_pairs={{0,4},{1,5},{2,6},{3,7},{4,0},{5,1},{6,2},{7,3},{8,12},{9,13},{10,... | collective-permute-start | bytes 18440 | tf_op jit(solution)/shard_map/ppermute | solution.py:546
  8.7 0.8 %copy-done = s32[4,10,384]{2,0,1:T(4,128)S(1)} copy-done((s32[4,10,384]{2,0,1:T(4,128)S(1)}, s32[4,10,384]{2,0,1:T(4,128)}, u32[]{:S(2)}) %copy-start) | copy-done | bytes 61464
  9.5 0.7 %copy-done.4 = s32[96,1]{0,1:T(1,128)S(1)} copy-done((s32[96,1]{0,1:T(1,128)S(1)}, s32[96,1]{0,1:T(1,128)}, u32[]{:S(2)}) %copy-start.4) | copy-done | bytes 408
  10.2 0.7 %copy-done.5 = s32[96]{0:T(128)S(1)} copy-done((s32[96]{0:T(128)S(1)}, s32[96]{0:T(128)}, u32[]{:S(2)}) %copy-start.5) | copy-done | bytes 408
  10.8 0.7 %copy-done.6 = s32[96]{0:T(128)S(1)} copy-done((s32[96]{0:T(128)S(1)}, s32[96]{0:T(128)}, u32[]{:S(2)}) %copy-start.6) | copy-done | bytes 408
  11.5 5.3 %payload.1 = (f32[24,56,128]{2,1,0:T(8,128)S(1)}, f32[24,56,128]{2,1,0:T(8,128)}, f32[8,128]{1,0:T(8,128)S(1)}) custom-call(s32[96]{0:T(128)S(1)} %bitcast.57, s32[96]{0:T(128)S(1)} %copy-done.5, s32[96]{0:T(128)S(1)} %copy-done.6, s32[10,4,384]{2,1,0:T(4,128)S(1)} %bitcast.52, bf16[96,384,128]{2,1,0:T(8,128)(2,1)} %weights.1), custom_call_target="tpu_custom_call" | custom-call | flops 2415919104 | bytes 9437184 | tf_op jit(solution)/shard_map/payload/pallas_call | solution.py:148
  16.8 0.1 collective-permute-start
  16.8 2.9 %reshape.128.kernel = bf16[384,2048]{1,0:T(8,128)(2,1)S(1)} reshape(bf16[384,4,2,256]{3,2,1,0:T(2,128)(2,1)} %param.21) | data formatting | bytes 3145728 | tf_op jit(solution)/shard_map/reshape | solution.py:602
  19.7 0.0 copy-start.9
  19.7 0.0 copy-start.1
  19.7 0.0 copy-start.7
  19.7 0.1 fusion.5
  19.8 0.8 %copy.19 = bf16[16,24,1,9]{1,3,0,2:T(8,128)(2,1)} copy(bf16[16,24,1,9]{3,1,0,2:T(8,128)(2,1)S(1)} %bitcast.61) | data formatting | bytes 13824 | tf_op jit(solution)/shard_map/stack | solution.py:608
  20.6 0.8 %copy.22 = bf16[16,24,1,9]{1,3,0,2:T(8,128)(2,1)} copy(bf16[16,24,1,9]{3,1,0,2:T(8,128)(2,1)S(1)} %bitcast.60) | data formatting | bytes 13824 | tf_op jit(solution)/shard_map/stack | solution.py:608
  21.4 0.8 %copy.21 = bf16[16,24,1,9]{1,3,0,2:T(8,128)(2,1)} copy(bf16[16,24,1,9]{3,1,0,2:T(8,128)(2,1)S(1)} %bitcast.59) | data formatting | bytes 13824 | tf_op jit(solution)/shard_map/stack | solution.py:608
  22.2 0.2 copy.20
  22.4 1.0 %maximum_bitcast_fusion = bf16[16,4,9,24]{3,2,0,1:T(8,128)(2,1)S(1)} fusion(bf16[16,24,1,9]{1,3,0,2:T(8,128)(2,1)} %copy.22, bf16[16,24,1,9]{1,3,0,2:T(8,128)(2,1)} %copy.21, bf16[16,24,1,9]{1,3,0,2:T(8,128)(2,1)S(1)} %copy.20, bf16[16,24,1,9]{1,3,0,2:T(8,128)(2,1)} %copy.19), kind=kLoop, calls=%fused_computation | loop fusion | flops 41472 | bytes 55296 | tf_op jit(solution)/shard_map/transpose | solution.py:609
  23.4 0.2 reshape.130
  23.6 0.0 copy-start.8
  23.7 0.0 copy-start.2
  23.7 1.0 %known_lfp.1 = f32[384,128]{1,0:T(8,128)S(1)} custom-call(s32[10,4,384]{2,1,0:T(4,128)S(1)} %bitcast.53, s32[1,384]{1,0:T(1,128)S(1)} %broadcast_in_dim.15.population, f32[4,2,4,256]{3,2,1,0:T(4,128)S(1)} %copy-done.7, bf16[384,2048]{1,0:T(8,128)(2,1)S(1)} %reshape.128.kernel), custom_call_target="tpu_custom_call" | custom-call | flops 805306368 | bytes 1572864 | tf_op jit(solution)/shard_map/known_lfp/pallas_call | solution.py:216
  24.8 0.5 %slice.24 = bf16[1,1]{1,0:T(2,128)(2,1)} slice(bf16[8,128]{1,0:T(8,128)(2,1)S(1)} %convert.33), slice={[0:1], [0:1]} | slice | bytes 4 | tf_op jit(solution)/shard_map/slice | solution.py:593
  25.4 0.0 collective-permute-done.3
  25.4 0.0 collective-permute-done.2
  25.4 1.4 %maximum_add_fusion.1 = bf16[4,24,128]{2,1,0:T(8,128)(2,1)S(1)} fusion(bf16[1,24,128]{2,1,0:T(8,128)(2,1)S(1)} %bitcast.67, bf16[1,24,128]{2,1,0:T(8,128)(2,1)} %bitcast.16, bf16[1,24,128]{2,1,0:T(8,128)(2,1)} %bitcast.15, bf16[1,24,128]{2,1,0:T(8,128)(2,1)S(1)} %bitcast.65, bf16[]{:T(256)} %bitcast.13), kind=kLoop, calls=%fused_computation.6 | loop fusion | flops 49152 | bytes 49154 | tf_op jit(solution)/shard_map/add | solution.py:593
  26.8 1.7 %collective-permute-start.4 = (bf16[96,128]{1,0:T(8,128)(2,1)S(1)}, bf16[96,128]{1,0:T(8,128)(2,1)S(1)}, u32[]{:S(2)}, u32[]{:S(2)}) collective-permute-start(bf16[96,128]{1,0:T(8,128)(2,1)S(1)} %bitcast.70), channel_id=1, source_target_pairs={{0,2},{1,3},{2,0},{3,1},{4,6},{5,7},{6,4},{7,5},{8,10},{9,11},{10,... | collective-permute-start | bytes 73736 | tf_op jit(solution)/shard_map/ppermute | solution.py:546
  28.5 1.4 %maximum_add_fusion = bf16[4,1,24,128]{3,2,1,0:T(8,128)(2,1)S(1)} fusion(bf16[1,1,24,128]{3,2,1,0:T(8,128)(2,1)S(1)} %bitcast.68, bf16[1,1,24,128]{3,2,1,0:T(8,128)(2,1)} %bitcast.11, bf16[1,1,24,128]{3,2,1,0:T(8,128)(2,1)} %bitcast.9, bf16[1,1,24,128]{3,2,1,0:T(8,128)(2,1)S(1)} %bitcast.66, bf16[]{:T(256)} %bitcast.13), kind=kLoop, calls=%fused_computation.5 | loop fusion | flops 49152 | bytes 49154 | tf_op jit(solution)/shard_map/add | solution.py:593
  29.8 0.8 %collective-permute-done.4 = bf16[96,128]{1,0:T(8,128)(2,1)S(1)} collective-permute-done((bf16[96,128]{1,0:T(8,128)(2,1)S(1)}, bf16[96,128]{1,0:T(8,128)(2,1)S(1)}, u32[]{:S(2)}, u32[]{:S(2)}) %collective-permute-start.4) | collective-permute-done | bytes 24608 | tf_op jit(solution)/shard_map/ppermute | solution.py:546
  30.7 0.5 %compress.1 = (f32[360,128]{1,0:T(8,128)S(1)}, bf16[416,128]{1,0:T(8,128)(2,1)S(1)}, bf16[128,128]{1,0:T(8,128)(2,1)S(1)}) custom-call(f32[24,56,128]{2,1,0:T(8,128)S(1)} %get-tuple-element.18.mine, f32[24,56,128]{2,1,0:T(8,128)S(1)} %collective-permute-done.got, f32[8,24,128]{2,1,0:T(8,128)S(1)} %bitcast_convert_fusion.given, f32[3,16,128]{2,1,0:T(8,128)S(1)} %bitcast.55, ...), custom_call_target="tpu_custom_call" | custom-call | tf_op jit(solution)/shard_map/compress/pallas_call | solution.py:341
  31.3 1.7 %collective-permute-start.5 = (bf16[416,128]{1,0:T(8,128)(2,1)S(1)}, bf16[416,128]{1,0:T(8,128)(2,1)S(1)}, u32[]{:S(2)}, u32[]{:S(2)}) collective-permute-start(bf16[416,128]{1,0:T(8,128)(2,1)S(1)} %get-tuple-element.22), channel_id=1, source_target_pairs={{0,2},{1,3},{2,0},{3,1},{4,6},{5,7},{6,4},{7,5},{8,10},{9,11},{10,... | collective-permute-start | bytes 319496 | tf_op jit(solution)/shard_map/ppermute | solution.py:546
  32.9 3.1 %collective-permute-done.5.got = bf16[416,128]{1,0:T(8,128)(2,1)S(1)} collective-permute-done((bf16[416,128]{1,0:T(8,128)(2,1)S(1)}, bf16[416,128]{1,0:T(8,128)(2,1)S(1)}, u32[]{:S(2)}, u32[]{:S(2)}) %collective-permute-start.5) | collective-permute-done | bytes 106528 | tf_op jit(solution)/shard_map/ppermute | solution.py:546
  36.0 0.2 fold.1
  36.2 1.4 %collective-permute-start.6 = (bf16[128,128]{1,0:T(8,128)(2,1)S(1)}, bf16[128,128]{1,0:T(8,128)(2,1)S(1)}, u32[]{:S(2)}, u32[]{:S(2)}) collective-permute-start(bf16[128,128]{1,0:T(8,128)(2,1)S(1)} %get-tuple-element.26), channel_id=1, source_target_pairs={{0,4},{1,5},{2,6},{3,7},{4,0},{5,1},{6,2},{7,3},{8,12},{9,13},{10,... | collective-permute-start | bytes 98312 | tf_op jit(solution)/shard_map/ppermute | solution.py:546
  37.6 2.9 %collective-permute-start.7 = (bf16[128,128]{1,0:T(8,128)(2,1)S(1)}, bf16[128,128]{1,0:T(8,128)(2,1)S(1)}, u32[]{:S(2)}, u32[]{:S(2)}) collective-permute-start(bf16[128,128]{1,0:T(8,128)(2,1)S(1)} %get-tuple-element.27), channel_id=1, source_target_pairs={{0,8},{1,9},{2,10},{3,11},{4,12},{5,13},{6,14},{7,15},{8,0},{9,1},... | collective-permute-start | bytes 98312 | tf_op jit(solution)/shard_map/ppermute | solution.py:546
  40.6 0.1 collective-permute-start.8
  40.6 0.0 collective-permute-done.6.refs_0_
  40.6 2.5 %collective-permute-done.7.refs_1_ = bf16[128,128]{1,0:T(8,128)(2,1)S(1)} collective-permute-done((bf16[128,128]{1,0:T(8,128)(2,1)S(1)}, bf16[128,128]{1,0:T(8,128)(2,1)S(1)}, u32[]{:S(2)}, u32[]{:S(2)}) %collective-permute-start.7) | collective-permute-done | bytes 32800 | tf_op jit(solution)/shard_map/ppermute | solution.py:546
  43.1 3.1 %collective-permute-done.8.refs_2_ = bf16[128,128]{1,0:T(8,128)(2,1)S(1)} collective-permute-done((bf16[128,128]{1,0:T(8,128)(2,1)S(1)}, bf16[128,128]{1,0:T(8,128)(2,1)S(1)}, u32[]{:S(2)}, u32[]{:S(2)}) %collective-permute-start.8) | collective-permute-done | bytes 32800 | tf_op jit(solution)/shard_map/ppermute | solution.py:546
  46.3 1.3 %finish.1 = (f32[4,384]{1,0:T(4,128)}, f32[4,4,384]{2,1,0:T(4,128)}, f32[8,128]{1,0:T(8,128)S(1)}, f32[8,128]{1,0:T(8,128)S(1)}) custom-call(f32[120,128]{1,0:T(8,128)S(1)} %get-tuple-element.24.held, bf16[128,128]{1,0:T(8,128)(2,1)S(1)} %get-tuple-element.25.carried, bf16[128,128]{1,0:T(8,128)(2,1)S(1)} %collective-permute-done.6.refs_0_, ...), custom_call_target="tpu_custom_call" | custom-call | tf_op jit(solution)/shard_map/finish/pallas_call | solution.py:505
  47.6 0.6 %copy-done.3 = f32[8,128]{1,0:T(8,128)} copy-done((f32[8,128]{1,0:T(8,128)}, f32[8,128]{1,0:T(8,128)S(1)}, u32[]{:S(2)}) %copy-start.3) | copy-done | bytes 4120
  48.2 1.2 %collective-permute-done.9.got = f32[8,128]{1,0:T(8,128)S(1)} collective-permute-done((f32[8,128]{1,0:T(8,128)S(1)}, f32[8,128]{1,0:T(8,128)S(1)}, u32[]{:S(2)}, u32[]{:S(2)}) %collective-permute-start.9) | collective-permute-done | bytes 4128 | tf_op jit(solution)/shard_map/ppermute | solution.py:546
  49.3 0.6 %copy-done.10 = f32[8,128]{1,0:T(8,128)} copy-done((f32[8,128]{1,0:T(8,128)}, f32[8,128]{1,0:T(8,128)S(1)}, u32[]{:S(2)}) %copy-start.10) | copy-done | bytes 4120
  49.9 1.4 %lfp_sum.1 = f32[24,40]{1,0:T(8,128)} custom-call(f32[8,128]{1,0:T(8,128)} %copy-done.3, f32[8,128]{1,0:T(8,128)} %copy-done.10), custom_call_target="tpu_custom_call" | custom-call | tf_op jit(solution)/shard_map/lfp_sum/pallas_call | solution.py:536
  (30 shorter events, 0.2 us)
Async XLA Ops:
  2.9 22.4 %collective-permute-start.3 = (bf16[24,128]{1,0:T(8,128)(2,1)S(1)}, bf16[24,128]{1,0:T(8,128)(2,1)S(1)}, u32[]{:S(2)}, u32[]{:S(2)}) collective-permute-start(bf16[24,128]{1,0:T(8,128)(2,1)S(1)} %bitcast.62), channel_id=1, source_target_pairs={{0,12},{1,13},{2,14},{3,15},{4,8},{5,9},{6,10},{7,11},{8,4},{9,5},... | collective-permute-start | bytes 18440 | tf_op jit(solution)/shard_map/ppermute | solution.py:546
  8.1 17.3 %collective-permute-start.2 = (bf16[24,128]{1,0:T(8,128)(2,1)S(1)}, bf16[24,128]{1,0:T(8,128)(2,1)}, u32[]{:S(2)}, u32[]{:S(2)}) collective-permute-start(bf16[24,128]{1,0:T(8,128)(2,1)S(1)} %bitcast.63), channel_id=1, source_target_pairs={{0,8},{1,9},{2,10},{3,11},{4,12},{5,13},{6,14},{7,15},{8,0},{9,1},... | collective-permute-start | bytes 18440 | tf_op jit(solution)/shard_map/ppermute | solution.py:546
  8.1 17.3 %collective-permute-start.1 = (bf16[24,128]{1,0:T(8,128)(2,1)S(1)}, bf16[24,128]{1,0:T(8,128)(2,1)}, u32[]{:S(2)}, u32[]{:S(2)}) collective-permute-start(bf16[24,128]{1,0:T(8,128)(2,1)S(1)} %bitcast.64), channel_id=1, source_target_pairs={{0,4},{1,5},{2,6},{3,7},{4,0},{5,1},{6,2},{7,3},{8,12},{9,13},{10,... | collective-permute-start | bytes 18440 | tf_op jit(solution)/shard_map/ppermute | solution.py:546
  8.7 0.8 %copy-start = (s32[4,10,384]{2,0,1:T(4,128)S(1)}, s32[4,10,384]{2,0,1:T(4,128)}, u32[]{:S(2)}) copy-start(s32[4,10,384]{2,0,1:T(4,128)} %param.11) | copy-start | bytes 184324
  9.5 0.7 %copy-start.4 = (s32[96,1]{0,1:T(1,128)S(1)}, s32[96,1]{0,1:T(1,128)}, u32[]{:S(2)}) copy-start(s32[96,1]{0,1:T(1,128)} %param.13) | copy-start | bytes 1156
  10.2 0.7 %copy-start.5 = (s32[96]{0:T(128)S(1)}, s32[96]{0:T(128)}, u32[]{:S(2)}) copy-start(s32[96]{0:T(128)} %target_block.1) | copy-start | bytes 1156
  10.8 0.7 %copy-start.6 = (s32[96]{0:T(128)S(1)}, s32[96]{0:T(128)}, u32[]{:S(2)}) copy-start(s32[96]{0:T(128)} %delay_slot.1) | copy-start | bytes 1156
  16.8 13.9 %collective-permute-start = (f32[24,56,128]{2,1,0:T(8,128)}, f32[24,56,128]{2,1,0:T(8,128)S(1)}, u32[]{:S(2)}, u32[]{:S(2)}) collective-permute-start(f32[24,56,128]{2,1,0:T(8,128)} %get-tuple-element.19), channel_id=1, source_target_pairs={{0,1},{1,0},{2,3},{3,2},{4,5},{5,4},{6,7},{7,6},{8,9},{9,8},{10,11... | collective-permute-start | bytes 2064392 | tf_op jit(solution)/shard_map/ppermute | solution.py:546
  19.7 3.9 %copy-start.9 = (s32[384]{0:T(512)S(1)}, s32[384]{0:T(512)}, u32[]{:S(2)}) copy-start(s32[384]{0:T(512)} %param.16) | copy-start | bytes 4612
  19.7 3.9 %copy-start.1 = (s32[4,10,384]{2,0,1:T(4,128)S(1)}, s32[4,10,384]{2,0,1:T(4,128)}, u32[]{:S(2)}) copy-start(s32[4,10,384]{2,0,1:T(4,128)} %param.11) | copy-start | bytes 184324
  19.7 3.9 %copy-start.7 = (f32[4,2,4,256]{3,2,1,0:T(4,128)S(1)}, f32[4,2,4,256]{3,2,1,0:T(4,128)}, u32[]{:S(2)}) copy-start(f32[4,2,4,256]{3,2,1,0:T(4,128)} %history.1) | copy-start | bytes 98308
  23.6 1.1 %copy-start.8 = (f32[4,4,384]{2,1,0:T(4,128)S(1)}, f32[4,4,384]{2,1,0:T(4,128)}, u32[]{:S(2)}) copy-start(f32[4,4,384]{2,1,0:T(4,128)} %param.19) | copy-start | bytes 73732
  23.7 7.0 %copy-start.2 = (f32[4,384]{1,0:T(4,128)S(1)}, f32[4,384]{1,0:T(4,128)}, u32[]{:S(2)}) copy-start(f32[4,384]{1,0:T(4,128)} %param.18) | copy-start | bytes 18436
  26.8 3.9 %collective-permute-start.4 = (bf16[96,128]{1,0:T(8,128)(2,1)S(1)}, bf16[96,128]{1,0:T(8,128)(2,1)S(1)}, u32[]{:S(2)}, u32[]{:S(2)}) collective-permute-start(bf16[96,128]{1,0:T(8,128)(2,1)S(1)} %bitcast.70), channel_id=1, source_target_pairs={{0,2},{1,3},{2,0},{3,1},{4,6},{5,7},{6,4},{7,5},{8,10},{9,11},{10,... | collective-permute-start | bytes 73736 | tf_op jit(solution)/shard_map/ppermute | solution.py:546
  31.3 4.7 %collective-permute-start.5 = (bf16[416,128]{1,0:T(8,128)(2,1)S(1)}, bf16[416,128]{1,0:T(8,128)(2,1)S(1)}, u32[]{:S(2)}, u32[]{:S(2)}) collective-permute-start(bf16[416,128]{1,0:T(8,128)(2,1)S(1)} %get-tuple-element.22), channel_id=1, source_target_pairs={{0,2},{1,3},{2,0},{3,1},{4,6},{5,7},{6,4},{7,5},{8,10},{9,11},{10,... | collective-permute-start | bytes 319496 | tf_op jit(solution)/shard_map/ppermute | solution.py:546
  36.2 4.4 %collective-permute-start.6 = (bf16[128,128]{1,0:T(8,128)(2,1)S(1)}, bf16[128,128]{1,0:T(8,128)(2,1)S(1)}, u32[]{:S(2)}, u32[]{:S(2)}) collective-permute-start(bf16[128,128]{1,0:T(8,128)(2,1)S(1)} %get-tuple-element.26), channel_id=1, source_target_pairs={{0,4},{1,5},{2,6},{3,7},{4,0},{5,1},{6,2},{7,3},{8,12},{9,13},{10,... | collective-permute-start | bytes 98312 | tf_op jit(solution)/shard_map/ppermute | solution.py:546
  37.6 5.5 %collective-permute-start.7 = (bf16[128,128]{1,0:T(8,128)(2,1)S(1)}, bf16[128,128]{1,0:T(8,128)(2,1)S(1)}, u32[]{:S(2)}, u32[]{:S(2)}) collective-permute-start(bf16[128,128]{1,0:T(8,128)(2,1)S(1)} %get-tuple-element.27), channel_id=1, source_target_pairs={{0,8},{1,9},{2,10},{3,11},{4,12},{5,13},{6,14},{7,15},{8,0},{9,1},... | collective-permute-start | bytes 98312 | tf_op jit(solution)/shard_map/ppermute | solution.py:546
  40.6 5.7 %collective-permute-start.8 = (bf16[128,128]{1,0:T(8,128)(2,1)S(1)}, bf16[128,128]{1,0:T(8,128)(2,1)S(1)}, u32[]{:S(2)}, u32[]{:S(2)}) collective-permute-start(bf16[128,128]{1,0:T(8,128)(2,1)S(1)} %get-tuple-element.28), channel_id=1, source_target_pairs={{0,12},{1,13},{2,14},{3,15},{4,8},{5,9},{6,10},{7,11},{8,4},{9,5},... | collective-permute-start | bytes 98312 | tf_op jit(solution)/shard_map/ppermute | solution.py:546
  47.6 0.6 %copy-start.3 = (f32[8,128]{1,0:T(8,128)}, f32[8,128]{1,0:T(8,128)S(1)}, u32[]{:S(2)}) copy-start(f32[8,128]{1,0:T(8,128)S(1)} %get-tuple-element.31.own) | copy-start | bytes 12292
  48.2 1.2 %collective-permute-start.9 = (f32[8,128]{1,0:T(8,128)S(1)}, f32[8,128]{1,0:T(8,128)S(1)}, u32[]{:S(2)}, u32[]{:S(2)}) collective-permute-start(f32[8,128]{1,0:T(8,128)S(1)} %get-tuple-element.32), channel_id=1, source_target_pairs={{0,1},{1,0},{2,3},{3,2},{4,5},{5,4},{6,7},{7,6},{8,9},{9,8},{10,11... | collective-permute-start | bytes 12296 | tf_op jit(solution)/shard_map/ppermute | solution.py:546
  49.3 0.6 %copy-start.10 = (f32[8,128]{1,0:T(8,128)}, f32[8,128]{1,0:T(8,128)S(1)}, u32[]{:S(2)}) copy-start(f32[8,128]{1,0:T(8,128)S(1)} %collective-permute-done.9.got) | copy-start | bytes 12292

commit v4 on v3

--- a/solution.py
+++ b/solution.py
@@ -32,14 +32,11 @@
     return pltpu.CompilerParams(vmem_limit_bytes=megabytes * 2**20)
 
 
-def cost(flops, size):
-    return pl.CostEstimate(flops=flops, bytes_accessed=size, transcendentals=0)
-
-
 class Plan:
     def __init__(self, area_count, trials, steps, delays, neurons, pops, channels):
         self.area_count, self.trials, self.steps, self.delays = area_count, trials, steps, delays
         self.lanes = area_count // 2
+        self.top = self.lanes.bit_length() - 2
         self.blocks, self.pops = neurons // 128, pops
         self.pop_size = neurons / pops
         self.arriving = trials * (steps + delays)
@@ -61,6 +58,9 @@
         self.held = self.main_up + 16
         self.last = up(self.main + self.packed, 16)
 
+    def mask(self, lane):
+        return (2 * lane) ^ (lane >> self.top)
+
     def keep(self, slots):
         rows = slots * self.held + self.tiles * self.signal
         return jax.ShapeDtypeStruct((rows, 128), F32)
@@ -79,8 +79,35 @@
         return jax.ShapeDtypeStruct((self.lanes * 2 * self.taps, 128), BF16)
 
 
+def facts_kernel(plan, spikes, leak, population, destination, target_block, delay_slot, out, codes):
+    trials, steps = plan.trials, plan.steps
+    last = jnp.full(spikes.shape[1:], -1, jnp.int32)
+    for step in range(steps):
+        last = jnp.where(spikes[step] > 0, step, last)
+    high, low = both(leak[...].reshape(1, -1))
+    blank = jnp.zeros((5 - trials, last.shape[1]), F32)
+    rows = jnp.concatenate(
+        [last.astype(F32), high, low, population[...].reshape(1, -1).astype(F32), blank], axis=0
+    )
+    rows = [rows[:, block * 128 : block * 128 + 128] for block in range(plan.blocks)]
+    out[...] = jnp.concatenate(rows, axis=0).astype(BF16)
+    for row, values in enumerate((destination, target_block, delay_slot)):
+        codes[row : row + 1] = values[...].reshape(1, -1)
+
+
+def facts_of(plan, spikes, leak, population, destination, target_block, delay_slot):
+    codes = jax.ShapeDtypeStruct((3, destination.shape[0]), jnp.int32)
+    return pl.pallas_call(
+        functools.partial(facts_kernel, plan),
+        out_shape=(jax.ShapeDtypeStruct((plan.blocks * 8, 128), BF16), codes),
+        in_specs=[VMEM] * 6,
+        out_specs=(VMEM, VMEM),
+        name="facts",
+    )(spikes, leak, population, destination, target_block, delay_slot)
+
+
 def payload_kernel(
-    destination, target_block, delay_slot, spikes, weights, keep, send, token,
+    plan, listed, spikes, weights, keep, send, token,
     codes, given, held, plain, lagged, total, sems, part_sems,
 ):
     steps, trials, neurons = spikes.shape
@@ -91,10 +118,8 @@
     chunk = held.shape[0] // part_sems.shape[0]
     chunks = unit_count // chunk
     small = [
-        pltpu.make_async_copy(destination, codes.at[0], sems.at[0]),
-        pltpu.make_async_copy(target_block, codes.at[1], sems.at[1]),
-        pltpu.make_async_copy(delay_slot, codes.at[2], sems.at[2]),
-        pltpu.make_async_copy(spikes, given, sems.at[3]),
+        pltpu.make_async_copy(listed, codes, sems.at[0]),
+        pltpu.make_async_copy(spikes, given, sems.at[1]),
     ]
     for copy in small:
         copy.start()
@@ -130,7 +155,8 @@
         for unit, value in zip(units, values):
             device = lax.bitwise_xor(codes[0, unit], me)
             lane = lax.shift_right_logical(device, 1)
-            place = lax.bitwise_and(device, 1) * half + lane * blocks + codes[1, unit]
+            bit = lax.bitwise_and(lax.bitwise_xor(device, lane >> plan.top), 1)
+            place = bit * half + lane * blocks + codes[1, unit]
             total[place] += value
         return 0
 
@@ -139,17 +165,17 @@
     send[...] = total[half:]
 
 
-def payload_sums(plan, spikes, weights, destination, target_block, delay_slot):
+def payload_sums(plan, spikes, weights, codes):
     steps, trials, neurons = spikes.shape
     unit_count = weights.shape[0]
     rows, delays = plan.arriving, plan.delays
     chunk = next(size for size in (16, 12, 8, 6, 4, 3, 2, 1) if unit_count % size == 0)
     half = jax.ShapeDtypeStruct((plan.lanes * plan.blocks, rows, 128), F32)
     return pl.pallas_call(
-        payload_kernel,
-        out_shape=(half, half, jax.ShapeDtypeStruct((8, 128), F32)),
-        in_specs=[HBM, HBM, HBM, HBM, HBM],
-        out_specs=(VMEM, VMEM, VMEM),
+        functools.partial(payload_kernel, plan),
+        out_shape=(half, half, jax.ShapeDtypeStruct((16, 128), BF16)),
+        in_specs=[HBM] * 3,
+        out_specs=(VMEM,) * 3,
         scratch_shapes=[
             pltpu.SMEM((3, unit_count), jnp.int32),
             pltpu.VMEM(spikes.shape, jnp.int32),
@@ -157,16 +183,15 @@
             pltpu.VMEM((trials * delays + rows, neurons), F32),
             pltpu.VMEM((delays, up(rows, 16), neurons), BF16),
             pltpu.VMEM((2 * plan.lanes * plan.blocks, rows, 128), F32),
-            pltpu.SemaphoreType.DMA((4,)),
+            pltpu.SemaphoreType.DMA((2,)),
             pltpu.SemaphoreType.DMA((unit_count // chunk,)),
         ],
-        compiler_params=params(52),
-        cost_estimate=cost(2 * unit_count * 256 * neurons * 128, 2 * unit_count * neurons * 128),
+        compiler_params=params(62),
         name="payload",
-    )(destination, target_block, delay_slot, spikes, weights)
-
-
-def known_kernel(spikes, population, history, kernel, out, series, fresh, lags):
+    )(codes, spikes, weights)
+
+
+def known_kernel(plan, spikes, population, history, kernel, out, reach, series, fresh, lags):
     steps, trials, neurons = spikes.shape
     pops, kinds, _, taps = history.shape
     group = kinds * trials
@@ -182,7 +207,7 @@
     back = dot(series[...].astype(BF16), flip)
 
     which = lax.broadcasted_iota(jnp.int32, (8, neurons), 0)
-    member = (which == population[...]).astype(F32).astype(BF16)
+    member = (which == population[...].reshape(1, -1)).astype(F32).astype(BF16)
     rows = spikes[...].reshape(steps * trials, neurons).astype(F32).astype(BF16)
     rates = (dot(member, rows, NT) / (neurons / pops)).astype(BF16)
     fresh[...] = jnp.zeros_like(fresh)
@@ -209,22 +234,42 @@
         total += dot(kernel[:, part * taps : (part + 1) * taps], lags[part].astype(BF16), NT)
     out[...] = total
 
-
-def known_lfp(spikes, population, history, kernel):
+    channels, share, wide = kernel.shape[0], plan.share, plan.taps_lanes
+    row = lax.broadcasted_iota(jnp.int32, (128, wide), 0)
+    column = lax.broadcasted_iota(jnp.int32, (128, wide), 1)
+    spread = (row == column // share).astype(F32).astype(BF16)
+    row = lax.broadcasted_iota(jnp.int32, (channels, wide), 0)
+    column = lax.broadcasted_iota(jnp.int32, (channels, wide), 1)
+    same = (row % share == column % share) & (column < (steps - 1) * share)
+    row = lax.broadcasted_iota(jnp.int32, (plan.area_count, channels), 0)
+    column = lax.broadcasted_iota(jnp.int32, (plan.area_count, channels), 1)
+    gather = (row == column // share).astype(F32).astype(BF16)
+    reach[...] = jnp.zeros_like(reach)
+    for pop in range(pops):
+        start = (pop * kinds + 1) * taps
+        wider = jnp.where(same, dot(kernel[:, start : start + 128], spread), 0.0)
+        packed = dot(gather, wider.astype(BF16))
+        for tile in range(wide // 128):
+            reach[:, tile * pops + pop, :] = packed[:, tile * 128 : tile * 128 + 128]
+
+
+def known_lfp(plan, spikes, population, history, kernel):
     pops, kinds, trials, taps = history.shape
     channels = kernel.shape[0]
     return pl.pallas_call(
-        known_kernel,
-        out_shape=jax.ShapeDtypeStruct((channels, 128), F32),
+        functools.partial(known_kernel, plan),
+        out_shape=(
+            jax.ShapeDtypeStruct((channels, 128), F32),
+            jax.ShapeDtypeStruct((plan.area_count, plan.taps, 128), F32),
+        ),
         in_specs=[VMEM] * 4,
-        out_specs=VMEM,
+        out_specs=(VMEM, VMEM),
         scratch_shapes=[
             pltpu.VMEM((pops * kinds * trials, taps), F32),
             pltpu.VMEM((pops * kinds * trials, taps), F32),
             pltpu.VMEM((pops * kinds, 128, taps), F32),
         ],
         compiler_params=params(16),
-        cost_estimate=cost(2 * channels * 128 * pops * kinds * taps * 4, 2 * kernel.size),
         name="known_lfp",
     )(spikes, population, history, kernel)
 
@@ -265,7 +310,7 @@
         for bit in range(2):
             lane = 2 * index + bit
             own = (lane == 0).astype(F32)
-            place = lax.bitwise_xor(2 * lane, me)
+            place = lax.bitwise_xor(plan.mask(lane), me)
             first = (lax.shift_right_logical(place, 1) * plan.pops).astype(F32)
             tops, members = [], []
             for block in range(blocks):
@@ -523,25 +568,6 @@
     )(held, carried, *gots)
 
 
-def lfp_kernel_body(plan, own, got, out):
-    value = own[...] + got[...]
-    pieces = [value]
-    for group in range(1, plan.groups):
-        pieces.append(pltpu.roll(value, 128 - group * plan.width, 1))
-    value = jnp.concatenate(pieces, axis=0) if plan.groups > 1 else value
-    out[...] = value[0 : plan.share, 0 : plan.width]
-
-
-def lfp_sum(plan, own, got):
-    return pl.pallas_call(
-        functools.partial(lfp_kernel_body, plan),
-        out_shape=jax.ShapeDtypeStruct((plan.share, plan.width), F32),
-        in_specs=[VMEM] * 2,
-        out_specs=VMEM,
-        name="lfp_sum",
-    )(own, got)
-
-
 def swap(values, bit, area_count):
     return lax.ppermute(values, "area", [(i, i ^ bit) for i in range(area_count)])
 
@@ -565,52 +591,38 @@
     trials, steps = spikes.shape[:2]
     delays = cycle_start.shape[1]
     channels = lfp_kernel.shape[0]
-    pops, kinds, _, taps = history.shape
+    pops = history.shape[0]
     plan = Plan(area_count, trials, steps, delays, neurons, pops, channels)
     share = plan.share
     spikes = jnp.transpose(spikes, (1, 0, 2))
-    top = area_count // 4
-    far = [top, 2 * top, 3 * top]
-
-    order = lax.broadcasted_iota(jnp.int32, spikes.shape, 0)
-    last = jnp.max(jnp.where(spikes > 0, order, -1), axis=0)
-    leak = lax.reduce_precision(leak_rate, 8, 7)
-    facts = jnp.concatenate(
-        [
-            last.astype(F32),
-            leak[None],
-            (leak_rate - leak)[None],
-            population.astype(F32)[None],
-            jnp.zeros((5 - trials, neurons), F32),
-        ]
-    ).astype(BF16)
-    facts = jnp.transpose(facts.reshape(8, blocks, 128), (1, 0, 2)).reshape(blocks * 8, 128)
-    facts = jnp.stack([facts] + [swap(facts, bit, area_count) for bit in far])
-
-    mine, goes, token = payload_sums(
-        plan, spikes, weights, destination[:, 0], target_block, delay_slot
+    quarter = plan.lanes // 4
+    far = [plan.mask(index * quarter) for index in (1, 2, 3)]
+
+    facts, codes = facts_of(
+        plan, spikes, leak_rate, population, destination[:, 0], target_block, delay_slot
     )
-    facts = facts + token[0, 0].astype(BF16)
+    facts = [facts] + [swap(facts, mask, area_count) for mask in far]
+    mine, goes, token = payload_sums(plan, spikes, weights, codes)
     got = swap(goes, 1, area_count)
-    bit = top // 2
-    while bit > 1:
-        more = swap(facts.reshape(-1, 128), bit, area_count).reshape(facts.shape)
-        facts = jnp.stack([facts, more], axis=1).reshape(-1, blocks * 8, 128)
-        bit //= 2
-    facts = facts.astype(F32)
-
-    flat = lax.optimization_barrier(lfp_kernel.reshape(channels, -1))
-    known = known_lfp(spikes, population[None], history, flat)
+    size = blocks * 8
+    facts = jnp.concatenate(facts)
+    lane = quarter // 2
+    while lane:
+        count = facts.shape[0]
+        message = facts
+        if lane == quarter // 2:
+            blank = jnp.zeros((max(0, 512 - count - token.shape[0]), 128), BF16)
+            message = jnp.concatenate([facts, token, blank])
+        more = swap(message, plan.mask(lane), area_count)[:count]
+        facts = jnp.stack([facts.reshape(-1, size, 128), more.reshape(-1, size, 128)], axis=1)
+        facts = facts.reshape(-1, 128)
+        lane //= 2
+    facts = facts.astype(F32).reshape(-1, size, 128)
+
+    flat = lfp_kernel.reshape(channels, -1)
+    known, first = known_lfp(plan, spikes, population, history, flat)
     known = known.reshape(area_count, share, 128)
     known = jnp.pad(known, ((0, 0), (0, plan.groups * 8 - share), (0, 0)))
-    reach = steps - 1
-    first = [flat[:, (pop * kinds + 1) * taps :][:, :reach] for pop in range(pops)]
-    first = jnp.stack(first, axis=1).astype(F32).reshape(area_count, share, pops, reach)
-    first = jnp.transpose(first, (0, 2, 3, 1)).reshape(area_count, pops, reach * share)
-    first = jnp.pad(first, ((0, 0), (0, 0), (0, plan.taps_lanes - reach * share)))
-    first = first.reshape(area_count, pops, plan.taps_lanes // 128, 128)
-    first = jnp.transpose(first, (0, 2, 1, 3)).reshape(area_count, -1, 128)
-    first = jnp.pad(first, ((0, 0), (0, plan.taps - first.shape[1]), (0, 0)))
 
     cycle = jnp.transpose(cycle_start, (1, 0, 2)).reshape(delays * trials, blocks, 128)
     cycle = jnp.transpose(cycle, (1, 0, 2))
@@ -618,15 +630,18 @@
     keep, send, carried = compress(plan, mine, got, facts, cycle, start, known, first)
 
     slots, stage = plan.lanes // 2, 0
-    got = swap(send, 2, area_count)
+    got = swap(send, plan.mask(1), area_count)
     while slots > 4:
         keep, send, carried = fold(plan, slots, stage, False, keep, got, carried)
         slots, stage = slots // 2, stage + 1
-        got = swap(send, 2 << stage, area_count)
+        got = swap(send, plan.mask(1 << stage), area_count)
     keep, *sends, carried = fold(plan, slots, stage, True, keep, got, carried)
-    gots = [swap(send, bit, area_count) for send, bit in zip(sends, far)]
+    gots = [swap(send, mask, area_count) for send, mask in zip(sends, far)]
     membrane, cycle_out, own, other = finish(plan, neurons, keep, carried, gots)
-    lfp = lfp_sum(plan, own, swap(other, 1, area_count))
+    lfp = own + swap(other, 1, area_count)
+    width = plan.width
+    lfp = [lfp[:, group * width : (group + 1) * width] for group in range(plan.groups)]
+    lfp = jnp.concatenate(lfp, axis=0)[:share]
     return membrane, cycle_out, lfp
 
 

time: 51.8 us -> 40.4 us (0.78)
  local copies, waits for them, and re-layouts: 10.4 us -> 3.76 us
  other arithmetic: 6 us -> 0.64 us
  Pallas kernels: 9.66 us -> 12.3 us
  waiting for transfers between devices: 10.7 us -> 8.58 us
    unnamed x22 -> x19, local copies, waits for them, and re-layouts: 4 us -> 0.76 us
    add x2 -> x1, other arithmetic: 2.73 us -> 0.01 us  [body(): lfp = own + swap(other, 1, area_count)]
    pallas_call x3, Pallas kernels: 7.62 us -> 10.2 us  [the longest x1 7.09 us: payload_sums(): pl.pallas_call(functools.partial(payload_kernel, plan), out_shape=(half,...]
    another operation x4 -> x0, local copies, waits for them, and re-layouts: 2.59 us -> none  [body(): jnp.stack(first, axis=1).astype(F32).reshape(area_count, share, pops, reach)]
    ppermute x10, waiting for transfers between devices: 10.7 us -> 8.58 us  [swap(): lax.ppermute(values, 'area', [(i, i ^ bit) for i in range(area_count)])]
    transpose x1 -> x0, other arithmetic: 0.99 us -> none  [body(): jnp.transpose(first, (0, 2, 3, 1)).reshape(area_count, pops, reach * share)]
    reduce_max x1 -> x0, other arithmetic: 0.86 us -> none  [body(): last = jnp.max(jnp.where(spikes > 0, order, -1), axis=0)]
    concatenate x2, other arithmetic: 1.37 us -> 0.61 us  [the longest x1 0.61 us: body(): lfp = jnp.concatenate(lfp, axis=0)[:share]]
  transfers between devices with their start and end apart: 10 -> 10, of which waited for: 5 -> 4; matrix products, arithmetic and copies ran while one was open for 20% -> 9% of each run, Pallas kernels for 12% -> 22%
where the time goes in v4:
time: 40.4 us; the launch traced here: 40.1 us
  starting transfers between devices  14.1 us (35%)
  Pallas kernels  12.3 us (30%)
  waiting for transfers between devices  8.58 us (21%)
  local copies, waits for them, and re-layouts  3.76 us (9%)
  between operations  0.85 us (2%)
  other arithmetic  0.64 us (2%)
    ppermute x10, starting transfers between devices, swap(): lax.ppermute(values, 'area', [(i, i ^ bit) for i in range(area_count)])  14.1 us
    ppermute x10, waiting for transfers between devices, swap(): lax.ppermute(values, 'area', [(i, i ^ bit) for i in range(area_count)])  8.58 us
    pallas_call x1, Pallas kernels, payload_sums(): pl.pallas_call(functools.partial(payload_kernel, plan), out_shape=(half,...  7.09 us
    reshape x1, local copies, waits for them, and re-layouts, body(): flat = lfp_kernel.reshape(channels, -1)  2.86 us
    pallas_call x1, Pallas kernels, known_lfp(): pl.pallas_call(functools.partial(known_kernel, plan), out_shape=(jax.Shap...  1.64 us
    pallas_call x1, Pallas kernels, facts_of(): pl.pallas_call(functools.partial(facts_kernel, plan), out_shape=(jax.Shap...  1.48 us
    pallas_call x1, Pallas kernels, finish(): pl.pallas_call(functools.partial(finish_kernel, plan), out_shape=(jax.Sha...  1.31 us
  transfers between devices with their start and end apart: 10, of which 4 were waited for; matrix products, arithmetic and copies ran while one was open for 9% of the time, Pallas kernels for 22%

profile of v4, /device:TPU:0, one launch (start us, length us, event | category | flops | bytes accessed | tf_op | source)
XLA Modules:
  0.0 40.1 jit_solution(2950852394691164829)
XLA Ops:
  0.6 1.5 %facts.1 = (bf16[24,128]{1,0:T(8,128)(2,1)}, s32[3,96]{1,0:T(4,128)}) custom-call(s32[10,4,384]{2,1,0:T(4,128)} %bitcast.17, f32[384]{0:T(512)} %leak.1, s32[384]{0:T(512)} %population.3, s32[96]{0:T(128)} %bitcast.26, s32[96]{0:T(128)} %target_block.1, s32[96]{0:T(128)} %delay_slot.1), custom_call_target="tpu_custom_call" | custom-call | tf_op jit(solution)/shard_map/facts/pallas_call | solution.py:100
  2.1 3.0 %collective-permute-start.1 = (bf16[24,128]{1,0:T(8,128)(2,1)}, bf16[24,128]{1,0:T(8,128)(2,1)S(1)}, u32[]{:S(2)}, u32[]{:S(2)}) collective-permute-start(bf16[24,128]{1,0:T(8,128)(2,1)} %get-tuple-element.25), channel_id=1, source_target_pairs={{0,4},{1,5},{2,6},{3,7},{4,0},{5,1},{6,2},{7,3},{8,12},{9,13},{10,... | collective-permute-start | bytes 18440 | tf_op jit(solution)/shard_map/ppermute | solution.py:572
  5.1 1.7 %collective-permute-start.2 = (bf16[24,128]{1,0:T(8,128)(2,1)}, bf16[24,128]{1,0:T(8,128)(2,1)S(1)}, u32[]{:S(2)}, u32[]{:S(2)}) collective-permute-start(bf16[24,128]{1,0:T(8,128)(2,1)} %get-tuple-element.25), channel_id=1, source_target_pairs={{0,9},{1,8},{2,11},{3,10},{4,13},{5,12},{6,15},{7,14},{8,1},{9,0},... | collective-permute-start | bytes 18440 | tf_op jit(solution)/shard_map/ppermute | solution.py:572
  6.9 0.3 collective-permute-start.3
  7.2 0.0 copy-start.6
  7.2 7.1 %payload.1 = (f32[24,56,128]{2,1,0:T(8,128)}, f32[24,56,128]{2,1,0:T(8,128)}, bf16[16,128]{1,0:T(8,128)(2,1)}) custom-call(s32[3,96]{1,0:T(4,128)} %get-tuple-element.22.listed, s32[10,4,384]{2,1,0:T(4,128)} %bitcast.18, bf16[96,384,128]{2,1,0:T(8,128)(2,1)} %weights.1), custom_call_target="tpu_custom_call" | custom-call | tf_op jit(solution)/shard_map/payload/pallas_call | solution.py:174
  14.3 0.7 %collective-permute-start = (f32[24,56,128]{2,1,0:T(8,128)}, f32[24,56,128]{2,1,0:T(8,128)S(1)}, u32[]{:S(2)}, u32[]{:S(2)}) collective-permute-start(f32[24,56,128]{2,1,0:T(8,128)} %get-tuple-element.24), channel_id=1, source_target_pairs={{0,1},{1,0},{2,3},{3,2},{4,5},{5,4},{6,7},{7,6},{8,9},{9,8},{10,11... | collective-permute-start | bytes 2064392 | tf_op jit(solution)/shard_map/ppermute | solution.py:572
  15.0 0.0 copy-done.6
  15.0 0.0 collective-permute-done.1
  15.0 0.0 collective-permute-done.2
  15.0 0.0 collective-permute-done.3
  15.1 0.7 %constant_dynamic-update-slice_fusion = bf16[512,128]{1,0:T(8,128)(2,1)S(1)} fusion(bf16[512,128]{1,0:T(8,128)(2,1)S(1)} %constant_dynamic-update-slice_fusion.1, bf16[16,128]{1,0:T(8,128)(2,1)} %get-tuple-element.26), kind=kLoop, calls=%fused_computation.5 | loop fusion | bytes 8192
  15.8 0.0 copy-start.5
  15.8 0.0 copy-start.1
  15.8 0.0 copy-start.2
  15.8 0.0 copy-start.3
  15.8 1.6 %collective-permute-start.4 = (bf16[512,128]{1,0:T(8,128)(2,1)S(1)}, bf16[512,128]{1,0:T(8,128)(2,1)S(1)}, u32[]{:S(2)}, u32[]{:S(2)}) collective-permute-start(bf16[512,128]{1,0:T(8,128)(2,1)S(1)} %broadcast_dynamic-update-slice_fusion), channel_id=1, source_target_pairs={{0,2},{1,3},{2,0},{3,1},{4,6},{5,7},{6,4},{7,5},{8,10},{9,11},{10,... | collective-permute-start | bytes 393224 | tf_op jit(solution)/shard_map/ppermute | solution.py:572
  17.4 2.9 %reshape.25.kernel = bf16[384,2048]{1,0:T(8,128)(2,1)S(1)} reshape(bf16[384,4,2,256]{3,2,1,0:T(2,128)(2,1)} %param.21) | data formatting | bytes 3145728 | tf_op jit(solution)/shard_map/reshape | solution.py:622
  20.3 0.0 copy-start
  20.3 0.0 copy-start.4
  20.3 0.0 copy-done.5
  20.4 0.0 copy-done.1
  20.4 0.0 copy-done.2
  20.4 0.0 copy-done.3
  20.4 1.6 %known_lfp.1 = (f32[384,128]{1,0:T(8,128)S(1)}, f32[16,8,128]{2,1,0:T(8,128)S(1)}) custom-call(s32[10,4,384]{2,1,0:T(4,128)S(1)} %bitcast.19, s32[384]{0:T(512)S(1)} %copy-done.3, f32[4,2,4,256]{3,2,1,0:T(4,128)S(1)} %copy-done.2, bf16[384,2048]{1,0:T(8,128)(2,1)S(1)} %reshape.25.kernel), custom_call_target="tpu_custom_call" | custom-call | tf_op jit(solution)/shard_map/known_lfp/pallas_call | solution.py:259
  22.0 0.0 collective-permute-done.4
  22.1 0.0 collective-permute-done.got
  22.1 0.0 copy-done
  22.1 0.0 copy-done.4
  22.1 0.5 %compress.1 = (f32[360,128]{1,0:T(8,128)S(1)}, bf16[416,128]{1,0:T(8,128)(2,1)S(1)}, bf16[128,128]{1,0:T(8,128)(2,1)S(1)}) custom-call(f32[24,56,128]{2,1,0:T(8,128)S(1)} %copy-done, f32[24,56,128]{2,1,0:T(8,128)S(1)} %collective-permute-done.got, f32[8,24,128]{2,1,0:T(8,128)S(1)} %bitcast_convert_fusion.given, f32[3,16,128]{2,1,0:T(8,128)S(1)} %bitcast.21, ...), custom_call_target="tpu_custom_call" | custom-call | tf_op jit(solution)/shard_map/compress/pallas_call | solution.py:386
  22.7 1.1 %collective-permute-start.5 = (bf16[416,128]{1,0:T(8,128)(2,1)S(1)}, bf16[416,128]{1,0:T(8,128)(2,1)S(1)}, u32[]{:S(2)}, u32[]{:S(2)}) collective-permute-start(bf16[416,128]{1,0:T(8,128)(2,1)S(1)} %get-tuple-element.30), channel_id=1, source_target_pairs={{0,2},{1,3},{2,0},{3,1},{4,6},{5,7},{6,4},{7,5},{8,10},{9,11},{10,... | collective-permute-start | bytes 319496 | tf_op jit(solution)/shard_map/ppermute | solution.py:572
  23.8 3.9 %collective-permute-done.5.got = bf16[416,128]{1,0:T(8,128)(2,1)S(1)} collective-permute-done((bf16[416,128]{1,0:T(8,128)(2,1)S(1)}, bf16[416,128]{1,0:T(8,128)(2,1)S(1)}, u32[]{:S(2)}, u32[]{:S(2)}) %collective-permute-start.5) | collective-permute-done | bytes 106528 | tf_op jit(solution)/shard_map/ppermute | solution.py:572
  27.7 0.2 fold.1
  27.8 0.7 %collective-permute-start.6 = (bf16[128,128]{1,0:T(8,128)(2,1)S(1)}, bf16[128,128]{1,0:T(8,128)(2,1)S(1)}, u32[]{:S(2)}, u32[]{:S(2)}) collective-permute-start(bf16[128,128]{1,0:T(8,128)(2,1)S(1)} %get-tuple-element.34), channel_id=1, source_target_pairs={{0,4},{1,5},{2,6},{3,7},{4,0},{5,1},{6,2},{7,3},{8,12},{9,13},{10,... | collective-permute-start | bytes 98312 | tf_op jit(solution)/shard_map/ppermute | solution.py:572
  28.6 2.2 %collective-permute-start.7 = (bf16[128,128]{1,0:T(8,128)(2,1)S(1)}, bf16[128,128]{1,0:T(8,128)(2,1)S(1)}, u32[]{:S(2)}, u32[]{:S(2)}) collective-permute-start(bf16[128,128]{1,0:T(8,128)(2,1)S(1)} %get-tuple-element.35), channel_id=1, source_target_pairs={{0,9},{1,8},{2,11},{3,10},{4,13},{5,12},{6,15},{7,14},{8,1},{9,0},... | collective-permute-start | bytes 98312 | tf_op jit(solution)/shard_map/ppermute | solution.py:572
  30.7 1.3 %collective-permute-start.8 = (bf16[128,128]{1,0:T(8,128)(2,1)S(1)}, bf16[128,128]{1,0:T(8,128)(2,1)S(1)}, u32[]{:S(2)}, u32[]{:S(2)}) collective-permute-start(bf16[128,128]{1,0:T(8,128)(2,1)S(1)} %get-tuple-element.36), channel_id=1, source_target_pairs={{0,13},{1,12},{2,15},{3,14},{4,9},{5,8},{6,11},{7,10},{8,5},{9,4},... | collective-permute-start | bytes 98312 | tf_op jit(solution)/shard_map/ppermute | solution.py:572
  32.0 0.0 collective-permute-done.6.refs_0_
  32.0 0.8 %collective-permute-done.7.refs_1_ = bf16[128,128]{1,0:T(8,128)(2,1)S(1)} collective-permute-done((bf16[128,128]{1,0:T(8,128)(2,1)S(1)}, bf16[128,128]{1,0:T(8,128)(2,1)S(1)}, u32[]{:S(2)}, u32[]{:S(2)}) %collective-permute-start.7) | collective-permute-done | bytes 32800 | tf_op jit(solution)/shard_map/ppermute | solution.py:572
  32.8 3.1 %collective-permute-done.8.refs_2_ = bf16[128,128]{1,0:T(8,128)(2,1)S(1)} collective-permute-done((bf16[128,128]{1,0:T(8,128)(2,1)S(1)}, bf16[128,128]{1,0:T(8,128)(2,1)S(1)}, u32[]{:S(2)}, u32[]{:S(2)}) %collective-permute-start.8) | collective-permute-done | bytes 32800 | tf_op jit(solution)/shard_map/ppermute | solution.py:572
  35.9 1.3 %finish.1 = (f32[4,384]{1,0:T(4,128)}, f32[4,4,384]{2,1,0:T(4,128)}, f32[8,128]{1,0:T(8,128)S(1)}, f32[8,128]{1,0:T(8,128)S(1)}) custom-call(f32[120,128]{1,0:T(8,128)S(1)} %get-tuple-element.32.held, bf16[128,128]{1,0:T(8,128)(2,1)S(1)} %get-tuple-element.33.carried, bf16[128,128]{1,0:T(8,128)(2,1)S(1)} %collective-permute-done.6.refs_0_, ...), custom_call_target="tpu_custom_call" | custom-call | tf_op jit(solution)/shard_map/finish/pallas_call | solution.py:550
  37.2 1.4 %collective-permute-start.9 = (f32[8,128]{1,0:T(8,128)S(1)}, f32[8,128]{1,0:T(8,128)S(1)}, u32[]{:S(2)}, u32[]{:S(2)}) collective-permute-start(f32[8,128]{1,0:T(8,128)S(1)} %get-tuple-element.40), channel_id=1, source_target_pairs={{0,1},{1,0},{2,3},{3,2},{4,5},{5,4},{6,7},{7,6},{8,9},{9,8},{10,11... | collective-permute-start | bytes 12296 | tf_op jit(solution)/shard_map/ppermute | solution.py:572
  38.6 0.8 %collective-permute-done.9 = f32[8,128]{1,0:T(8,128)S(1)} collective-permute-done((f32[8,128]{1,0:T(8,128)S(1)}, f32[8,128]{1,0:T(8,128)S(1)}, u32[]{:S(2)}, u32[]{:S(2)}) %collective-permute-start.9) | collective-permute-done | bytes 4128 | tf_op jit(solution)/shard_map/ppermute | solution.py:572
  39.5 0.1 fusion
  39.5 0.6 %pad_maximum_fusion.2 = f32[24,40]{1,0:T(8,128)} fusion(f32[8,40]{1,0:T(8,128)S(1)} %get-tuple-element.42, f32[8,40]{1,0:T(8,128)S(1)} %get-tuple-element.43, f32[8,40]{1,0:T(8,128)S(1)} %get-tuple-element.41), kind=kLoop, calls=%fused_computation.10 | loop fusion | flops 1920 | bytes 7680 | tf_op jit(solution)/shard_map/concatenate | solution.py:644
  (13 shorter events, 0.1 us)
Async XLA Ops:
  2.1 12.9 %collective-permute-start.1 = (bf16[24,128]{1,0:T(8,128)(2,1)}, bf16[24,128]{1,0:T(8,128)(2,1)S(1)}, u32[]{:S(2)}, u32[]{:S(2)}) collective-permute-start(bf16[24,128]{1,0:T(8,128)(2,1)} %get-tuple-element.25), channel_id=1, source_target_pairs={{0,4},{1,5},{2,6},{3,7},{4,0},{5,1},{6,2},{7,3},{8,12},{9,13},{10,... | collective-permute-start | bytes 18440 | tf_op jit(solution)/shard_map/ppermute | solution.py:572
  5.1 9.9 %collective-permute-start.2 = (bf16[24,128]{1,0:T(8,128)(2,1)}, bf16[24,128]{1,0:T(8,128)(2,1)S(1)}, u32[]{:S(2)}, u32[]{:S(2)}) collective-permute-start(bf16[24,128]{1,0:T(8,128)(2,1)} %get-tuple-element.25), channel_id=1, source_target_pairs={{0,9},{1,8},{2,11},{3,10},{4,13},{5,12},{6,15},{7,14},{8,1},{9,0},... | collective-permute-start | bytes 18440 | tf_op jit(solution)/shard_map/ppermute | solution.py:572
  6.9 8.2 %collective-permute-start.3 = (bf16[24,128]{1,0:T(8,128)(2,1)}, bf16[24,128]{1,0:T(8,128)(2,1)S(1)}, u32[]{:S(2)}, u32[]{:S(2)}) collective-permute-start(bf16[24,128]{1,0:T(8,128)(2,1)} %get-tuple-element.25), channel_id=1, source_target_pairs={{0,13},{1,12},{2,15},{3,14},{4,9},{5,8},{6,11},{7,10},{8,5},{9,4},... | collective-permute-start | bytes 18440 | tf_op jit(solution)/shard_map/ppermute | solution.py:572
  7.2 7.8 %copy-start.6 = (bf16[24,128]{1,0:T(8,128)(2,1)S(1)}, bf16[24,128]{1,0:T(8,128)(2,1)}, u32[]{:S(2)}) copy-start(bf16[24,128]{1,0:T(8,128)(2,1)} %get-tuple-element.25) | copy-start | bytes 18436
  14.3 7.8 %collective-permute-start = (f32[24,56,128]{2,1,0:T(8,128)}, f32[24,56,128]{2,1,0:T(8,128)S(1)}, u32[]{:S(2)}, u32[]{:S(2)}) collective-permute-start(f32[24,56,128]{2,1,0:T(8,128)} %get-tuple-element.24), channel_id=1, source_target_pairs={{0,1},{1,0},{2,3},{3,2},{4,5},{5,4},{6,7},{7,6},{8,9},{9,8},{10,11... | collective-permute-start | bytes 2064392 | tf_op jit(solution)/shard_map/ppermute | solution.py:572
  15.8 4.5 %copy-start.5 = (f32[4,4,384]{2,1,0:T(4,128)S(1)}, f32[4,4,384]{2,1,0:T(4,128)}, u32[]{:S(2)}) copy-start(f32[4,4,384]{2,1,0:T(4,128)} %param.19) | copy-start | bytes 73732
  15.8 4.6 %copy-start.1 = (s32[4,10,384]{2,0,1:T(4,128)S(1)}, s32[4,10,384]{2,0,1:T(4,128)}, u32[]{:S(2)}) copy-start(s32[4,10,384]{2,0,1:T(4,128)} %param.11) | copy-start | bytes 184324
  15.8 4.6 %copy-start.2 = (f32[4,2,4,256]{3,2,1,0:T(4,128)S(1)}, f32[4,2,4,256]{3,2,1,0:T(4,128)}, u32[]{:S(2)}) copy-start(f32[4,2,4,256]{3,2,1,0:T(4,128)} %history.1) | copy-start | bytes 98308
  15.8 4.6 %copy-start.3 = (s32[384]{0:T(512)S(1)}, s32[384]{0:T(512)}, u32[]{:S(2)}) copy-start(s32[384]{0:T(512)} %population.3) | copy-start | bytes 4612
  15.8 6.2 %collective-permute-start.4 = (bf16[512,128]{1,0:T(8,128)(2,1)S(1)}, bf16[512,128]{1,0:T(8,128)(2,1)S(1)}, u32[]{:S(2)}, u32[]{:S(2)}) collective-permute-start(bf16[512,128]{1,0:T(8,128)(2,1)S(1)} %broadcast_dynamic-update-slice_fusion), channel_id=1, source_target_pairs={{0,2},{1,3},{2,0},{3,1},{4,6},{5,7},{6,4},{7,5},{8,10},{9,11},{10,... | collective-permute-start | bytes 393224 | tf_op jit(solution)/shard_map/ppermute | solution.py:572
  20.3 1.9 %copy-start = (f32[24,56,128]{2,1,0:T(8,128)S(1)}, f32[24,56,128]{2,1,0:T(8,128)}, u32[]{:S(2)}) copy-start(f32[24,56,128]{2,1,0:T(8,128)} %get-tuple-element.23.mine) | copy-start | bytes 2064388
  20.3 1.9 %copy-start.4 = (f32[4,384]{1,0:T(4,128)S(1)}, f32[4,384]{1,0:T(4,128)}, u32[]{:S(2)}) copy-start(f32[4,384]{1,0:T(4,128)} %param.18) | copy-start | bytes 18436
  22.7 5.0 %collective-permute-start.5 = (bf16[416,128]{1,0:T(8,128)(2,1)S(1)}, bf16[416,128]{1,0:T(8,128)(2,1)S(1)}, u32[]{:S(2)}, u32[]{:S(2)}) collective-permute-start(bf16[416,128]{1,0:T(8,128)(2,1)S(1)} %get-tuple-element.30), channel_id=1, source_target_pairs={{0,2},{1,3},{2,0},{3,1},{4,6},{5,7},{6,4},{7,5},{8,10},{9,11},{10,... | collective-permute-start | bytes 319496 | tf_op jit(solution)/shard_map/ppermute | solution.py:572
  27.8 4.2 %collective-permute-start.6 = (bf16[128,128]{1,0:T(8,128)(2,1)S(1)}, bf16[128,128]{1,0:T(8,128)(2,1)S(1)}, u32[]{:S(2)}, u32[]{:S(2)}) collective-permute-start(bf16[128,128]{1,0:T(8,128)(2,1)S(1)} %get-tuple-element.34), channel_id=1, source_target_pairs={{0,4},{1,5},{2,6},{3,7},{4,0},{5,1},{6,2},{7,3},{8,12},{9,13},{10,... | collective-permute-start | bytes 98312 | tf_op jit(solution)/shard_map/ppermute | solution.py:572
  28.6 4.2 %collective-permute-start.7 = (bf16[128,128]{1,0:T(8,128)(2,1)S(1)}, bf16[128,128]{1,0:T(8,128)(2,1)S(1)}, u32[]{:S(2)}, u32[]{:S(2)}) collective-permute-start(bf16[128,128]{1,0:T(8,128)(2,1)S(1)} %get-tuple-element.35), channel_id=1, source_target_pairs={{0,9},{1,8},{2,11},{3,10},{4,13},{5,12},{6,15},{7,14},{8,1},{9,0},... | collective-permute-start | bytes 98312 | tf_op jit(solution)/shard_map/ppermute | solution.py:572
  30.7 5.1 %collective-permute-start.8 = (bf16[128,128]{1,0:T(8,128)(2,1)S(1)}, bf16[128,128]{1,0:T(8,128)(2,1)S(1)}, u32[]{:S(2)}, u32[]{:S(2)}) collective-permute-start(bf16[128,128]{1,0:T(8,128)(2,1)S(1)} %get-tuple-element.36), channel_id=1, source_target_pairs={{0,13},{1,12},{2,15},{3,14},{4,9},{5,8},{6,11},{7,10},{8,5},{9,4},... | collective-permute-start | bytes 98312 | tf_op jit(solution)/shard_map/ppermute | solution.py:572
  37.2 2.3 %collective-permute-start.9 = (f32[8,128]{1,0:T(8,128)S(1)}, f32[8,128]{1,0:T(8,128)S(1)}, u32[]{:S(2)}, u32[]{:S(2)}) collective-permute-start(f32[8,128]{1,0:T(8,128)S(1)} %get-tuple-element.40), channel_id=1, source_target_pairs={{0,1},{1,0},{2,3},{3,2},{4,5},{5,4},{6,7},{7,6},{8,9},{9,8},{10,11... | collective-permute-start | bytes 12296 | tf_op jit(solution)/shard_map/ppermute | solution.py:572

commit v5 on v4

--- a/solution.py
+++ b/solution.py
@@ -8,6 +8,7 @@
 from jax.sharding import PartitionSpec as P
 
 BF16, F32 = jnp.bfloat16, jnp.float32
+PAD = 112
 VMEM = pl.BlockSpec(memory_space=pltpu.VMEM)
 HBM = pl.BlockSpec(memory_space=pltpu.HBM)
 NT = (((1,), (1,)), ((), ()))
@@ -79,27 +80,31 @@
         return jax.ShapeDtypeStruct((self.lanes * 2 * self.taps, 128), BF16)
 
 
-def facts_kernel(plan, spikes, leak, population, destination, target_block, delay_slot, out, codes):
+def facts_kernel(plan, spikes, leak, population, destination, target_block, delay_slot, out, given):
     trials, steps = plan.trials, plan.steps
     last = jnp.full(spikes.shape[1:], -1, jnp.int32)
     for step in range(steps):
         last = jnp.where(spikes[step] > 0, step, last)
-    high, low = both(leak[...].reshape(1, -1))
-    blank = jnp.zeros((5 - trials, last.shape[1]), F32)
-    rows = jnp.concatenate(
-        [last.astype(F32), high, low, population[...].reshape(1, -1).astype(F32), blank], axis=0
-    )
-    rows = [rows[:, block * 128 : block * 128 + 128] for block in range(plan.blocks)]
-    out[...] = jnp.concatenate(rows, axis=0).astype(BF16)
+        given[step * trials : (step + 1) * trials] = spikes[step]
+    blank = jnp.zeros((6 - trials, last.shape[1]), F32)
+    rows = [last.astype(F32), leak[...].reshape(1, -1), population[...].astype(F32).reshape(1, -1)]
+    rows = jnp.concatenate(rows + [blank], axis=0)
+    for block in range(plan.blocks):
+        out[block * 8 : block * 8 + 8] = rows[:, block * 128 : block * 128 + 128]
+    given[plan.width :] = jnp.zeros((given.shape[0] - plan.width, given.shape[1]), jnp.int32)
     for row, values in enumerate((destination, target_block, delay_slot)):
-        codes[row : row + 1] = values[...].reshape(1, -1)
+        row += up(plan.width, 8)
+        given[row : row + 1, 0 : values.shape[0]] = values[...].reshape(1, -1)
 
 
 def facts_of(plan, spikes, leak, population, destination, target_block, delay_slot):
-    codes = jax.ShapeDtypeStruct((3, destination.shape[0]), jnp.int32)
+    rows = up(plan.width, 8) + 8
     return pl.pallas_call(
         functools.partial(facts_kernel, plan),
-        out_shape=(jax.ShapeDtypeStruct((plan.blocks * 8, 128), BF16), codes),
+        out_shape=(
+            jax.ShapeDtypeStruct((plan.blocks * 8, 128), F32),
+            jax.ShapeDtypeStruct((rows, spikes.shape[2]), jnp.int32),
+        ),
         in_specs=[VMEM] * 6,
         out_specs=(VMEM, VMEM),
         name="facts",
@@ -107,22 +112,17 @@
 
 
 def payload_kernel(
-    plan, listed, spikes, weights, keep, send, token,
-    codes, given, held, plain, lagged, total, sems, part_sems,
+    plan, given, weights, keep, send, token, codes, held, plain, lagged, total, sem, part_sems
 ):
-    steps, trials, neurons = spikes.shape
+    steps, trials = plan.steps, plan.trials
     unit_count = weights.shape[0]
     delays = lagged.shape[0]
-    blocks = neurons // 128
+    blocks = plan.blocks
     half, rows = keep.shape[:2]
     chunk = held.shape[0] // part_sems.shape[0]
     chunks = unit_count // chunk
-    small = [
-        pltpu.make_async_copy(listed, codes, sems.at[0]),
-        pltpu.make_async_copy(spikes, given, sems.at[1]),
-    ]
-    for copy in small:
-        copy.start()
+    listed = pltpu.make_async_copy(given.at[pl.ds(up(plan.width, 8), 8)], codes, sem)
+    listed.start()
 
     def part(index):
         where = pl.ds(index * chunk, chunk)
@@ -134,15 +134,14 @@
     plain[...] = jnp.zeros_like(plain)
     lagged[...] = jnp.zeros_like(lagged)
     token[...] = jnp.zeros_like(token)
-    for copy in small:
-        copy.wait()
     front = trials * delays
     for step in range(steps):
         start = front + step * trials
-        plain[start : start + trials, :] = given[step].astype(F32)
+        plain[start : start + trials, :] = given[step * trials : (step + 1) * trials].astype(F32)
     for delay in range(delays):
         start = front - trials * (delay + 1)
         lagged[delay, 0:rows, :] = plain[start : start + rows, :].astype(BF16)
+    listed.wait()
     me = lax.axis_index("area")
 
     def some(index, _):
@@ -165,35 +164,43 @@
     send[...] = total[half:]
 
 
-def payload_sums(plan, spikes, weights, codes):
-    steps, trials, neurons = spikes.shape
-    unit_count = weights.shape[0]
+def payload_sums(plan, given, weights):
+    unit_count, neurons = weights.shape[:2]
     rows, delays = plan.arriving, plan.delays
     chunk = next(size for size in (16, 12, 8, 6, 4, 3, 2, 1) if unit_count % size == 0)
     half = jax.ShapeDtypeStruct((plan.lanes * plan.blocks, rows, 128), F32)
     return pl.pallas_call(
         functools.partial(payload_kernel, plan),
-        out_shape=(half, half, jax.ShapeDtypeStruct((16, 128), BF16)),
-        in_specs=[HBM] * 3,
+        out_shape=(half, half, jax.ShapeDtypeStruct((8, 128), F32)),
+        in_specs=[VMEM, HBM],
         out_specs=(VMEM,) * 3,
         scratch_shapes=[
-            pltpu.SMEM((3, unit_count), jnp.int32),
-            pltpu.VMEM(spikes.shape, jnp.int32),
+            pltpu.SMEM((8, neurons), jnp.int32),
             pltpu.VMEM(weights.shape, BF16),
-            pltpu.VMEM((trials * delays + rows, neurons), F32),
+            pltpu.VMEM((plan.trials * delays + rows, neurons), F32),
             pltpu.VMEM((delays, up(rows, 16), neurons), BF16),
             pltpu.VMEM((2 * plan.lanes * plan.blocks, rows, 128), F32),
-            pltpu.SemaphoreType.DMA((2,)),
+            pltpu.SemaphoreType.DMA,
             pltpu.SemaphoreType.DMA((unit_count // chunk,)),
         ],
-        compiler_params=params(62),
+        compiler_params=params(52),
         name="payload",
-    )(codes, spikes, weights)
-
-
-def known_kernel(plan, spikes, population, history, kernel, out, reach, series, fresh, lags):
-    steps, trials, neurons = spikes.shape
+    )(given, weights)
+
+
+def known_kernel(plan, given, population, history, kernel, out, reach, series, fresh, lags, sorted_):
+    steps, trials, neurons = plan.steps, plan.trials, given.shape[1]
     pops, kinds, _, taps = history.shape
+    channels, parts = kernel.shape[0], pops * kinds
+    some = 256 // parts
+    row = lax.broadcasted_iota(jnp.int32, (256, 256), 0)
+    column = lax.broadcasted_iota(jnp.int32, (256, 256), 1)
+    order = (column == row % some * parts + row // some).astype(F32).astype(BF16)
+    for index in range(channels // some):
+        rows = kernel[index * some : (index + 1) * some].reshape(256, taps)
+        rows = dot(order, rows).astype(BF16)
+        for part in range(parts):
+            sorted_[part, index * some : (index + 1) * some] = rows[part * some : (part + 1) * some]
     group = kinds * trials
     lane = lax.broadcasted_iota(jnp.int32, (pops * group, taps), 1)
     for pop in range(pops):
@@ -208,7 +215,7 @@
 
     which = lax.broadcasted_iota(jnp.int32, (8, neurons), 0)
     member = (which == population[...].reshape(1, -1)).astype(F32).astype(BF16)
-    rows = spikes[...].reshape(steps * trials, neurons).astype(F32).astype(BF16)
+    rows = given[0 : steps * trials].astype(F32).astype(BF16)
     rates = (dot(member, rows, NT) / (neurons / pops)).astype(BF16)
     fresh[...] = jnp.zeros_like(fresh)
     row = lax.broadcasted_iota(jnp.int32, (steps * trials, taps), 0)
@@ -229,12 +236,12 @@
                 row = part * trials + trial
                 spot = trial * steps + step
                 lags[part, spot : spot + 1, :] = shifted[row : row + 1, :]
-    total = dot(kernel[:, 0:taps], lags[0].astype(BF16), NT)
-    for part in range(1, pops * kinds):
-        total += dot(kernel[:, part * taps : (part + 1) * taps], lags[part].astype(BF16), NT)
+    total = dot(sorted_[0], lags[0].astype(BF16), NT)
+    for part in range(1, parts):
+        total += dot(sorted_[part], lags[part].astype(BF16), NT)
     out[...] = total
 
-    channels, share, wide = kernel.shape[0], plan.share, plan.taps_lanes
+    share, wide = plan.share, plan.taps_lanes
     row = lax.broadcasted_iota(jnp.int32, (128, wide), 0)
     column = lax.broadcasted_iota(jnp.int32, (128, wide), 1)
     spread = (row == column // share).astype(F32).astype(BF16)
@@ -246,14 +253,13 @@
     gather = (row == column // share).astype(F32).astype(BF16)
     reach[...] = jnp.zeros_like(reach)
     for pop in range(pops):
-        start = (pop * kinds + 1) * taps
-        wider = jnp.where(same, dot(kernel[:, start : start + 128], spread), 0.0)
+        wider = jnp.where(same, dot(sorted_[pop * kinds + 1, :, 0:128], spread), 0.0)
         packed = dot(gather, wider.astype(BF16))
         for tile in range(wide // 128):
             reach[:, tile * pops + pop, :] = packed[:, tile * 128 : tile * 128 + 128]
 
 
-def known_lfp(plan, spikes, population, history, kernel):
+def known_lfp(plan, given, population, history, kernel):
     pops, kinds, trials, taps = history.shape
     channels = kernel.shape[0]
     return pl.pallas_call(
@@ -268,10 +274,11 @@
             pltpu.VMEM((pops * kinds * trials, taps), F32),
             pltpu.VMEM((pops * kinds * trials, taps), F32),
             pltpu.VMEM((pops * kinds, 128, taps), F32),
+            pltpu.VMEM((pops * kinds, channels, taps), BF16),
         ],
         compiler_params=params(16),
         name="known_lfp",
-    )(spikes, population, history, kernel)
+    )(given, population, history, kernel)
 
 
 def pack_signal(plan, values):
@@ -297,7 +304,7 @@
 
 
 def compress_kernel(
-    plan, mine, got, given, cycle, start, known, taps, keep, send, carried, signal, room
+    plan, mine, got, near, far, cycle, start, known, taps, keep, send, carried, signal, room
 ):
     trials, steps, delays, blocks = plan.trials, plan.steps, plan.delays, plan.blocks
     me = lax.axis_index("area")
@@ -317,10 +324,11 @@
                 arriving = mine[lane * blocks + block] + got[lane * blocks + block]
                 early = arriving[0 : trials * delays] + own * cycle[block]
                 arriving = jnp.concatenate([early, arriving[trials * delays :]], axis=0)
-                facts = given[lane, block * 8 : block * 8 + 8]
+                spot = pl.multiple_of((index * blocks + block) * 8, 8)
+                facts = (far if bit else near)[pl.ds(spot, 8)]
                 last = facts[0:trials]
-                leak = facts[trials : trials + 1] + facts[trials + 1 : trials + 2]
-                population = facts[trials + 2 : trials + 3]
+                leak = facts[trials : trials + 1]
+                population = facts[trials + 1 : trials + 2]
                 membrane = own * start[block]
                 for step in range(steps):
                     current = arriving[step * trials : (step + 1) * trials]
@@ -382,11 +390,11 @@
     out[base:] = rows.astype(BF16)
 
 
-def compress(plan, mine, got, given, cycle, start, known, taps):
+def compress(plan, mine, got, near, far, cycle, start, known, taps):
     return pl.pallas_call(
         functools.partial(compress_kernel, plan),
         out_shape=(plan.keep(plan.lanes // 2), plan.send(plan.lanes // 2, 0), plan.carried()),
-        in_specs=[VMEM] * 7,
+        in_specs=[VMEM] * 8,
         out_specs=(VMEM,) * 3,
         scratch_shapes=[
             pltpu.VMEM((plan.signal, plan.signal_lanes), F32),
@@ -394,7 +402,7 @@
         ],
         compiler_params=params(32),
         name="compress",
-    )(mine, got, given, cycle, start, known, taps)
+    )(mine, got, near, far, cycle, start, known, taps)
 
 
 def fold_kernel(plan, slots, stage, direct, held, got, carried, keep, *refs):
@@ -598,36 +606,33 @@
     quarter = plan.lanes // 4
     far = [plan.mask(index * quarter) for index in (1, 2, 3)]
 
-    facts, codes = facts_of(
+    facts, given = facts_of(
         plan, spikes, leak_rate, population, destination[:, 0], target_block, delay_slot
     )
+    size = facts.shape[0]
     facts = [facts] + [swap(facts, mask, area_count) for mask in far]
-    mine, goes, token = payload_sums(plan, spikes, weights, codes)
+    mine, goes, token = payload_sums(plan, given, weights)
     got = swap(goes, 1, area_count)
-    size = blocks * 8
-    facts = jnp.concatenate(facts)
-    lane = quarter // 2
-    while lane:
-        count = facts.shape[0]
-        message = facts
-        if lane == quarter // 2:
-            blank = jnp.zeros((max(0, 512 - count - token.shape[0]), 128), BF16)
-            message = jnp.concatenate([facts, token, blank])
-        more = swap(message, plan.mask(lane), area_count)[:count]
-        facts = jnp.stack([facts.reshape(-1, size, 128), more.reshape(-1, size, 128)], axis=1)
-        facts = facts.reshape(-1, 128)
-        lane //= 2
-    facts = facts.astype(F32).reshape(-1, size, 128)
-
-    flat = lfp_kernel.reshape(channels, -1)
-    known, first = known_lfp(plan, spikes, population, history, flat)
+    blank = jnp.zeros((max(0, PAD - 4 * size - token.shape[0]), 128), F32)
+    near = jnp.concatenate(facts + [token, blank])
+    count, lane = 4 * size, quarter // 2
+    while True:
+        more = swap(near, plan.mask(lane), area_count)
+        if lane == 1:
+            break
+        near = jnp.stack(
+            [near[:count].reshape(-1, size, 128), more[:count].reshape(-1, size, 128)], axis=1
+        ).reshape(-1, 128)
+        count, lane = 2 * count, lane // 2
+
+    known, first = known_lfp(plan, given, population, history, lfp_kernel)
     known = known.reshape(area_count, share, 128)
     known = jnp.pad(known, ((0, 0), (0, plan.groups * 8 - share), (0, 0)))
 
     cycle = jnp.transpose(cycle_start, (1, 0, 2)).reshape(delays * trials, blocks, 128)
     cycle = jnp.transpose(cycle, (1, 0, 2))
     start = jnp.transpose(membrane_start.reshape(trials, blocks, 128), (1, 0, 2))
-    keep, send, carried = compress(plan, mine, got, facts, cycle, start, known, first)
+    keep, send, carried = compress(plan, mine, got, near, more, cycle, start, known, first)
 
     slots, stage = plan.lanes // 2, 0
     got = swap(send, plan.mask(1), area_count)

time: 40.4 us -> 36.5 us (0.903)
  local copies, waits for them, and re-layouts: 3.76 us -> 1.04 us
  Pallas kernels: 12.3 us -> 11.1 us
  starting transfers between devices: 14.1 us -> 15.3 us
  waiting for transfers between devices: 8.58 us -> 7.51 us
    reshape x1 -> x0, local copies, waits for them, and re-layouts: 2.86 us -> none  [body(): flat = lfp_kernel.reshape(channels, -1)]
    pallas_call x1, Pallas kernels: 7.09 us -> 5.24 us  [payload_sums(): pl.pallas_call(functools.partial(payload_kernel, plan), out_shape=(half,...]
    ppermute x10, starting transfers between devices: 14.1 us -> 15.3 us  [swap(): lax.ppermute(values, 'area', [(i, i ^ bit) for i in range(area_count)])]
    ppermute x10, waiting for transfers between devices: 8.58 us -> 7.51 us  [swap(): lax.ppermute(values, 'area', [(i, i ^ bit) for i in range(area_count)])]
    pallas_call x1, Pallas kernels: 1.64 us -> 2.21 us  [known_lfp(): pl.pallas_call(functools.partial(known_kernel, plan), out_shape=(jax.Shap...]
    unnamed x19 -> x21, local copies, waits for them, and re-layouts: 0.76 us -> 0.93 us
  transfers between devices with their start and end apart: 10 -> 10, of which waited for: 4 -> 5; matrix products, arithmetic and copies ran while one was open for 9% -> 0% of each run, Pallas kernels for 22% -> 21%
where the time goes in v5:
time: 36.5 us; the launch traced here: 36.3 us
  starting transfers between devices  15.3 us (42%)
  Pallas kernels  11.1 us (30%)
  waiting for transfers between devices  7.51 us (21%)
  local copies, waits for them, and re-layouts  1.04 us (3%)
  between operations  0.8 us (2%)
  other arithmetic  0.61 us (2%)
    ppermute x10, starting transfers between devices, swap(): lax.ppermute(values, 'area', [(i, i ^ bit) for i in range(area_count)])  15.3 us
    ppermute x10, waiting for transfers between devices, swap(): lax.ppermute(values, 'area', [(i, i ^ bit) for i in range(area_count)])  7.51 us
    pallas_call x1, Pallas kernels, payload_sums(): pl.pallas_call(functools.partial(payload_kernel, plan), out_shape=(half,...  5.24 us
    pallas_call x1, Pallas kernels, known_lfp(): pl.pallas_call(functools.partial(known_kernel, plan), out_shape=(jax.Shap...  2.21 us
    pallas_call x1, Pallas kernels, facts_of(): pl.pallas_call(functools.partial(facts_kernel, plan), out_shape=(jax.Shap...  1.63 us
    pallas_call x1, Pallas kernels, finish(): pl.pallas_call(functools.partial(finish_kernel, plan), out_shape=(jax.Sha...  1.32 us
    unnamed x21, local copies, waits for them, and re-layouts  0.93 us
  transfers between devices with their start and end apart: 10, of which 5 were waited for; matrix products, arithmetic and copies ran while one was open for 0% of the time, Pallas kernels for 21%

profile of v5, /device:TPU:0, one launch (start us, length us, event | category | flops | bytes accessed | tf_op | source)
XLA Modules:
  0.0 36.3 jit_solution(108599048741893163)
XLA Ops:
  0.6 0.0 copy-start
  0.6 1.6 %facts.1 = (f32[24,128]{1,0:T(8,128)}, s32[48,384]{1,0:T(8,128)}) custom-call(s32[10,4,384]{2,1,0:T(4,128)} %bitcast.13, f32[384]{0:T(512)} %leak.1, s32[384]{0:T(512)} %population.3, s32[96]{0:T(128)} %bitcast.15, s32[96]{0:T(128)} %target_block.1, s32[96]{0:T(128)} %delay_slot.1), custom_call_target="tpu_custom_call" | custom-call | tf_op jit(solution)/shard_map/facts/pallas_call | solution.py:102
  2.3 3.0 %collective-permute-start.1 = (f32[24,128]{1,0:T(8,128)}, f32[24,128]{1,0:T(8,128)S(1)}, u32[]{:S(2)}, u32[]{:S(2)}) collective-permute-start(f32[24,128]{1,0:T(8,128)} %get-tuple-element.25), channel_id=1, source_target_pairs={{0,4},{1,5},{2,6},{3,7},{4,0},{5,1},{6,2},{7,3},{8,12},{9,13},{10,... | collective-permute-start | bytes 36872 | tf_op jit(solution)/shard_map/ppermute | solution.py:580
  5.3 1.7 %collective-permute-start.2 = (f32[24,128]{1,0:T(8,128)}, f32[24,128]{1,0:T(8,128)S(1)}, u32[]{:S(2)}, u32[]{:S(2)}) collective-permute-start(f32[24,128]{1,0:T(8,128)} %get-tuple-element.25), channel_id=1, source_target_pairs={{0,9},{1,8},{2,11},{3,10},{4,13},{5,12},{6,15},{7,14},{8,1},{9,0},... | collective-permute-start | bytes 36872 | tf_op jit(solution)/shard_map/ppermute | solution.py:580
  7.0 0.3 collective-permute-start.3
  7.4 0.0 copy-start.1
  7.4 0.9 %copy-done.1 = s32[48,384]{1,0:T(8,128)S(1)} copy-done((s32[48,384]{1,0:T(8,128)S(1)}, s32[48,384]{1,0:T(8,128)}, u32[]{:S(2)}) %copy-start.1) | copy-done | bytes 73752
  8.3 0.0 copy-start.7
  8.3 0.0 copy-start.6
  8.3 0.0 copy-start.2
  8.3 0.0 copy-start.3
  8.3 0.0 copy-start.4
  8.3 0.0 copy-start.5
  8.3 5.2 %payload.1 = (f32[24,56,128]{2,1,0:T(8,128)S(1)}, f32[24,56,128]{2,1,0:T(8,128)}, f32[8,128]{1,0:T(8,128)S(1)}) custom-call(s32[48,384]{1,0:T(8,128)S(1)} %copy-done.1, bf16[96,384,128]{2,1,0:T(8,128)(2,1)} %weights.1), custom_call_target="tpu_custom_call" | custom-call | tf_op jit(solution)/shard_map/payload/pallas_call | solution.py:172
  13.5 0.7 %collective-permute-start = (f32[24,56,128]{2,1,0:T(8,128)}, f32[24,56,128]{2,1,0:T(8,128)S(1)}, u32[]{:S(2)}, u32[]{:S(2)}) collective-permute-start(f32[24,56,128]{2,1,0:T(8,128)} %get-tuple-element.24), channel_id=1, source_target_pairs={{0,1},{1,0},{2,3},{3,2},{4,5},{5,4},{6,7},{7,6},{8,9},{9,8},{10,11... | collective-permute-start | bytes 2064392 | tf_op jit(solution)/shard_map/ppermute | solution.py:580
  14.2 0.0 copy-done.7
  14.2 0.0 collective-permute-done.1
  14.2 0.0 collective-permute-done.2
  14.3 0.0 collective-permute-done.3
  14.3 1.6 %collective-permute-start.4 = (f32[112,128]{1,0:T(8,128)S(1)}, f32[112,128]{1,0:T(8,128)S(1)}, u32[]{:S(2)}, u32[]{:S(2)}) collective-permute-start(f32[112,128]{1,0:T(8,128)S(1)} %constant_dynamic-update-slice_fusion.near), channel_id=1, source_target_pairs={{0,2},{1,3},{2,0},{3,1},{4,6},{5,7},{6,4},{7,5},{8,10},{9,11},{10,... | collective-permute-start | bytes 172040 | tf_op jit(solution)/shard_map/ppermute | solution.py:580
  15.9 0.0 copy-done.6
  15.9 0.0 copy-done
  15.9 0.0 copy-done.2
  15.9 0.0 copy-done.3
  16.0 0.0 copy-done.4
  16.0 2.2 %known_lfp.1 = (f32[384,128]{1,0:T(8,128)S(1)}, f32[16,8,128]{2,1,0:T(8,128)S(1)}) custom-call(s32[48,384]{1,0:T(8,128)S(1)} %copy-done.2, s32[384]{0:T(512)S(1)} %copy-done.4, f32[4,2,4,256]{3,2,1,0:T(4,128)S(1)} %copy-done.3, bf16[384,4,2,256]{3,2,1,0:T(2,128)(2,1)S(1)} %copy-done), custom_call_target="tpu_custom_call" | custom-call | tf_op jit(solution)/shard_map/known_lfp/pallas_call | solution.py:265
  18.2 0.4 %collective-permute-done.4.far = f32[112,128]{1,0:T(8,128)S(1)} collective-permute-done((f32[112,128]{1,0:T(8,128)S(1)}, f32[112,128]{1,0:T(8,128)S(1)}, u32[]{:S(2)}, u32[]{:S(2)}) %collective-permute-start.4) | collective-permute-done | bytes 57376 | tf_op jit(solution)/shard_map/ppermute | solution.py:580
  18.6 0.0 collective-permute-done.got
  18.6 0.0 copy-done.5
  18.6 0.6 %compress.1 = (f32[360,128]{1,0:T(8,128)S(1)}, bf16[416,128]{1,0:T(8,128)(2,1)S(1)}, bf16[128,128]{1,0:T(8,128)(2,1)S(1)}) custom-call(f32[24,56,128]{2,1,0:T(8,128)S(1)} %get-tuple-element.23.mine, f32[24,56,128]{2,1,0:T(8,128)S(1)} %collective-permute-done.got, f32[112,128]{1,0:T(8,128)S(1)} %constant_dynamic-update-slice_fusion.near, ...), custom_call_target="tpu_custom_call" | custom-call | tf_op jit(solution)/shard_map/compress/pallas_call | solution.py:394
  19.1 1.5 %collective-permute-start.5 = (bf16[416,128]{1,0:T(8,128)(2,1)S(1)}, bf16[416,128]{1,0:T(8,128)(2,1)S(1)}, u32[]{:S(2)}, u32[]{:S(2)}) collective-permute-start(bf16[416,128]{1,0:T(8,128)(2,1)S(1)} %get-tuple-element.30), channel_id=1, source_target_pairs={{0,2},{1,3},{2,0},{3,1},{4,6},{5,7},{6,4},{7,5},{8,10},{9,11},{10,... | collective-permute-start | bytes 319496 | tf_op jit(solution)/shard_map/ppermute | solution.py:580
  20.7 3.2 %collective-permute-done.5.got = bf16[416,128]{1,0:T(8,128)(2,1)S(1)} collective-permute-done((bf16[416,128]{1,0:T(8,128)(2,1)S(1)}, bf16[416,128]{1,0:T(8,128)(2,1)S(1)}, u32[]{:S(2)}, u32[]{:S(2)}) %collective-permute-start.5) | collective-permute-done | bytes 106528 | tf_op jit(solution)/shard_map/ppermute | solution.py:580
  23.9 0.2 fold.1
  24.0 0.7 %collective-permute-start.6 = (bf16[128,128]{1,0:T(8,128)(2,1)S(1)}, bf16[128,128]{1,0:T(8,128)(2,1)S(1)}, u32[]{:S(2)}, u32[]{:S(2)}) collective-permute-start(bf16[128,128]{1,0:T(8,128)(2,1)S(1)} %get-tuple-element.34), channel_id=1, source_target_pairs={{0,4},{1,5},{2,6},{3,7},{4,0},{5,1},{6,2},{7,3},{8,12},{9,13},{10,... | collective-permute-start | bytes 98312 | tf_op jit(solution)/shard_map/ppermute | solution.py:580
  24.8 1.4 %collective-permute-start.7 = (bf16[128,128]{1,0:T(8,128)(2,1)S(1)}, bf16[128,128]{1,0:T(8,128)(2,1)S(1)}, u32[]{:S(2)}, u32[]{:S(2)}) collective-permute-start(bf16[128,128]{1,0:T(8,128)(2,1)S(1)} %get-tuple-element.35), channel_id=1, source_target_pairs={{0,9},{1,8},{2,11},{3,10},{4,13},{5,12},{6,15},{7,14},{8,1},{9,0},... | collective-permute-start | bytes 98312 | tf_op jit(solution)/shard_map/ppermute | solution.py:580
  26.1 2.1 %collective-permute-start.8 = (bf16[128,128]{1,0:T(8,128)(2,1)S(1)}, bf16[128,128]{1,0:T(8,128)(2,1)S(1)}, u32[]{:S(2)}, u32[]{:S(2)}) collective-permute-start(bf16[128,128]{1,0:T(8,128)(2,1)S(1)} %get-tuple-element.36), channel_id=1, source_target_pairs={{0,13},{1,12},{2,15},{3,14},{4,9},{5,8},{6,11},{7,10},{8,5},{9,4},... | collective-permute-start | bytes 98312 | tf_op jit(solution)/shard_map/ppermute | solution.py:580
  28.2 0.0 collective-permute-done.6.refs_0_
  28.2 0.8 %collective-permute-done.7.refs_1_ = bf16[128,128]{1,0:T(8,128)(2,1)S(1)} collective-permute-done((bf16[128,128]{1,0:T(8,128)(2,1)S(1)}, bf16[128,128]{1,0:T(8,128)(2,1)S(1)}, u32[]{:S(2)}, u32[]{:S(2)}) %collective-permute-start.7) | collective-permute-done | bytes 32800 | tf_op jit(solution)/shard_map/ppermute | solution.py:580
  29.0 2.3 %collective-permute-done.8.refs_2_ = bf16[128,128]{1,0:T(8,128)(2,1)S(1)} collective-permute-done((bf16[128,128]{1,0:T(8,128)(2,1)S(1)}, bf16[128,128]{1,0:T(8,128)(2,1)S(1)}, u32[]{:S(2)}, u32[]{:S(2)}) %collective-permute-start.8) | collective-permute-done | bytes 32800 | tf_op jit(solution)/shard_map/ppermute | solution.py:580
  31.3 1.3 %finish.1 = (f32[4,384]{1,0:T(4,128)}, f32[4,4,384]{2,1,0:T(4,128)}, f32[8,128]{1,0:T(8,128)S(1)}, f32[8,128]{1,0:T(8,128)S(1)}) custom-call(f32[120,128]{1,0:T(8,128)S(1)} %get-tuple-element.32.held, bf16[128,128]{1,0:T(8,128)(2,1)S(1)} %get-tuple-element.33.carried, bf16[128,128]{1,0:T(8,128)(2,1)S(1)} %collective-permute-done.6.refs_0_, ...), custom_call_target="tpu_custom_call" | custom-call | tf_op jit(solution)/shard_map/finish/pallas_call | solution.py:558
  32.6 2.2 %collective-permute-start.9 = (f32[8,128]{1,0:T(8,128)S(1)}, f32[8,128]{1,0:T(8,128)S(1)}, u32[]{:S(2)}, u32[]{:S(2)}) collective-permute-start(f32[8,128]{1,0:T(8,128)S(1)} %get-tuple-element.40), channel_id=1, source_target_pairs={{0,1},{1,0},{2,3},{3,2},{4,5},{5,4},{6,7},{7,6},{8,9},{9,8},{10,11... | collective-permute-start | bytes 12296 | tf_op jit(solution)/shard_map/ppermute | solution.py:580
  34.8 0.8 %collective-permute-done.9 = f32[8,128]{1,0:T(8,128)S(1)} collective-permute-done((f32[8,128]{1,0:T(8,128)S(1)}, f32[8,128]{1,0:T(8,128)S(1)}, u32[]{:S(2)}, u32[]{:S(2)}) %collective-permute-start.9) | collective-permute-done | bytes 4128 | tf_op jit(solution)/shard_map/ppermute | solution.py:580
  35.7 0.1 fusion
  35.7 0.6 %pad_maximum_fusion = f32[24,40]{1,0:T(8,128)} fusion(f32[8,40]{1,0:T(8,128)S(1)} %get-tuple-element.42, f32[8,40]{1,0:T(8,128)S(1)} %get-tuple-element.43, f32[8,40]{1,0:T(8,128)S(1)} %get-tuple-element.41), kind=kLoop, calls=%fused_computation.7 | loop fusion | flops 1920 | bytes 7680 | tf_op jit(solution)/shard_map/concatenate | solution.py:649
  (10 shorter events, 0.1 us)
Async XLA Ops:
  0.6 15.3 %copy-start = (bf16[384,4,2,256]{3,2,1,0:T(2,128)(2,1)S(1)}, bf16[384,4,2,256]{3,2,1,0:T(2,128)(2,1)}, u32[]{:S(2)}) copy-start(bf16[384,4,2,256]{3,2,1,0:T(2,128)(2,1)} %kernel.1) | copy-start | bytes 4718596
  2.3 12.0 %collective-permute-start.1 = (f32[24,128]{1,0:T(8,128)}, f32[24,128]{1,0:T(8,128)S(1)}, u32[]{:S(2)}, u32[]{:S(2)}) collective-permute-start(f32[24,128]{1,0:T(8,128)} %get-tuple-element.25), channel_id=1, source_target_pairs={{0,4},{1,5},{2,6},{3,7},{4,0},{5,1},{6,2},{7,3},{8,12},{9,13},{10,... | collective-permute-start | bytes 36872 | tf_op jit(solution)/shard_map/ppermute | solution.py:580
  5.3 9.0 %collective-permute-start.2 = (f32[24,128]{1,0:T(8,128)}, f32[24,128]{1,0:T(8,128)S(1)}, u32[]{:S(2)}, u32[]{:S(2)}) collective-permute-start(f32[24,128]{1,0:T(8,128)} %get-tuple-element.25), channel_id=1, source_target_pairs={{0,9},{1,8},{2,11},{3,10},{4,13},{5,12},{6,15},{7,14},{8,1},{9,0},... | collective-permute-start | bytes 36872 | tf_op jit(solution)/shard_map/ppermute | solution.py:580
  7.0 7.2 %collective-permute-start.3 = (f32[24,128]{1,0:T(8,128)}, f32[24,128]{1,0:T(8,128)S(1)}, u32[]{:S(2)}, u32[]{:S(2)}) collective-permute-start(f32[24,128]{1,0:T(8,128)} %get-tuple-element.25), channel_id=1, source_target_pairs={{0,13},{1,12},{2,15},{3,14},{4,9},{5,8},{6,11},{7,10},{8,5},{9,4},... | collective-permute-start | bytes 36872 | tf_op jit(solution)/shard_map/ppermute | solution.py:580
  7.4 0.9 %copy-start.1 = (s32[48,384]{1,0:T(8,128)S(1)}, s32[48,384]{1,0:T(8,128)}, u32[]{:S(2)}) copy-start(s32[48,384]{1,0:T(8,128)} %get-tuple-element.22.given) | copy-start | bytes 221188
  8.3 6.0 %copy-start.7 = (f32[24,128]{1,0:T(8,128)S(1)}, f32[24,128]{1,0:T(8,128)}, u32[]{:S(2)}) copy-start(f32[24,128]{1,0:T(8,128)} %get-tuple-element.25) | copy-start | bytes 36868
  8.3 7.6 %copy-start.6 = (f32[4,4,384]{2,1,0:T(4,128)S(1)}, f32[4,4,384]{2,1,0:T(4,128)}, u32[]{:S(2)}) copy-start(f32[4,4,384]{2,1,0:T(4,128)} %param.19) | copy-start | bytes 73732
  8.3 7.7 %copy-start.2 = (s32[48,384]{1,0:T(8,128)S(1)}, s32[48,384]{1,0:T(8,128)}, u32[]{:S(2)}) copy-start(s32[48,384]{1,0:T(8,128)} %get-tuple-element.22.given) | copy-start | bytes 221188
  8.3 7.7 %copy-start.3 = (f32[4,2,4,256]{3,2,1,0:T(4,128)S(1)}, f32[4,2,4,256]{3,2,1,0:T(4,128)}, u32[]{:S(2)}) copy-start(f32[4,2,4,256]{3,2,1,0:T(4,128)} %history.1) | copy-start | bytes 98308
  8.3 7.7 %copy-start.4 = (s32[384]{0:T(512)S(1)}, s32[384]{0:T(512)}, u32[]{:S(2)}) copy-start(s32[384]{0:T(512)} %population.3) | copy-start | bytes 4612
  8.3 10.3 %copy-start.5 = (f32[4,384]{1,0:T(4,128)S(1)}, f32[4,384]{1,0:T(4,128)}, u32[]{:S(2)}) copy-start(f32[4,384]{1,0:T(4,128)} %param.18) | copy-start | bytes 18436
  13.5 5.0 %collective-permute-start = (f32[24,56,128]{2,1,0:T(8,128)}, f32[24,56,128]{2,1,0:T(8,128)S(1)}, u32[]{:S(2)}, u32[]{:S(2)}) collective-permute-start(f32[24,56,128]{2,1,0:T(8,128)} %get-tuple-element.24), channel_id=1, source_target_pairs={{0,1},{1,0},{2,3},{3,2},{4,5},{5,4},{6,7},{7,6},{8,9},{9,8},{10,11... | collective-permute-start | bytes 2064392 | tf_op jit(solution)/shard_map/ppermute | solution.py:580
  14.3 4.2 %collective-permute-start.4 = (f32[112,128]{1,0:T(8,128)S(1)}, f32[112,128]{1,0:T(8,128)S(1)}, u32[]{:S(2)}, u32[]{:S(2)}) collective-permute-start(f32[112,128]{1,0:T(8,128)S(1)} %constant_dynamic-update-slice_fusion.near), channel_id=1, source_target_pairs={{0,2},{1,3},{2,0},{3,1},{4,6},{5,7},{6,4},{7,5},{8,10},{9,11},{10,... | collective-permute-start | bytes 172040 | tf_op jit(solution)/shard_map/ppermute | solution.py:580
  19.1 4.7 %collective-permute-start.5 = (bf16[416,128]{1,0:T(8,128)(2,1)S(1)}, bf16[416,128]{1,0:T(8,128)(2,1)S(1)}, u32[]{:S(2)}, u32[]{:S(2)}) collective-permute-start(bf16[416,128]{1,0:T(8,128)(2,1)S(1)} %get-tuple-element.30), channel_id=1, source_target_pairs={{0,2},{1,3},{2,0},{3,1},{4,6},{5,7},{6,4},{7,5},{8,10},{9,11},{10,... | collective-permute-start | bytes 319496 | tf_op jit(solution)/shard_map/ppermute | solution.py:580
  24.0 4.2 %collective-permute-start.6 = (bf16[128,128]{1,0:T(8,128)(2,1)S(1)}, bf16[128,128]{1,0:T(8,128)(2,1)S(1)}, u32[]{:S(2)}, u32[]{:S(2)}) collective-permute-start(bf16[128,128]{1,0:T(8,128)(2,1)S(1)} %get-tuple-element.34), channel_id=1, source_target_pairs={{0,4},{1,5},{2,6},{3,7},{4,0},{5,1},{6,2},{7,3},{8,12},{9,13},{10,... | collective-permute-start | bytes 98312 | tf_op jit(solution)/shard_map/ppermute | solution.py:580
  24.8 4.2 %collective-permute-start.7 = (bf16[128,128]{1,0:T(8,128)(2,1)S(1)}, bf16[128,128]{1,0:T(8,128)(2,1)S(1)}, u32[]{:S(2)}, u32[]{:S(2)}) collective-permute-start(bf16[128,128]{1,0:T(8,128)(2,1)S(1)} %get-tuple-element.35), channel_id=1, source_target_pairs={{0,9},{1,8},{2,11},{3,10},{4,13},{5,12},{6,15},{7,14},{8,1},{9,0},... | collective-permute-start | bytes 98312 | tf_op jit(solution)/shard_map/ppermute | solution.py:580
  26.1 5.2 %collective-permute-start.8 = (bf16[128,128]{1,0:T(8,128)(2,1)S(1)}, bf16[128,128]{1,0:T(8,128)(2,1)S(1)}, u32[]{:S(2)}, u32[]{:S(2)}) collective-permute-start(bf16[128,128]{1,0:T(8,128)(2,1)S(1)} %get-tuple-element.36), channel_id=1, source_target_pairs={{0,13},{1,12},{2,15},{3,14},{4,9},{5,8},{6,11},{7,10},{8,5},{9,4},... | collective-permute-start | bytes 98312 | tf_op jit(solution)/shard_map/ppermute | solution.py:580
  32.6 3.0 %collective-permute-start.9 = (f32[8,128]{1,0:T(8,128)S(1)}, f32[8,128]{1,0:T(8,128)S(1)}, u32[]{:S(2)}, u32[]{:S(2)}) collective-permute-start(f32[8,128]{1,0:T(8,128)S(1)} %get-tuple-element.40), channel_id=1, source_target_pairs={{0,1},{1,0},{2,3},{3,2},{4,5},{5,4},{6,7},{7,6},{8,9},{9,8},{10,11... | collective-permute-start | bytes 12296 | tf_op jit(solution)/shard_map/ppermute | solution.py:580

commit v6 on v5

--- a/solution.py
+++ b/solution.py
@@ -9,6 +9,7 @@
 
 BF16, F32 = jnp.bfloat16, jnp.float32
 PAD = 112
+LATE = (2, 3, 1)
 VMEM = pl.BlockSpec(memory_space=pltpu.VMEM)
 HBM = pl.BlockSpec(memory_space=pltpu.HBM)
 NT = (((1,), (1,)), ((), ()))
@@ -431,7 +432,7 @@
         rows = got[slot * size : slot * size + plan.held].astype(F32)
         rows = rows + held[slot * plan.held : (slot + 1) * plan.held]
         if direct and slot:
-            out = sends[slot - 1]
+            out = sends[LATE.index(slot)]
             room[0 : plan.main] = rows[: plan.main]
             room[plan.main : plan.main + plan.packed] = pack_signal(plan, tail)
             out[0 : plan.last] = room[...].astype(BF16)
@@ -498,7 +499,7 @@
         far, near = divmod(lane, span)
         if far:
             spot = plan.last + 16 + near * taps
-            slot = gots[far - 1][spot : spot + taps]
+            slot = gots[LATE.index(far)][spot : spot + taps]
         else:
             slot = carried[lane * taps : (lane + 1) * taps]
         slot = slot.astype(F32)
@@ -604,13 +605,13 @@
     share = plan.share
     spikes = jnp.transpose(spikes, (1, 0, 2))
     quarter = plan.lanes // 4
-    far = [plan.mask(index * quarter) for index in (1, 2, 3)]
 
     facts, given = facts_of(
         plan, spikes, leak_rate, population, destination[:, 0], target_block, delay_slot
     )
     size = facts.shape[0]
-    facts = [facts] + [swap(facts, mask, area_count) for mask in far]
+    came = {index: swap(facts, plan.mask(index * quarter), area_count) for index in (1, 2, 3)}
+    facts = [facts] + [came[index] for index in (1, 2, 3)]
     mine, goes, token = payload_sums(plan, given, weights)
     got = swap(goes, 1, area_count)
     blank = jnp.zeros((max(0, PAD - 4 * size - token.shape[0]), 128), F32)
@@ -641,7 +642,9 @@
         slots, stage = slots // 2, stage + 1
         got = swap(send, plan.mask(1 << stage), area_count)
     keep, *sends, carried = fold(plan, slots, stage, True, keep, got, carried)
-    gots = [swap(send, mask, area_count) for send, mask in zip(sends, far)]
+    gots = [
+        swap(send, plan.mask(index * quarter), area_count) for send, index in zip(sends, LATE)
+    ]
     membrane, cycle_out, own, other = finish(plan, neurons, keep, carried, gots)
     lfp = own + swap(other, 1, area_count)
     width = plan.width

time: 36.5 us -> 34.7 us (0.951)
  starting transfers between devices: 15.3 us -> 12.3 us
  waiting for transfers between devices: 7.51 us -> 8.72 us
    ppermute x10, starting transfers between devices: 15.3 us -> 12.3 us  [swap(): lax.ppermute(values, 'area', [(i, i ^ bit) for i in range(area_count)])]
    ppermute x10, waiting for transfers between devices: 7.51 us -> 8.72 us  [swap(): lax.ppermute(values, 'area', [(i, i ^ bit) for i in range(area_count)])]
  transfers between devices with their start and end apart: 10 -> 10, of which waited for: 5 -> 6; matrix products, arithmetic and copies ran while one was open for 0% -> 0% of each run, Pallas kernels for 21% -> 22%
where the time goes in v6:
time: 34.7 us; the launch traced here: 34.6 us
  starting transfers between devices  12.3 us (35%)
  Pallas kernels  11.1 us (32%)
  waiting for transfers between devices  8.72 us (25%)
  local copies, waits for them, and re-layouts  1.04 us (3%)
  between operations  0.8 us (2%)
  other arithmetic  0.61 us (2%)
    ppermute x10, starting transfers between devices, swap(): lax.ppermute(values, 'area', [(i, i ^ bit) for i in range(area_count)])  12.3 us
    ppermute x10, waiting for transfers between devices, swap(): lax.ppermute(values, 'area', [(i, i ^ bit) for i in range(area_count)])  8.72 us
    pallas_call x1, Pallas kernels, payload_sums(): pl.pallas_call(functools.partial(payload_kernel, plan), out_shape=(half,...  5.23 us
    pallas_call x1, Pallas kernels, known_lfp(): pl.pallas_call(functools.partial(known_kernel, plan), out_shape=(jax.Shap...  2.21 us
    pallas_call x1, Pallas kernels, facts_of(): pl.pallas_call(functools.partial(facts_kernel, plan), out_shape=(jax.Shap...  1.63 us
    pallas_call x1, Pallas kernels, finish(): pl.pallas_call(functools.partial(finish_kernel, plan), out_shape=(jax.Sha...  1.32 us
    unnamed x21, local copies, waits for them, and re-layouts  0.93 us
  transfers between devices with their start and end apart: 10, of which 6 were waited for; matrix products, arithmetic and copies ran while one was open for 0% of the time, Pallas kernels for 22%

profile of v6, /device:TPU:0, one launch (start us, length us, event | category | flops | bytes accessed | tf_op | source)
XLA Modules:
  0.0 34.6 jit_solution(13004174537807686450)
XLA Ops:
  0.6 0.0 copy-start
  0.6 1.6 %facts.1 = (f32[24,128]{1,0:T(8,128)}, s32[48,384]{1,0:T(8,128)}) custom-call(s32[10,4,384]{2,1,0:T(4,128)} %bitcast.13, f32[384]{0:T(512)} %leak.1, s32[384]{0:T(512)} %population.3, s32[96]{0:T(128)} %bitcast.15, s32[96]{0:T(128)} %target_block.1, s32[96]{0:T(128)} %delay_slot.1), custom_call_target="tpu_custom_call" | custom-call | tf_op jit(solution)/shard_map/facts/pallas_call | solution.py:103
  2.3 3.0 %collective-permute-start.1 = (f32[24,128]{1,0:T(8,128)}, f32[24,128]{1,0:T(8,128)S(1)}, u32[]{:S(2)}, u32[]{:S(2)}) collective-permute-start(f32[24,128]{1,0:T(8,128)} %get-tuple-element.25), channel_id=1, source_target_pairs={{0,4},{1,5},{2,6},{3,7},{4,0},{5,1},{6,2},{7,3},{8,12},{9,13},{10,... | collective-permute-start | bytes 36872 | tf_op jit(solution)/shard_map/ppermute | solution.py:581
  5.3 1.7 %collective-permute-start.2 = (f32[24,128]{1,0:T(8,128)}, f32[24,128]{1,0:T(8,128)S(1)}, u32[]{:S(2)}, u32[]{:S(2)}) collective-permute-start(f32[24,128]{1,0:T(8,128)} %get-tuple-element.25), channel_id=1, source_target_pairs={{0,9},{1,8},{2,11},{3,10},{4,13},{5,12},{6,15},{7,14},{8,1},{9,0},... | collective-permute-start | bytes 36872 | tf_op jit(solution)/shard_map/ppermute | solution.py:581
  7.0 0.3 collective-permute-start.3
  7.4 0.0 copy-start.1
  7.4 0.9 %copy-done.1 = s32[48,384]{1,0:T(8,128)S(1)} copy-done((s32[48,384]{1,0:T(8,128)S(1)}, s32[48,384]{1,0:T(8,128)}, u32[]{:S(2)}) %copy-start.1) | copy-done | bytes 73752
  8.3 0.0 copy-start.7
  8.3 0.0 copy-start.6
  8.3 0.0 copy-start.2
  8.3 0.0 copy-start.3
  8.3 0.0 copy-start.4
  8.3 0.0 copy-start.5
  8.3 5.2 %payload.1 = (f32[24,56,128]{2,1,0:T(8,128)S(1)}, f32[24,56,128]{2,1,0:T(8,128)}, f32[8,128]{1,0:T(8,128)S(1)}) custom-call(s32[48,384]{1,0:T(8,128)S(1)} %copy-done.1, bf16[96,384,128]{2,1,0:T(8,128)(2,1)} %weights.1), custom_call_target="tpu_custom_call" | custom-call | tf_op jit(solution)/shard_map/payload/pallas_call | solution.py:173
  13.5 0.7 %collective-permute-start = (f32[24,56,128]{2,1,0:T(8,128)}, f32[24,56,128]{2,1,0:T(8,128)S(1)}, u32[]{:S(2)}, u32[]{:S(2)}) collective-permute-start(f32[24,56,128]{2,1,0:T(8,128)} %get-tuple-element.24), channel_id=1, source_target_pairs={{0,1},{1,0},{2,3},{3,2},{4,5},{5,4},{6,7},{7,6},{8,9},{9,8},{10,11... | collective-permute-start | bytes 2064392 | tf_op jit(solution)/shard_map/ppermute | solution.py:581
  14.2 0.0 copy-done.7
  14.2 0.0 collective-permute-done.1
  14.3 0.0 collective-permute-done.2
  14.3 0.0 collective-permute-done.3
  14.3 1.6 %collective-permute-start.4 = (f32[112,128]{1,0:T(8,128)S(1)}, f32[112,128]{1,0:T(8,128)S(1)}, u32[]{:S(2)}, u32[]{:S(2)}) collective-permute-start(f32[112,128]{1,0:T(8,128)S(1)} %constant_dynamic-update-slice_fusion.near), channel_id=1, source_target_pairs={{0,2},{1,3},{2,0},{3,1},{4,6},{5,7},{6,4},{7,5},{8,10},{9,11},{10,... | collective-permute-start | bytes 172040 | tf_op jit(solution)/shard_map/ppermute | solution.py:581
  15.9 0.0 copy-done.6
  15.9 0.0 copy-done
  15.9 0.0 copy-done.2
  15.9 0.0 copy-done.3
  16.0 0.0 copy-done.4
  16.0 2.2 %known_lfp.1 = (f32[384,128]{1,0:T(8,128)S(1)}, f32[16,8,128]{2,1,0:T(8,128)S(1)}) custom-call(s32[48,384]{1,0:T(8,128)S(1)} %copy-done.2, s32[384]{0:T(512)S(1)} %copy-done.4, f32[4,2,4,256]{3,2,1,0:T(4,128)S(1)} %copy-done.3, bf16[384,4,2,256]{3,2,1,0:T(2,128)(2,1)S(1)} %copy-done), custom_call_target="tpu_custom_call" | custom-call | tf_op jit(solution)/shard_map/known_lfp/pallas_call | solution.py:266
  18.2 0.4 %collective-permute-done.4.far = f32[112,128]{1,0:T(8,128)S(1)} collective-permute-done((f32[112,128]{1,0:T(8,128)S(1)}, f32[112,128]{1,0:T(8,128)S(1)}, u32[]{:S(2)}, u32[]{:S(2)}) %collective-permute-start.4) | collective-permute-done | bytes 57376 | tf_op jit(solution)/shard_map/ppermute | solution.py:581
  18.6 0.0 collective-permute-done.got
  18.6 0.0 copy-done.5
  18.6 0.5 %compress.1 = (f32[360,128]{1,0:T(8,128)S(1)}, bf16[416,128]{1,0:T(8,128)(2,1)S(1)}, bf16[128,128]{1,0:T(8,128)(2,1)S(1)}) custom-call(f32[24,56,128]{2,1,0:T(8,128)S(1)} %get-tuple-element.23.mine, f32[24,56,128]{2,1,0:T(8,128)S(1)} %collective-permute-done.got, f32[112,128]{1,0:T(8,128)S(1)} %constant_dynamic-update-slice_fusion.near, ...), custom_call_target="tpu_custom_call" | custom-call | tf_op jit(solution)/shard_map/compress/pallas_call | solution.py:395
  19.1 1.5 %collective-permute-start.5 = (bf16[416,128]{1,0:T(8,128)(2,1)S(1)}, bf16[416,128]{1,0:T(8,128)(2,1)S(1)}, u32[]{:S(2)}, u32[]{:S(2)}) collective-permute-start(bf16[416,128]{1,0:T(8,128)(2,1)S(1)} %get-tuple-element.30), channel_id=1, source_target_pairs={{0,2},{1,3},{2,0},{3,1},{4,6},{5,7},{6,4},{7,5},{8,10},{9,11},{10,... | collective-permute-start | bytes 319496 | tf_op jit(solution)/shard_map/ppermute | solution.py:581
  20.7 3.2 %collective-permute-done.5.got = bf16[416,128]{1,0:T(8,128)(2,1)S(1)} collective-permute-done((bf16[416,128]{1,0:T(8,128)(2,1)S(1)}, bf16[416,128]{1,0:T(8,128)(2,1)S(1)}, u32[]{:S(2)}, u32[]{:S(2)}) %collective-permute-start.5) | collective-permute-done | bytes 106528 | tf_op jit(solution)/shard_map/ppermute | solution.py:581
  23.9 0.2 fold.1
  24.0 0.1 collective-permute-start.6
  24.1 2.7 %collective-permute-start.7 = (bf16[128,128]{1,0:T(8,128)(2,1)S(1)}, bf16[128,128]{1,0:T(8,128)(2,1)S(1)}, u32[]{:S(2)}, u32[]{:S(2)}) collective-permute-start(bf16[128,128]{1,0:T(8,128)(2,1)S(1)} %get-tuple-element.35), channel_id=1, source_target_pairs={{0,13},{1,12},{2,15},{3,14},{4,9},{5,8},{6,11},{7,10},{8,5},{9,4},... | collective-permute-start | bytes 98312 | tf_op jit(solution)/shard_map/ppermute | solution.py:581
  26.8 0.5 %collective-permute-start.8 = (bf16[128,128]{1,0:T(8,128)(2,1)S(1)}, bf16[128,128]{1,0:T(8,128)(2,1)S(1)}, u32[]{:S(2)}, u32[]{:S(2)}) collective-permute-start(bf16[128,128]{1,0:T(8,128)(2,1)S(1)} %get-tuple-element.36), channel_id=1, source_target_pairs={{0,4},{1,5},{2,6},{3,7},{4,0},{5,1},{6,2},{7,3},{8,12},{9,13},{10,... | collective-permute-start | bytes 98312 | tf_op jit(solution)/shard_map/ppermute | solution.py:581
  27.3 1.4 %collective-permute-done.6.refs_0_ = bf16[128,128]{1,0:T(8,128)(2,1)S(1)} collective-permute-done((bf16[128,128]{1,0:T(8,128)(2,1)S(1)}, bf16[128,128]{1,0:T(8,128)(2,1)S(1)}, u32[]{:S(2)}, u32[]{:S(2)}) %collective-permute-start.6) | collective-permute-done | bytes 32800 | tf_op jit(solution)/shard_map/ppermute | solution.py:581
  28.7 0.8 %collective-permute-done.7.refs_1_ = bf16[128,128]{1,0:T(8,128)(2,1)S(1)} collective-permute-done((bf16[128,128]{1,0:T(8,128)(2,1)S(1)}, bf16[128,128]{1,0:T(8,128)(2,1)S(1)}, u32[]{:S(2)}, u32[]{:S(2)}) %collective-permute-start.7) | collective-permute-done | bytes 32800 | tf_op jit(solution)/shard_map/ppermute | solution.py:581
  29.4 1.9 %collective-permute-done.8.refs_2_ = bf16[128,128]{1,0:T(8,128)(2,1)S(1)} collective-permute-done((bf16[128,128]{1,0:T(8,128)(2,1)S(1)}, bf16[128,128]{1,0:T(8,128)(2,1)S(1)}, u32[]{:S(2)}, u32[]{:S(2)}) %collective-permute-start.8) | collective-permute-done | bytes 32800 | tf_op jit(solution)/shard_map/ppermute | solution.py:581
  31.4 1.3 %finish.1 = (f32[4,384]{1,0:T(4,128)}, f32[4,4,384]{2,1,0:T(4,128)}, f32[8,128]{1,0:T(8,128)S(1)}, f32[8,128]{1,0:T(8,128)S(1)}) custom-call(f32[120,128]{1,0:T(8,128)S(1)} %get-tuple-element.32.held, bf16[128,128]{1,0:T(8,128)(2,1)S(1)} %get-tuple-element.33.carried, bf16[128,128]{1,0:T(8,128)(2,1)S(1)} %collective-permute-done.6.refs_0_, ...), custom_call_target="tpu_custom_call" | custom-call | tf_op jit(solution)/shard_map/finish/pallas_call | solution.py:559
  32.7 0.1 collective-permute-start.9
  32.8 1.1 %collective-permute-done.9 = f32[8,128]{1,0:T(8,128)S(1)} collective-permute-done((f32[8,128]{1,0:T(8,128)S(1)}, f32[8,128]{1,0:T(8,128)S(1)}, u32[]{:S(2)}, u32[]{:S(2)}) %collective-permute-start.9) | collective-permute-done | bytes 4128 | tf_op jit(solution)/shard_map/ppermute | solution.py:581
  33.9 0.1 fusion
  34.0 0.6 %pad_maximum_fusion = f32[24,40]{1,0:T(8,128)} fusion(f32[8,40]{1,0:T(8,128)S(1)} %get-tuple-element.42, f32[8,40]{1,0:T(8,128)S(1)} %get-tuple-element.43, f32[8,40]{1,0:T(8,128)S(1)} %get-tuple-element.41), kind=kLoop, calls=%fused_computation.7 | loop fusion | flops 1920 | bytes 7680 | tf_op jit(solution)/shard_map/concatenate | solution.py:652
  (10 shorter events, 0.1 us)
Async XLA Ops:
  0.6 15.3 %copy-start = (bf16[384,4,2,256]{3,2,1,0:T(2,128)(2,1)S(1)}, bf16[384,4,2,256]{3,2,1,0:T(2,128)(2,1)}, u32[]{:S(2)}) copy-start(bf16[384,4,2,256]{3,2,1,0:T(2,128)(2,1)} %kernel.1) | copy-start | bytes 4718596
  2.3 12.0 %collective-permute-start.1 = (f32[24,128]{1,0:T(8,128)}, f32[24,128]{1,0:T(8,128)S(1)}, u32[]{:S(2)}, u32[]{:S(2)}) collective-permute-start(f32[24,128]{1,0:T(8,128)} %get-tuple-element.25), channel_id=1, source_target_pairs={{0,4},{1,5},{2,6},{3,7},{4,0},{5,1},{6,2},{7,3},{8,12},{9,13},{10,... | collective-permute-start | bytes 36872 | tf_op jit(solution)/shard_map/ppermute | solution.py:581
  5.3 9.0 %collective-permute-start.2 = (f32[24,128]{1,0:T(8,128)}, f32[24,128]{1,0:T(8,128)S(1)}, u32[]{:S(2)}, u32[]{:S(2)}) collective-permute-start(f32[24,128]{1,0:T(8,128)} %get-tuple-element.25), channel_id=1, source_target_pairs={{0,9},{1,8},{2,11},{3,10},{4,13},{5,12},{6,15},{7,14},{8,1},{9,0},... | collective-permute-start | bytes 36872 | tf_op jit(solution)/shard_map/ppermute | solution.py:581
  7.0 7.2 %collective-permute-start.3 = (f32[24,128]{1,0:T(8,128)}, f32[24,128]{1,0:T(8,128)S(1)}, u32[]{:S(2)}, u32[]{:S(2)}) collective-permute-start(f32[24,128]{1,0:T(8,128)} %get-tuple-element.25), channel_id=1, source_target_pairs={{0,13},{1,12},{2,15},{3,14},{4,9},{5,8},{6,11},{7,10},{8,5},{9,4},... | collective-permute-start | bytes 36872 | tf_op jit(solution)/shard_map/ppermute | solution.py:581
  7.4 0.9 %copy-start.1 = (s32[48,384]{1,0:T(8,128)S(1)}, s32[48,384]{1,0:T(8,128)}, u32[]{:S(2)}) copy-start(s32[48,384]{1,0:T(8,128)} %get-tuple-element.22.given) | copy-start | bytes 221188
  8.3 6.0 %copy-start.7 = (f32[24,128]{1,0:T(8,128)S(1)}, f32[24,128]{1,0:T(8,128)}, u32[]{:S(2)}) copy-start(f32[24,128]{1,0:T(8,128)} %get-tuple-element.25) | copy-start | bytes 36868
  8.3 7.6 %copy-start.6 = (f32[4,4,384]{2,1,0:T(4,128)S(1)}, f32[4,4,384]{2,1,0:T(4,128)}, u32[]{:S(2)}) copy-start(f32[4,4,384]{2,1,0:T(4,128)} %param.19) | copy-start | bytes 73732
  8.3 7.7 %copy-start.2 = (s32[48,384]{1,0:T(8,128)S(1)}, s32[48,384]{1,0:T(8,128)}, u32[]{:S(2)}) copy-start(s32[48,384]{1,0:T(8,128)} %get-tuple-element.22.given) | copy-start | bytes 221188
  8.3 7.7 %copy-start.3 = (f32[4,2,4,256]{3,2,1,0:T(4,128)S(1)}, f32[4,2,4,256]{3,2,1,0:T(4,128)}, u32[]{:S(2)}) copy-start(f32[4,2,4,256]{3,2,1,0:T(4,128)} %history.1) | copy-start | bytes 98308
  8.3 7.7 %copy-start.4 = (s32[384]{0:T(512)S(1)}, s32[384]{0:T(512)}, u32[]{:S(2)}) copy-start(s32[384]{0:T(512)} %population.3) | copy-start | bytes 4612
  8.3 10.3 %copy-start.5 = (f32[4,384]{1,0:T(4,128)S(1)}, f32[4,384]{1,0:T(4,128)}, u32[]{:S(2)}) copy-start(f32[4,384]{1,0:T(4,128)} %param.18) | copy-start | bytes 18436
  13.5 5.0 %collective-permute-start = (f32[24,56,128]{2,1,0:T(8,128)}, f32[24,56,128]{2,1,0:T(8,128)S(1)}, u32[]{:S(2)}, u32[]{:S(2)}) collective-permute-start(f32[24,56,128]{2,1,0:T(8,128)} %get-tuple-element.24), channel_id=1, source_target_pairs={{0,1},{1,0},{2,3},{3,2},{4,5},{5,4},{6,7},{7,6},{8,9},{9,8},{10,11... | collective-permute-start | bytes 2064392 | tf_op jit(solution)/shard_map/ppermute | solution.py:581
  14.3 4.2 %collective-permute-start.4 = (f32[112,128]{1,0:T(8,128)S(1)}, f32[112,128]{1,0:T(8,128)S(1)}, u32[]{:S(2)}, u32[]{:S(2)}) collective-permute-start(f32[112,128]{1,0:T(8,128)S(1)} %constant_dynamic-update-slice_fusion.near), channel_id=1, source_target_pairs={{0,2},{1,3},{2,0},{3,1},{4,6},{5,7},{6,4},{7,5},{8,10},{9,11},{10,... | collective-permute-start | bytes 172040 | tf_op jit(solution)/shard_map/ppermute | solution.py:581
  19.1 4.7 %collective-permute-start.5 = (bf16[416,128]{1,0:T(8,128)(2,1)S(1)}, bf16[416,128]{1,0:T(8,128)(2,1)S(1)}, u32[]{:S(2)}, u32[]{:S(2)}) collective-permute-start(bf16[416,128]{1,0:T(8,128)(2,1)S(1)} %get-tuple-element.30), channel_id=1, source_target_pairs={{0,2},{1,3},{2,0},{3,1},{4,6},{5,7},{6,4},{7,5},{8,10},{9,11},{10,... | collective-permute-start | bytes 319496 | tf_op jit(solution)/shard_map/ppermute | solution.py:581
  24.0 4.6 %collective-permute-start.6 = (bf16[128,128]{1,0:T(8,128)(2,1)S(1)}, bf16[128,128]{1,0:T(8,128)(2,1)S(1)}, u32[]{:S(2)}, u32[]{:S(2)}) collective-permute-start(bf16[128,128]{1,0:T(8,128)(2,1)S(1)} %get-tuple-element.34), channel_id=1, source_target_pairs={{0,9},{1,8},{2,11},{3,10},{4,13},{5,12},{6,15},{7,14},{8,1},{9,0},... | collective-permute-start | bytes 98312 | tf_op jit(solution)/shard_map/ppermute | solution.py:581
  24.1 5.3 %collective-permute-start.7 = (bf16[128,128]{1,0:T(8,128)(2,1)S(1)}, bf16[128,128]{1,0:T(8,128)(2,1)S(1)}, u32[]{:S(2)}, u32[]{:S(2)}) collective-permute-start(bf16[128,128]{1,0:T(8,128)(2,1)S(1)} %get-tuple-element.35), channel_id=1, source_target_pairs={{0,13},{1,12},{2,15},{3,14},{4,9},{5,8},{6,11},{7,10},{8,5},{9,4},... | collective-permute-start | bytes 98312 | tf_op jit(solution)/shard_map/ppermute | solution.py:581
  26.8 4.5 %collective-permute-start.8 = (bf16[128,128]{1,0:T(8,128)(2,1)S(1)}, bf16[128,128]{1,0:T(8,128)(2,1)S(1)}, u32[]{:S(2)}, u32[]{:S(2)}) collective-permute-start(bf16[128,128]{1,0:T(8,128)(2,1)S(1)} %get-tuple-element.36), channel_id=1, source_target_pairs={{0,4},{1,5},{2,6},{3,7},{4,0},{5,1},{6,2},{7,3},{8,12},{9,13},{10,... | collective-permute-start | bytes 98312 | tf_op jit(solution)/shard_map/ppermute | solution.py:581
  32.7 1.2 %collective-permute-start.9 = (f32[8,128]{1,0:T(8,128)S(1)}, f32[8,128]{1,0:T(8,128)S(1)}, u32[]{:S(2)}, u32[]{:S(2)}) collective-permute-start(f32[8,128]{1,0:T(8,128)S(1)} %get-tuple-element.40), channel_id=1, source_target_pairs={{0,1},{1,0},{2,3},{3,2},{4,5},{5,4},{6,7},{7,6},{8,9},{9,8},{10,11... | collective-permute-start | bytes 12296 | tf_op jit(solution)/shard_map/ppermute | solution.py:581

commit v7 on v6

--- a/solution.py
+++ b/solution.py
@@ -103,8 +103,8 @@
     return pl.pallas_call(
         functools.partial(facts_kernel, plan),
         out_shape=(
-            jax.ShapeDtypeStruct((plan.blocks * 8, 128), F32),
-            jax.ShapeDtypeStruct((rows, spikes.shape[2]), jnp.int32),
+            pltpu.VMEM((plan.blocks * 8, 128), F32),
+            pltpu.VMEM((rows, spikes.shape[2]), jnp.int32),
         ),
         in_specs=[VMEM] * 6,
         out_specs=(VMEM, VMEM),
@@ -184,9 +184,9 @@
             pltpu.SemaphoreType.DMA,
             pltpu.SemaphoreType.DMA((unit_count // chunk,)),
         ],
-        compiler_params=params(52),
+        compiler_params=params(24),
         name="payload",
-    )(given, weights)
+    )(given, pltpu.with_memory_space_constraint(weights, pltpu.HBM))
 
 
 def known_kernel(plan, given, population, history, kernel, out, reach, series, fresh, lags, sorted_):

time: 34.7 us -> 33.2 us (0.957)
  local copies, waits for them, and re-layouts: 1.04 us -> 0.15 us
  Pallas kernels: 11.1 us -> 10.5 us
    unnamed x21 -> x15, local copies, waits for them, and re-layouts: 0.93 us -> 0.04 us
    pallas_call x1, Pallas kernels: 1.63 us -> 1 us  [facts_of(): pl.pallas_call(functools.partial(facts_kernel, plan), out_shape=(pltpu.VM...]
where the time goes in v7:
time: 33.2 us; the launch traced here: 33.1 us
  starting transfers between devices  12.3 us (37%)
  Pallas kernels  10.5 us (32%)
  waiting for transfers between devices  8.72 us (26%)
  between operations  0.8 us (2%)
  other arithmetic  0.61 us (2%)
    ppermute x10, starting transfers between devices, swap(): lax.ppermute(values, 'area', [(i, i ^ bit) for i in range(area_count)])  12.3 us
    ppermute x10, waiting for transfers between devices, swap(): lax.ppermute(values, 'area', [(i, i ^ bit) for i in range(area_count)])  8.72 us
    pallas_call x1, Pallas kernels, payload_sums(): pl.pallas_call(functools.partial(payload_kernel, plan), out_shape=(half,...  5.19 us
    pallas_call x1, Pallas kernels, known_lfp(): pl.pallas_call(functools.partial(known_kernel, plan), out_shape=(jax.Shap...  2.23 us
    pallas_call x1, Pallas kernels, finish(): pl.pallas_call(functools.partial(finish_kernel, plan), out_shape=(jax.Sha...  1.32 us
    pallas_call x1, Pallas kernels, facts_of(): pl.pallas_call(functools.partial(facts_kernel, plan), out_shape=(pltpu.VM...  1 us
  transfers between devices with their start and end apart: 10, of which 6 were waited for; matrix products, arithmetic and copies ran while one was open for 0% of the time, Pallas kernels for 22%

profile of v7, /device:TPU:0, one launch (start us, length us, event | category | flops | bytes accessed | tf_op | source)
XLA Modules:
  0.0 33.1 jit_solution(16329792111861658838)
XLA Ops:
  0.6 0.0 copy-start.2
  0.6 0.0 copy-start.4
  0.7 0.0 copy-start.1
  0.7 0.0 copy-start
  0.7 0.0 copy-start.3
  0.7 1.0 %facts.1 = (f32[24,128]{1,0:T(8,128)S(1)}, s32[48,384]{1,0:T(8,128)S(1)}) custom-call(s32[10,4,384]{2,1,0:T(4,128)} %bitcast.13, f32[384]{0:T(512)} %leak.1, s32[384]{0:T(512)} %population.3, s32[96]{0:T(128)} %bitcast.15, s32[96]{0:T(128)} %target_block.1, s32[96]{0:T(128)} %delay_slot.1), custom_call_target="tpu_custom_call" | custom-call | tf_op jit(solution)/shard_map/facts/pallas_call | solution.py:103
  1.7 3.1 %collective-permute-start.1 = (f32[24,128]{1,0:T(8,128)S(1)}, f32[24,128]{1,0:T(8,128)S(1)}, u32[]{:S(2)}, u32[]{:S(2)}) collective-permute-start(f32[24,128]{1,0:T(8,128)S(1)} %get-tuple-element.25), channel_id=1, source_target_pairs={{0,4},{1,5},{2,6},{3,7},{4,0},{5,1},{6,2},{7,3},{8,12},{9,13},{10,... | collective-permute-start | bytes 36872 | tf_op jit(solution)/shard_map/ppermute | solution.py:581
  4.8 1.7 %collective-permute-start.2 = (f32[24,128]{1,0:T(8,128)S(1)}, f32[24,128]{1,0:T(8,128)S(1)}, u32[]{:S(2)}, u32[]{:S(2)}) collective-permute-start(f32[24,128]{1,0:T(8,128)S(1)} %get-tuple-element.25), channel_id=1, source_target_pairs={{0,9},{1,8},{2,11},{3,10},{4,13},{5,12},{6,15},{7,14},{8,1},{9,0},... | collective-permute-start | bytes 36872 | tf_op jit(solution)/shard_map/ppermute | solution.py:581
  6.5 0.4 %collective-permute-start.3 = (f32[24,128]{1,0:T(8,128)S(1)}, f32[24,128]{1,0:T(8,128)S(1)}, u32[]{:S(2)}, u32[]{:S(2)}) collective-permute-start(f32[24,128]{1,0:T(8,128)S(1)} %get-tuple-element.25), channel_id=1, source_target_pairs={{0,13},{1,12},{2,15},{3,14},{4,9},{5,8},{6,11},{7,10},{8,5},{9,4},... | collective-permute-start | bytes 36872 | tf_op jit(solution)/shard_map/ppermute | solution.py:581
  6.9 5.2 %payload.1 = (f32[24,56,128]{2,1,0:T(8,128)S(1)}, f32[24,56,128]{2,1,0:T(8,128)}, f32[8,128]{1,0:T(8,128)S(1)}) custom-call(s32[48,384]{1,0:T(8,128)S(1)} %get-tuple-element.22.given, bf16[96,384,128]{2,1,0:T(8,128)(2,1)} %weights.1), custom_call_target="tpu_custom_call" | custom-call | tf_op jit(solution)/shard_map/payload/pallas_call | solution.py:173
  12.1 0.6 %collective-permute-start = (f32[24,56,128]{2,1,0:T(8,128)}, f32[24,56,128]{2,1,0:T(8,128)S(1)}, u32[]{:S(2)}, u32[]{:S(2)}) collective-permute-start(f32[24,56,128]{2,1,0:T(8,128)} %get-tuple-element.24), channel_id=1, source_target_pairs={{0,1},{1,0},{2,3},{3,2},{4,5},{5,4},{6,7},{7,6},{8,9},{9,8},{10,11... | collective-permute-start | bytes 2064392 | tf_op jit(solution)/shard_map/ppermute | solution.py:581
  12.8 0.0 collective-permute-done.1
  12.8 0.0 collective-permute-done.2
  12.8 0.0 collective-permute-done.3
  12.8 1.6 %collective-permute-start.4 = (f32[112,128]{1,0:T(8,128)S(1)}, f32[112,128]{1,0:T(8,128)S(1)}, u32[]{:S(2)}, u32[]{:S(2)}) collective-permute-start(f32[112,128]{1,0:T(8,128)S(1)} %constant_dynamic-update-slice_fusion.near), channel_id=1, source_target_pairs={{0,2},{1,3},{2,0},{3,1},{4,6},{5,7},{6,4},{7,5},{8,10},{9,11},{10,... | collective-permute-start | bytes 172040 | tf_op jit(solution)/shard_map/ppermute | solution.py:581
  14.4 0.0 copy-done.4
  14.4 0.0 copy-done.2
  14.4 0.0 copy-done.1
  14.5 0.0 copy-done
  14.5 2.2 %known_lfp.1 = (f32[384,128]{1,0:T(8,128)S(1)}, f32[16,8,128]{2,1,0:T(8,128)S(1)}) custom-call(s32[48,384]{1,0:T(8,128)S(1)} %get-tuple-element.22.given, s32[384]{0:T(512)S(1)} %copy-done.2, f32[4,2,4,256]{3,2,1,0:T(4,128)S(1)} %copy-done.1, bf16[384,4,2,256]{3,2,1,0:T(2,128)(2,1)S(1)} %copy-done), custom_call_target="tpu_custom_call" | custom-call | tf_op jit(solution)/shard_map/known_lfp/pallas_call | solution.py:266
  16.7 0.4 %collective-permute-done.4.far = f32[112,128]{1,0:T(8,128)S(1)} collective-permute-done((f32[112,128]{1,0:T(8,128)S(1)}, f32[112,128]{1,0:T(8,128)S(1)}, u32[]{:S(2)}, u32[]{:S(2)}) %collective-permute-start.4) | collective-permute-done | bytes 57376 | tf_op jit(solution)/shard_map/ppermute | solution.py:581
  17.1 0.0 collective-permute-done.got
  17.1 0.0 copy-done.3
  17.1 0.6 %compress.1 = (f32[360,128]{1,0:T(8,128)S(1)}, bf16[416,128]{1,0:T(8,128)(2,1)S(1)}, bf16[128,128]{1,0:T(8,128)(2,1)S(1)}) custom-call(f32[24,56,128]{2,1,0:T(8,128)S(1)} %get-tuple-element.23.mine, f32[24,56,128]{2,1,0:T(8,128)S(1)} %collective-permute-done.got, f32[112,128]{1,0:T(8,128)S(1)} %constant_dynamic-update-slice_fusion.near, ...), custom_call_target="tpu_custom_call" | custom-call | tf_op jit(solution)/shard_map/compress/pallas_call | solution.py:395
  17.6 1.5 %collective-permute-start.5 = (bf16[416,128]{1,0:T(8,128)(2,1)S(1)}, bf16[416,128]{1,0:T(8,128)(2,1)S(1)}, u32[]{:S(2)}, u32[]{:S(2)}) collective-permute-start(bf16[416,128]{1,0:T(8,128)(2,1)S(1)} %get-tuple-element.30), channel_id=1, source_target_pairs={{0,2},{1,3},{2,0},{3,1},{4,6},{5,7},{6,4},{7,5},{8,10},{9,11},{10,... | collective-permute-start | bytes 319496 | tf_op jit(solution)/shard_map/ppermute | solution.py:581
  19.2 3.2 %collective-permute-done.5.got = bf16[416,128]{1,0:T(8,128)(2,1)S(1)} collective-permute-done((bf16[416,128]{1,0:T(8,128)(2,1)S(1)}, bf16[416,128]{1,0:T(8,128)(2,1)S(1)}, u32[]{:S(2)}, u32[]{:S(2)}) %collective-permute-start.5) | collective-permute-done | bytes 106528 | tf_op jit(solution)/shard_map/ppermute | solution.py:581
  22.4 0.2 fold.1
  22.6 0.1 collective-permute-start.6
  22.6 2.7 %collective-permute-start.7 = (bf16[128,128]{1,0:T(8,128)(2,1)S(1)}, bf16[128,128]{1,0:T(8,128)(2,1)S(1)}, u32[]{:S(2)}, u32[]{:S(2)}) collective-permute-start(bf16[128,128]{1,0:T(8,128)(2,1)S(1)} %get-tuple-element.35), channel_id=1, source_target_pairs={{0,13},{1,12},{2,15},{3,14},{4,9},{5,8},{6,11},{7,10},{8,5},{9,4},... | collective-permute-start | bytes 98312 | tf_op jit(solution)/shard_map/ppermute | solution.py:581
  25.4 0.5 %collective-permute-start.8 = (bf16[128,128]{1,0:T(8,128)(2,1)S(1)}, bf16[128,128]{1,0:T(8,128)(2,1)S(1)}, u32[]{:S(2)}, u32[]{:S(2)}) collective-permute-start(bf16[128,128]{1,0:T(8,128)(2,1)S(1)} %get-tuple-element.36), channel_id=1, source_target_pairs={{0,4},{1,5},{2,6},{3,7},{4,0},{5,1},{6,2},{7,3},{8,12},{9,13},{10,... | collective-permute-start | bytes 98312 | tf_op jit(solution)/shard_map/ppermute | solution.py:581
  25.8 1.4 %collective-permute-done.6.refs_0_ = bf16[128,128]{1,0:T(8,128)(2,1)S(1)} collective-permute-done((bf16[128,128]{1,0:T(8,128)(2,1)S(1)}, bf16[128,128]{1,0:T(8,128)(2,1)S(1)}, u32[]{:S(2)}, u32[]{:S(2)}) %collective-permute-start.6) | collective-permute-done | bytes 32800 | tf_op jit(solution)/shard_map/ppermute | solution.py:581
  27.2 0.8 %collective-permute-done.7.refs_1_ = bf16[128,128]{1,0:T(8,128)(2,1)S(1)} collective-permute-done((bf16[128,128]{1,0:T(8,128)(2,1)S(1)}, bf16[128,128]{1,0:T(8,128)(2,1)S(1)}, u32[]{:S(2)}, u32[]{:S(2)}) %collective-permute-start.7) | collective-permute-done | bytes 32800 | tf_op jit(solution)/shard_map/ppermute | solution.py:581
  28.0 1.9 %collective-permute-done.8.refs_2_ = bf16[128,128]{1,0:T(8,128)(2,1)S(1)} collective-permute-done((bf16[128,128]{1,0:T(8,128)(2,1)S(1)}, bf16[128,128]{1,0:T(8,128)(2,1)S(1)}, u32[]{:S(2)}, u32[]{:S(2)}) %collective-permute-start.8) | collective-permute-done | bytes 32800 | tf_op jit(solution)/shard_map/ppermute | solution.py:581
  29.9 1.3 %finish.1 = (f32[4,384]{1,0:T(4,128)}, f32[4,4,384]{2,1,0:T(4,128)}, f32[8,128]{1,0:T(8,128)S(1)}, f32[8,128]{1,0:T(8,128)S(1)}) custom-call(f32[120,128]{1,0:T(8,128)S(1)} %get-tuple-element.32.held, bf16[128,128]{1,0:T(8,128)(2,1)S(1)} %get-tuple-element.33.carried, bf16[128,128]{1,0:T(8,128)(2,1)S(1)} %collective-permute-done.6.refs_0_, ...), custom_call_target="tpu_custom_call" | custom-call | tf_op jit(solution)/shard_map/finish/pallas_call | solution.py:559
  31.2 0.1 collective-permute-start.9
  31.3 1.1 %collective-permute-done.9 = f32[8,128]{1,0:T(8,128)S(1)} collective-permute-done((f32[8,128]{1,0:T(8,128)S(1)}, f32[8,128]{1,0:T(8,128)S(1)}, u32[]{:S(2)}, u32[]{:S(2)}) %collective-permute-start.9) | collective-permute-done | bytes 4128 | tf_op jit(solution)/shard_map/ppermute | solution.py:581
  32.4 0.1 fusion
  32.5 0.6 %pad_maximum_fusion = f32[24,40]{1,0:T(8,128)} fusion(f32[8,40]{1,0:T(8,128)S(1)} %get-tuple-element.42, f32[8,40]{1,0:T(8,128)S(1)} %get-tuple-element.43, f32[8,40]{1,0:T(8,128)S(1)} %get-tuple-element.41), kind=kLoop, calls=%fused_computation.7 | loop fusion | flops 1920 | bytes 7680 | tf_op jit(solution)/shard_map/concatenate | solution.py:652
  (10 shorter events, 0.1 us)
Async XLA Ops:
  0.6 13.8 %copy-start.2 = (s32[384]{0:T(512)S(1)}, s32[384]{0:T(512)}, u32[]{:S(2)}) copy-start(s32[384]{0:T(512)} %population.3) | copy-start | bytes 4612
  0.6 13.7 %copy-start.4 = (f32[4,4,384]{2,1,0:T(4,128)S(1)}, f32[4,4,384]{2,1,0:T(4,128)}, u32[]{:S(2)}) copy-start(f32[4,4,384]{2,1,0:T(4,128)} %param.19) | copy-start | bytes 73732
  0.7 13.8 %copy-start.1 = (f32[4,2,4,256]{3,2,1,0:T(4,128)S(1)}, f32[4,2,4,256]{3,2,1,0:T(4,128)}, u32[]{:S(2)}) copy-start(f32[4,2,4,256]{3,2,1,0:T(4,128)} %history.1) | copy-start | bytes 98308
  0.7 13.8 %copy-start = (bf16[384,4,2,256]{3,2,1,0:T(2,128)(2,1)S(1)}, bf16[384,4,2,256]{3,2,1,0:T(2,128)(2,1)}, u32[]{:S(2)}) copy-start(bf16[384,4,2,256]{3,2,1,0:T(2,128)(2,1)} %kernel.1) | copy-start | bytes 4718596
  0.7 16.4 %copy-start.3 = (f32[4,384]{1,0:T(4,128)S(1)}, f32[4,384]{1,0:T(4,128)}, u32[]{:S(2)}) copy-start(f32[4,384]{1,0:T(4,128)} %param.18) | copy-start | bytes 18436
  1.7 11.1 %collective-permute-start.1 = (f32[24,128]{1,0:T(8,128)S(1)}, f32[24,128]{1,0:T(8,128)S(1)}, u32[]{:S(2)}, u32[]{:S(2)}) collective-permute-start(f32[24,128]{1,0:T(8,128)S(1)} %get-tuple-element.25), channel_id=1, source_target_pairs={{0,4},{1,5},{2,6},{3,7},{4,0},{5,1},{6,2},{7,3},{8,12},{9,13},{10,... | collective-permute-start | bytes 36872 | tf_op jit(solution)/shard_map/ppermute | solution.py:581
  4.8 8.0 %collective-permute-start.2 = (f32[24,128]{1,0:T(8,128)S(1)}, f32[24,128]{1,0:T(8,128)S(1)}, u32[]{:S(2)}, u32[]{:S(2)}) collective-permute-start(f32[24,128]{1,0:T(8,128)S(1)} %get-tuple-element.25), channel_id=1, source_target_pairs={{0,9},{1,8},{2,11},{3,10},{4,13},{5,12},{6,15},{7,14},{8,1},{9,0},... | collective-permute-start | bytes 36872 | tf_op jit(solution)/shard_map/ppermute | solution.py:581
  6.5 6.3 %collective-permute-start.3 = (f32[24,128]{1,0:T(8,128)S(1)}, f32[24,128]{1,0:T(8,128)S(1)}, u32[]{:S(2)}, u32[]{:S(2)}) collective-permute-start(f32[24,128]{1,0:T(8,128)S(1)} %get-tuple-element.25), channel_id=1, source_target_pairs={{0,13},{1,12},{2,15},{3,14},{4,9},{5,8},{6,11},{7,10},{8,5},{9,4},... | collective-permute-start | bytes 36872 | tf_op jit(solution)/shard_map/ppermute | solution.py:581
  12.1 4.9 %collective-permute-start = (f32[24,56,128]{2,1,0:T(8,128)}, f32[24,56,128]{2,1,0:T(8,128)S(1)}, u32[]{:S(2)}, u32[]{:S(2)}) collective-permute-start(f32[24,56,128]{2,1,0:T(8,128)} %get-tuple-element.24), channel_id=1, source_target_pairs={{0,1},{1,0},{2,3},{3,2},{4,5},{5,4},{6,7},{7,6},{8,9},{9,8},{10,11... | collective-permute-start | bytes 2064392 | tf_op jit(solution)/shard_map/ppermute | solution.py:581
  12.8 4.2 %collective-permute-start.4 = (f32[112,128]{1,0:T(8,128)S(1)}, f32[112,128]{1,0:T(8,128)S(1)}, u32[]{:S(2)}, u32[]{:S(2)}) collective-permute-start(f32[112,128]{1,0:T(8,128)S(1)} %constant_dynamic-update-slice_fusion.near), channel_id=1, source_target_pairs={{0,2},{1,3},{2,0},{3,1},{4,6},{5,7},{6,4},{7,5},{8,10},{9,11},{10,... | collective-permute-start | bytes 172040 | tf_op jit(solution)/shard_map/ppermute | solution.py:581
  17.6 4.7 %collective-permute-start.5 = (bf16[416,128]{1,0:T(8,128)(2,1)S(1)}, bf16[416,128]{1,0:T(8,128)(2,1)S(1)}, u32[]{:S(2)}, u32[]{:S(2)}) collective-permute-start(bf16[416,128]{1,0:T(8,128)(2,1)S(1)} %get-tuple-element.30), channel_id=1, source_target_pairs={{0,2},{1,3},{2,0},{3,1},{4,6},{5,7},{6,4},{7,5},{8,10},{9,11},{10,... | collective-permute-start | bytes 319496 | tf_op jit(solution)/shard_map/ppermute | solution.py:581
  22.6 4.6 %collective-permute-start.6 = (bf16[128,128]{1,0:T(8,128)(2,1)S(1)}, bf16[128,128]{1,0:T(8,128)(2,1)S(1)}, u32[]{:S(2)}, u32[]{:S(2)}) collective-permute-start(bf16[128,128]{1,0:T(8,128)(2,1)S(1)} %get-tuple-element.34), channel_id=1, source_target_pairs={{0,9},{1,8},{2,11},{3,10},{4,13},{5,12},{6,15},{7,14},{8,1},{9,0},... | collective-permute-start | bytes 98312 | tf_op jit(solution)/shard_map/ppermute | solution.py:581
  22.6 5.3 %collective-permute-start.7 = (bf16[128,128]{1,0:T(8,128)(2,1)S(1)}, bf16[128,128]{1,0:T(8,128)(2,1)S(1)}, u32[]{:S(2)}, u32[]{:S(2)}) collective-permute-start(bf16[128,128]{1,0:T(8,128)(2,1)S(1)} %get-tuple-element.35), channel_id=1, source_target_pairs={{0,13},{1,12},{2,15},{3,14},{4,9},{5,8},{6,11},{7,10},{8,5},{9,4},... | collective-permute-start | bytes 98312 | tf_op jit(solution)/shard_map/ppermute | solution.py:581
  25.4 4.5 %collective-permute-start.8 = (bf16[128,128]{1,0:T(8,128)(2,1)S(1)}, bf16[128,128]{1,0:T(8,128)(2,1)S(1)}, u32[]{:S(2)}, u32[]{:S(2)}) collective-permute-start(bf16[128,128]{1,0:T(8,128)(2,1)S(1)} %get-tuple-element.36), channel_id=1, source_target_pairs={{0,4},{1,5},{2,6},{3,7},{4,0},{5,1},{6,2},{7,3},{8,12},{9,13},{10,... | collective-permute-start | bytes 98312 | tf_op jit(solution)/shard_map/ppermute | solution.py:581
  31.2 1.2 %collective-permute-start.9 = (f32[8,128]{1,0:T(8,128)S(1)}, f32[8,128]{1,0:T(8,128)S(1)}, u32[]{:S(2)}, u32[]{:S(2)}) collective-permute-start(f32[8,128]{1,0:T(8,128)S(1)} %get-tuple-element.40), channel_id=1, source_target_pairs={{0,1},{1,0},{2,3},{3,2},{4,5},{5,4},{6,7},{7,6},{8,9},{9,8},{10,11... | collective-permute-start | bytes 12296 | tf_op jit(solution)/shard_map/ppermute | solution.py:581

commit v8 on v7

--- a/solution.py
+++ b/solution.py
@@ -10,6 +10,7 @@
 BF16, F32 = jnp.bfloat16, jnp.float32
 PAD = 112
 LATE = (2, 3, 1)
+RING = (1, 2, 3)
 VMEM = pl.BlockSpec(memory_space=pltpu.VMEM)
 HBM = pl.BlockSpec(memory_space=pltpu.HBM)
 NT = (((1,), (1,)), ((), ()))
@@ -61,7 +62,28 @@
         self.last = up(self.main + self.packed, 16)
 
     def mask(self, lane):
-        return (2 * lane) ^ (lane >> self.top)
+        return (2 * lane) ^ ((lane >> self.top) ^ (lane >> (self.top - 1) & 1))
+
+    def quarter(self, device):
+        return (device >> 1) // (self.lanes // 4)
+
+    def ring(self, shift):
+        pairs = []
+        for device in range(self.area_count):
+            here = self.quarter(device)
+            apart = here ^ (here + shift) % 4
+            pairs.append((device, device ^ self.mask(apart * (self.lanes // 4))))
+        return pairs
+
+    def ring_place(self, pair, me):
+        size = self.lanes // 8
+        apart, rest = pair // size, pair % size
+        turned = (apart % 2 == 1) & (self.quarter(me) % 2 == 0)
+        shift = jnp.where(turned, 4 - apart, apart)
+        place = jnp.int32(0)
+        for index, value in enumerate(RING, 1):
+            place = jnp.where(shift == value, index, place)
+        return place * size + rest
 
     def keep(self, slots):
         rows = slots * self.held + self.tiles * self.signal
@@ -155,7 +177,7 @@
         for unit, value in zip(units, values):
             device = lax.bitwise_xor(codes[0, unit], me)
             lane = lax.shift_right_logical(device, 1)
-            bit = lax.bitwise_and(lax.bitwise_xor(device, lane >> plan.top), 1)
+            bit = lax.bitwise_and(device ^ (lane >> plan.top) ^ (lane >> (plan.top - 1)), 1)
             place = bit * half + lane * blocks + codes[1, unit]
             total[place] += value
         return 0
@@ -314,6 +336,7 @@
     owner = lax.broadcasted_iota(jnp.int32, (plan.signal_lanes, 128), 0).astype(F32)
 
     def pair(index, _):
+        source = plan.ring_place(index, me)
         sums = jnp.zeros((2 * plan.signal, plan.signal_lanes), F32)
         for bit in range(2):
             lane = 2 * index + bit
@@ -325,7 +348,7 @@
                 arriving = mine[lane * blocks + block] + got[lane * blocks + block]
                 early = arriving[0 : trials * delays] + own * cycle[block]
                 arriving = jnp.concatenate([early, arriving[trials * delays :]], axis=0)
-                spot = pl.multiple_of((index * blocks + block) * 8, 8)
+                spot = pl.multiple_of((source * blocks + block) * 8, 8)
                 facts = (far if bit else near)[pl.ds(spot, 8)]
                 last = facts[0:trials]
                 leak = facts[trials : trials + 1]
@@ -471,30 +494,11 @@
     )(held, got, carried)
 
 
-def finish_kernel(plan, held, carried, *refs):
-    gots, (membrane, cycle, own, other, mixed, reach, late, parts) = refs[:3], refs[3:]
-    trials, steps, delays = plan.trials, plan.steps, plan.delays
+def fresh_lfp(plan, core, channels, signal, carried, gots, mixed, reach, late):
+    steps, pops = plan.steps, plan.pops
     taps = 2 * plan.taps
-    rows = held[0 : plan.held]
-    main, channels = rows[: plan.main_up], rows[plan.main_up :]
-    tail = held[plan.held :]
-    parts[0 : plan.main] = main[: plan.main]
-    for got in gots:
-        arrived = got[0 : plan.last].astype(F32)
-        parts[0 : plan.main] += arrived[: plan.main]
-        channels = channels + got[plan.last : plan.last + 16].astype(F32)
-        tail = tail + unpack_signal(plan, arrived[plan.main : plan.main + plan.packed])
-    for block in range(plan.blocks):
-        lanes = slice(block * 128, block * 128 + 128)
-        base = block * plan.each
-        membrane[:, lanes] = parts[base : base + trials]
-        for delay in range(delays):
-            spot = base + trials * (1 + delay)
-            cycle[:, delay, lanes] = parts[spot : spot + trials]
-
     me = lax.shift_right_logical(lax.axis_index("area"), 1)
     span = plan.lanes // 4
-    pops, wide = plan.pops, plan.taps_lanes // 128
     for lane in range(plan.lanes):
         far, near = divmod(lane, span)
         if far:
@@ -504,13 +508,46 @@
             slot = carried[lane * taps : (lane + 1) * taps]
         slot = slot.astype(F32)
         spot = lax.bitwise_xor(me, lane)
-        for core in range(2):
-            for tile in range(wide):
-                top = core * plan.taps + tile * pops
-                mixed[core, spot, 0:pops, tile * 128 : tile * 128 + 128] = slot[top : top + pops]
-    for core in range(2):
-        for lane in range(plan.lanes):
-            reach[core, lane * pops : (lane + 1) * pops] = mixed[core, lane, 0:pops]
+        for tile in range(plan.taps_lanes // 128):
+            top = core * plan.taps + tile * pops
+            mixed[spot, 0:pops, tile * 128 : tile * 128 + 128] = slot[top : top + pops]
+    for lane in range(plan.lanes):
+        reach[lane * pops : (lane + 1) * pops] = mixed[lane, 0:pops]
+    products = None
+    for tile in range(plan.tiles):
+        right = reach[tile * 128 : tile * 128 + plan.tile].astype(BF16)
+        one = dot(signal[tile][:, : plan.tile], right)
+        products = one if products is None else products + one
+    step_of = lax.broadcasted_iota(jnp.int32, (plan.width, 128), 0) % steps
+    value = jnp.zeros((plan.width, 128), F32)
+    width = products.shape[1]
+    for lag in range(1, steps):
+        moved = products
+        if lag > 1:
+            moved = pltpu.roll(products, width - (lag - 1) * plan.share, 1)
+        moved = pltpu.roll(moved[:, 0:128], lag, 0)
+        value = value + jnp.where(step_of >= lag, moved, 0.0)
+    late[...] = jnp.zeros_like(late)
+    late[0 : plan.width] = value
+    fresh = jnp.transpose(late[...])
+    lane = lax.broadcasted_iota(jnp.int32, (8, 128), 1)
+    for group in range(plan.groups):
+        piece = jnp.where(lane < plan.width, fresh[group * 8 : group * 8 + 8], 0.0)
+        if group:
+            piece = pltpu.roll(piece, group * plan.width, 1)
+        channels = channels + piece
+    return channels
+
+
+def other_kernel(plan, held, carried, *refs):
+    gots, (other, signal_out, mixed, reach, late) = refs[:3], refs[3:]
+    trials, steps = plan.trials, plan.steps
+    channels = held[plan.main_up + 8 : plan.main_up + 16]
+    tail = held[plan.held :]
+    for got in gots:
+        channels = channels + got[plan.last : plan.last + 16].astype(F32)[8:]
+        arrived = got[0 : plan.last].astype(F32)
+        tail = tail + unpack_signal(plan, arrived[plan.main : plan.main + plan.packed])
     new = lax.broadcasted_iota(jnp.int32, (plan.width, plan.signal), 0)
     old = lax.broadcasted_iota(jnp.int32, (plan.width, plan.signal), 1)
     order = (old == (new % steps) * trials + new // steps).astype(F32).astype(BF16)
@@ -519,62 +556,71 @@
         dot(order, signal[tile * plan.signal : (tile + 1) * plan.signal]).astype(BF16)
         for tile in range(plan.tiles)
     ]
-    step_of = lax.broadcasted_iota(jnp.int32, (plan.width, 128), 0) % steps
-    late[...] = jnp.zeros_like(late)
-    sums = []
-    for core in range(2):
-        products = None
-        for tile in range(plan.tiles):
-            right = reach[core, tile * 128 : tile * 128 + plan.tile].astype(BF16)
-            one = dot(signal[tile][:, : plan.tile], right)
-            products = one if products is None else products + one
-        value = jnp.zeros((plan.width, 128), F32)
-        width = products.shape[1]
-        for lag in range(1, steps):
-            moved = products
-            if lag > 1:
-                moved = pltpu.roll(products, width - (lag - 1) * plan.share, 1)
-            moved = pltpu.roll(moved[:, 0:128], lag, 0)
-            value = value + jnp.where(step_of >= lag, moved, 0.0)
-        sums.append(value)
-    lane = lax.broadcasted_iota(jnp.int32, (plan.width, 128), 1)
-    late[0 : plan.width] = jnp.where(lane < 64, sums[0], pltpu.roll(sums[1], 64, 1))
-    fresh = jnp.transpose(late[...])
-    lane = lax.broadcasted_iota(jnp.int32, (8, 128), 1)
-    row = lax.broadcasted_iota(jnp.int32, (8, 128), 0)
-    for core, out in enumerate((own, other)):
-        value = channels[core * 8 : core * 8 + 8]
-        for group in range(plan.groups):
-            piece = fresh[core * 64 + group * 8 : core * 64 + group * 8 + 8]
-            piece = jnp.where(lane < plan.width, piece, 0.0)
-            if group:
-                piece = pltpu.roll(piece, group * plan.width, 1)
-            value = value + piece
-        out[...] = value
-
-
-def finish(plan, neurons, held, carried, gots):
+    for tile in range(plan.tiles):
+        signal_out[tile * plan.width : (tile + 1) * plan.width] = signal[tile].astype(F32)
+    other[...] = fresh_lfp(plan, 1, channels, signal, carried, gots, mixed, reach, late)
+
+
+def own_kernel(plan, held, carried, signal_in, *refs):
+    gots, (membrane, cycle, own, mixed, reach, late, parts) = refs[:3], refs[3:]
     trials, delays = plan.trials, plan.delays
-    part = jax.ShapeDtypeStruct((8, 128), F32)
+    channels = held[plan.main_up : plan.main_up + 8]
+    parts[0 : plan.main] = held[0 : plan.main]
+    for got in gots:
+        channels = channels + got[plan.last : plan.last + 16].astype(F32)[:8]
+        parts[0 : plan.main] += got[0 : plan.last].astype(F32)[: plan.main]
+    for block in range(plan.blocks):
+        lanes = slice(block * 128, block * 128 + 128)
+        base = block * plan.each
+        membrane[:, lanes] = parts[base : base + trials]
+        for delay in range(delays):
+            spot = base + trials * (1 + delay)
+            cycle[:, delay, lanes] = parts[spot : spot + trials]
+    signal = [
+        signal_in[tile * plan.width : (tile + 1) * plan.width].astype(BF16)
+        for tile in range(plan.tiles)
+    ]
+    own[...] = fresh_lfp(plan, 0, channels, signal, carried, gots, mixed, reach, late)
+
+
+def taps_scratch(plan):
+    return [
+        pltpu.VMEM((plan.lanes, 8, plan.taps_lanes), F32),
+        pltpu.VMEM((plan.signal_lanes, plan.taps_lanes), F32),
+        pltpu.VMEM((128, 128), F32),
+    ]
+
+
+def finish_other(plan, held, carried, gots):
     return pl.pallas_call(
-        functools.partial(finish_kernel, plan),
+        functools.partial(other_kernel, plan),
+        out_shape=(
+            jax.ShapeDtypeStruct((8, 128), F32),
+            jax.ShapeDtypeStruct((plan.tiles * plan.width, 128), F32),
+        ),
+        in_specs=[VMEM] * (2 + len(gots)),
+        out_specs=(VMEM,) * 2,
+        scratch_shapes=taps_scratch(plan),
+        compiler_params=params(16),
+        name="finish_other",
+    )(held, carried, *gots)
+
+
+def finish_own(plan, neurons, held, carried, signal, gots):
+    trials, delays = plan.trials, plan.delays
+    return pl.pallas_call(
+        functools.partial(own_kernel, plan),
         out_shape=(
             jax.ShapeDtypeStruct((trials, neurons), F32),
             jax.ShapeDtypeStruct((trials, delays, neurons), F32),
-            part,
-            part,
+            jax.ShapeDtypeStruct((8, 128), F32),
         ),
-        in_specs=[VMEM] * (2 + len(gots)),
-        out_specs=(VMEM,) * 4,
-        scratch_shapes=[
-            pltpu.VMEM((2, plan.lanes, 8, plan.taps_lanes), F32),
-            pltpu.VMEM((2, plan.signal_lanes, plan.taps_lanes), F32),
-            pltpu.VMEM((128, 128), F32),
-            pltpu.VMEM((plan.main_up, 128), F32),
-        ],
+        in_specs=[VMEM] * (3 + len(gots)),
+        out_specs=(VMEM,) * 3,
+        scratch_shapes=taps_scratch(plan) + [pltpu.VMEM((plan.main_up, 128), F32)],
         compiler_params=params(16),
-        name="finish",
-    )(held, carried, *gots)
+        name="finish_own",
+    )(held, carried, signal, *gots)
 
 
 def swap(values, bit, area_count):
@@ -610,8 +656,7 @@
         plan, spikes, leak_rate, population, destination[:, 0], target_block, delay_slot
     )
     size = facts.shape[0]
-    came = {index: swap(facts, plan.mask(index * quarter), area_count) for index in (1, 2, 3)}
-    facts = [facts] + [came[index] for index in (1, 2, 3)]
+    facts = [facts] + [lax.ppermute(facts, "area", plan.ring(shift)) for shift in RING]
     mine, goes, token = payload_sums(plan, given, weights)
     got = swap(goes, 1, area_count)
     blank = jnp.zeros((max(0, PAD - 4 * size - token.shape[0]), 128), F32)
@@ -645,8 +690,10 @@
     gots = [
         swap(send, plan.mask(index * quarter), area_count) for send, index in zip(sends, LATE)
     ]
-    membrane, cycle_out, own, other = finish(plan, neurons, keep, carried, gots)
-    lfp = own + swap(other, 1, area_count)
+    other, signal = finish_other(plan, keep, carried, gots)
+    other = swap(other, 1, area_count)
+    membrane, cycle_out, own = finish_own(plan, neurons, keep, carried, signal, gots)
+    lfp = own + other
     width = plan.width
     lfp = [lfp[:, group * width : (group + 1) * width] for group in range(plan.groups)]
     lfp = jnp.concatenate(lfp, axis=0)[:share]

time: 33.2 us -> 32.3 us (0.973)
  waiting for transfers between devices: 8.72 us -> 6.49 us
  starting transfers between devices: 12.3 us -> 13.4 us
    ppermute x0 -> x3, starting transfers between devices: none -> 6.18 us  [body(): lax.ppermute(facts, 'area', plan.ring(shift))]
    ppermute x10 -> x7, starting transfers between devices: 12.3 us -> 7.2 us  [swap(): lax.ppermute(values, 'area', [(i, i ^ bit) for i in range(area_count)])]
    ppermute x10 -> x7, waiting for transfers between devices: 8.72 us -> 6.48 us  [swap(): lax.ppermute(values, 'area', [(i, i ^ bit) for i in range(area_count)])]
    pallas_call x1 -> x2, Pallas kernels: 1.32 us -> 1.59 us  [the longest x1 0.98 us: finish_own(): pl.pallas_call(functools.partial(own_kernel, plan), out_shape=(jax.ShapeD...]
  transfers between devices with their start and end apart: 10 -> 10, of which waited for: 6 -> 4; matrix products, arithmetic and copies ran while one was open for 0% -> 0% of each run, Pallas kernels for 22% -> 26%
where the time goes in v8:
time: 32.3 us; the launch traced here: 32.1 us
  starting transfers between devices  13.4 us (41%)
  Pallas kernels  10.7 us (33%)
  waiting for transfers between devices  6.49 us (20%)
  between operations  0.8 us (2%)
  other arithmetic  0.61 us (2%)
    ppermute x7, starting transfers between devices, swap(): lax.ppermute(values, 'area', [(i, i ^ bit) for i in range(area_count)])  7.2 us
    ppermute x7, waiting for transfers between devices, swap(): lax.ppermute(values, 'area', [(i, i ^ bit) for i in range(area_count)])  6.48 us
    ppermute x3, starting transfers between devices, body(): lax.ppermute(facts, 'area', plan.ring(shift))  6.18 us
    pallas_call x1, Pallas kernels, payload_sums(): pl.pallas_call(functools.partial(payload_kernel, plan), out_shape=(half,...  5.19 us
    pallas_call x1, Pallas kernels, known_lfp(): pl.pallas_call(functools.partial(known_kernel, plan), out_shape=(jax.Shap...  2.23 us
    pallas_call x1, Pallas kernels, facts_of(): pl.pallas_call(functools.partial(facts_kernel, plan), out_shape=(pltpu.VM...  1 us
    pallas_call x1, Pallas kernels, finish_own(): pl.pallas_call(functools.partial(own_kernel, plan), out_shape=(jax.ShapeD...  0.98 us
  transfers between devices with their start and end apart: 10, of which 4 were waited for; matrix products, arithmetic and copies ran while one was open for 0% of the time, Pallas kernels for 26%

profile of v8, /device:TPU:0, one launch (start us, length us, event | category | flops | bytes accessed | tf_op | source)
XLA Modules:
  0.0 32.1 jit_solution(7640114043102964500)
XLA Ops:
  0.6 0.0 copy-start.2
  0.6 0.0 copy-start.4
  0.7 0.0 copy-start.1
  0.7 0.0 copy-start
  0.7 0.0 copy-start.3
  0.7 1.0 %facts.1 = (f32[24,128]{1,0:T(8,128)S(1)}, s32[48,384]{1,0:T(8,128)S(1)}) custom-call(s32[10,4,384]{2,1,0:T(4,128)} %bitcast.13, f32[384]{0:T(512)} %leak.1, s32[384]{0:T(512)} %population.3, s32[96]{0:T(128)} %bitcast.15, s32[96]{0:T(128)} %target_block.1, s32[96]{0:T(128)} %delay_slot.1), custom_call_target="tpu_custom_call" | custom-call | tf_op jit(solution)/shard_map/facts/pallas_call | solution.py:125
  1.7 2.5 %collective-permute-start.1 = (f32[24,128]{1,0:T(8,128)S(1)}, f32[24,128]{1,0:T(8,128)S(1)}, u32[]{:S(2)}, u32[]{:S(2)}) collective-permute-start(f32[24,128]{1,0:T(8,128)S(1)} %get-tuple-element.26), channel_id=1, source_target_pairs={{0,5},{1,4},{2,7},{3,6},{4,8},{5,9},{6,10},{7,11},{8,13},{9,12},{1... | collective-permute-start | bytes 36872 | tf_op jit(solution)/shard_map/ppermute | solution.py:659
  4.2 2.9 %collective-permute-start.2 = (f32[24,128]{1,0:T(8,128)S(1)}, f32[24,128]{1,0:T(8,128)S(1)}, u32[]{:S(2)}, u32[]{:S(2)}) collective-permute-start(f32[24,128]{1,0:T(8,128)S(1)} %get-tuple-element.26), channel_id=1, source_target_pairs={{0,9},{1,8},{2,11},{3,10},{4,13},{5,12},{6,15},{7,14},{8,1},{9,0},... | collective-permute-start | bytes 36872 | tf_op jit(solution)/shard_map/ppermute | solution.py:659
  7.1 0.8 %collective-permute-start.3 = (f32[24,128]{1,0:T(8,128)S(1)}, f32[24,128]{1,0:T(8,128)S(1)}, u32[]{:S(2)}, u32[]{:S(2)}) collective-permute-start(f32[24,128]{1,0:T(8,128)S(1)} %get-tuple-element.26), channel_id=1, source_target_pairs={{0,12},{1,13},{2,14},{3,15},{4,1},{5,0},{6,3},{7,2},{8,4},{9,5},{1... | collective-permute-start | bytes 36872 | tf_op jit(solution)/shard_map/ppermute | solution.py:659
  7.9 5.2 %payload.1 = (f32[24,56,128]{2,1,0:T(8,128)S(1)}, f32[24,56,128]{2,1,0:T(8,128)}, f32[8,128]{1,0:T(8,128)S(1)}) custom-call(s32[48,384]{1,0:T(8,128)S(1)} %get-tuple-element.23.given, bf16[96,384,128]{2,1,0:T(8,128)(2,1)} %weights.1), custom_call_target="tpu_custom_call" | custom-call | tf_op jit(solution)/shard_map/payload/pallas_call | solution.py:195
  13.1 0.7 %collective-permute-start = (f32[24,56,128]{2,1,0:T(8,128)}, f32[24,56,128]{2,1,0:T(8,128)S(1)}, u32[]{:S(2)}, u32[]{:S(2)}) collective-permute-start(f32[24,56,128]{2,1,0:T(8,128)} %get-tuple-element.25), channel_id=1, source_target_pairs={{0,1},{1,0},{2,3},{3,2},{4,5},{5,4},{6,7},{7,6},{8,9},{9,8},{10,11... | collective-permute-start | bytes 2064392 | tf_op jit(solution)/shard_map/ppermute | solution.py:627
  13.8 0.0 collective-permute-done.1
  13.8 0.0 collective-permute-done.2
  13.8 0.0 collective-permute-done.3
  13.9 1.6 %collective-permute-start.4 = (f32[112,128]{1,0:T(8,128)S(1)}, f32[112,128]{1,0:T(8,128)S(1)}, u32[]{:S(2)}, u32[]{:S(2)}) collective-permute-start(f32[112,128]{1,0:T(8,128)S(1)} %constant_dynamic-update-slice_fusion.near), channel_id=1, source_target_pairs={{0,2},{1,3},{2,0},{3,1},{4,6},{5,7},{6,4},{7,5},{8,10},{9,11},{10,... | collective-permute-start | bytes 172040 | tf_op jit(solution)/shard_map/ppermute | solution.py:627
  15.4 0.0 copy-done.4
  15.5 0.0 copy-done.2
  15.5 0.0 copy-done.1
  15.5 0.0 copy-done
  15.5 2.2 %known_lfp.1 = (f32[384,128]{1,0:T(8,128)S(1)}, f32[16,8,128]{2,1,0:T(8,128)S(1)}) custom-call(s32[48,384]{1,0:T(8,128)S(1)} %get-tuple-element.23.given, s32[384]{0:T(512)S(1)} %copy-done.2, f32[4,2,4,256]{3,2,1,0:T(4,128)S(1)} %copy-done.1, bf16[384,4,2,256]{3,2,1,0:T(2,128)(2,1)S(1)} %copy-done), custom_call_target="tpu_custom_call" | custom-call | tf_op jit(solution)/shard_map/known_lfp/pallas_call | solution.py:288
  17.8 0.4 %collective-permute-done.4.far = f32[112,128]{1,0:T(8,128)S(1)} collective-permute-done((f32[112,128]{1,0:T(8,128)S(1)}, f32[112,128]{1,0:T(8,128)S(1)}, u32[]{:S(2)}, u32[]{:S(2)}) %collective-permute-start.4) | collective-permute-done | bytes 57376 | tf_op jit(solution)/shard_map/ppermute | solution.py:627
  18.1 0.0 collective-permute-done.got
  18.1 0.0 copy-done.3
  18.1 0.5 %compress.1 = (f32[360,128]{1,0:T(8,128)S(1)}, bf16[416,128]{1,0:T(8,128)(2,1)S(1)}, bf16[128,128]{1,0:T(8,128)(2,1)S(1)}) custom-call(f32[24,56,128]{2,1,0:T(8,128)S(1)} %get-tuple-element.24.mine, f32[24,56,128]{2,1,0:T(8,128)S(1)} %collective-permute-done.got, f32[112,128]{1,0:T(8,128)S(1)} %constant_dynamic-update-slice_fusion.near, ...), custom_call_target="tpu_custom_call" | custom-call | tf_op jit(solution)/shard_map/compress/pallas_call | solution.py:418
  18.7 1.5 %collective-permute-start.5 = (bf16[416,128]{1,0:T(8,128)(2,1)S(1)}, bf16[416,128]{1,0:T(8,128)(2,1)S(1)}, u32[]{:S(2)}, u32[]{:S(2)}) collective-permute-start(bf16[416,128]{1,0:T(8,128)(2,1)S(1)} %get-tuple-element.31), channel_id=1, source_target_pairs={{0,2},{1,3},{2,0},{3,1},{4,6},{5,7},{6,4},{7,5},{8,10},{9,11},{10,... | collective-permute-start | bytes 319496 | tf_op jit(solution)/shard_map/ppermute | solution.py:627
  20.2 3.2 %collective-permute-done.5.got = bf16[416,128]{1,0:T(8,128)(2,1)S(1)} collective-permute-done((bf16[416,128]{1,0:T(8,128)(2,1)S(1)}, bf16[416,128]{1,0:T(8,128)(2,1)S(1)}, u32[]{:S(2)}, u32[]{:S(2)}) %collective-permute-start.5) | collective-permute-done | bytes 106528 | tf_op jit(solution)/shard_map/ppermute | solution.py:627
  23.4 0.2 fold.1
  23.6 0.1 collective-permute-start.6
  23.7 0.9 %collective-permute-start.7 = (bf16[128,128]{1,0:T(8,128)(2,1)S(1)}, bf16[128,128]{1,0:T(8,128)(2,1)S(1)}, u32[]{:S(2)}, u32[]{:S(2)}) collective-permute-start(bf16[128,128]{1,0:T(8,128)(2,1)S(1)} %get-tuple-element.36), channel_id=1, source_target_pairs={{0,12},{1,13},{2,14},{3,15},{4,8},{5,9},{6,10},{7,11},{8,4},{9,5},... | collective-permute-start | bytes 98312 | tf_op jit(solution)/shard_map/ppermute | solution.py:627
  24.6 2.0 %collective-permute-start.8 = (bf16[128,128]{1,0:T(8,128)(2,1)S(1)}, bf16[128,128]{1,0:T(8,128)(2,1)S(1)}, u32[]{:S(2)}, u32[]{:S(2)}) collective-permute-start(bf16[128,128]{1,0:T(8,128)(2,1)S(1)} %get-tuple-element.37), channel_id=1, source_target_pairs={{0,5},{1,4},{2,7},{3,6},{4,1},{5,0},{6,3},{7,2},{8,13},{9,12},{10,... | collective-permute-start | bytes 98312 | tf_op jit(solution)/shard_map/ppermute | solution.py:627
  26.6 2.2 %collective-permute-done.6.refs_0_ = bf16[128,128]{1,0:T(8,128)(2,1)S(1)} collective-permute-done((bf16[128,128]{1,0:T(8,128)(2,1)S(1)}, bf16[128,128]{1,0:T(8,128)(2,1)S(1)}, u32[]{:S(2)}, u32[]{:S(2)}) %collective-permute-start.6) | collective-permute-done | bytes 32800 | tf_op jit(solution)/shard_map/ppermute | solution.py:627
  28.8 0.7 %collective-permute-done.7.refs_1_ = bf16[128,128]{1,0:T(8,128)(2,1)S(1)} collective-permute-done((bf16[128,128]{1,0:T(8,128)(2,1)S(1)}, bf16[128,128]{1,0:T(8,128)(2,1)S(1)}, u32[]{:S(2)}, u32[]{:S(2)}) %collective-permute-start.7) | collective-permute-done | bytes 32800 | tf_op jit(solution)/shard_map/ppermute | solution.py:627
  29.5 0.0 collective-permute-done.8.refs_2_
  29.5 0.6 %finish_other.1 = (f32[8,128]{1,0:T(8,128)S(1)}, f32[40,128]{1,0:T(8,128)S(1)}) custom-call(f32[120,128]{1,0:T(8,128)S(1)} %get-tuple-element.33.held, bf16[128,128]{1,0:T(8,128)(2,1)S(1)} %get-tuple-element.34.carried, bf16[128,128]{1,0:T(8,128)(2,1)S(1)} %collective-permute-done.6.refs_0_, bf16[128,128]{1,0:T(8,128)(2,1)S(1)} %collective-permute-done.7.refs_1_, ...), custom_call_target="tpu_custom_call" | custom-call | tf_op jit(solution)/shard_map/finish_other/pallas_call | solution.py:595
  30.1 0.4 %collective-permute-start.9 = (f32[8,128]{1,0:T(8,128)S(1)}, f32[8,128]{1,0:T(8,128)S(1)}, u32[]{:S(2)}, u32[]{:S(2)}) collective-permute-start(f32[8,128]{1,0:T(8,128)S(1)} %get-tuple-element.42), channel_id=1, source_target_pairs={{0,1},{1,0},{2,3},{3,2},{4,5},{5,4},{6,7},{7,6},{8,9},{9,8},{10,11... | collective-permute-start | bytes 12296 | tf_op jit(solution)/shard_map/ppermute | solution.py:627
  30.5 1.0 %finish_own.1 = (f32[4,384]{1,0:T(4,128)}, f32[4,4,384]{2,1,0:T(4,128)}, f32[8,128]{1,0:T(8,128)S(1)}) custom-call(f32[120,128]{1,0:T(8,128)S(1)} %get-tuple-element.33.held, bf16[128,128]{1,0:T(8,128)(2,1)S(1)} %get-tuple-element.34.carried, f32[40,128]{1,0:T(8,128)S(1)} %get-tuple-element.38.signal_in, ...), custom_call_target="tpu_custom_call" | custom-call | tf_op jit(solution)/shard_map/finish_own/pallas_call | solution.py:611
  31.5 0.0 collective-permute-done.9
  31.5 0.1 fusion
  31.5 0.6 %pad_maximum_fusion = f32[24,40]{1,0:T(8,128)} fusion(f32[8,40]{1,0:T(8,128)S(1)} %get-tuple-element.44, f32[8,40]{1,0:T(8,128)S(1)} %get-tuple-element.45, f32[8,40]{1,0:T(8,128)S(1)} %get-tuple-element.43), kind=kLoop, calls=%fused_computation.7 | loop fusion | flops 1920 | bytes 7680 | tf_op jit(solution)/shard_map/concatenate | solution.py:699
  (10 shorter events, 0.1 us)
Async XLA Ops:
  0.6 14.9 %copy-start.2 = (s32[384]{0:T(512)S(1)}, s32[384]{0:T(512)}, u32[]{:S(2)}) copy-start(s32[384]{0:T(512)} %population.3) | copy-start | bytes 4612
  0.6 14.8 %copy-start.4 = (f32[4,4,384]{2,1,0:T(4,128)S(1)}, f32[4,4,384]{2,1,0:T(4,128)}, u32[]{:S(2)}) copy-start(f32[4,4,384]{2,1,0:T(4,128)} %param.19) | copy-start | bytes 73732
  0.7 14.9 %copy-start.1 = (f32[4,2,4,256]{3,2,1,0:T(4,128)S(1)}, f32[4,2,4,256]{3,2,1,0:T(4,128)}, u32[]{:S(2)}) copy-start(f32[4,2,4,256]{3,2,1,0:T(4,128)} %history.1) | copy-start | bytes 98308
  0.7 14.9 %copy-start = (bf16[384,4,2,256]{3,2,1,0:T(2,128)(2,1)S(1)}, bf16[384,4,2,256]{3,2,1,0:T(2,128)(2,1)}, u32[]{:S(2)}) copy-start(bf16[384,4,2,256]{3,2,1,0:T(2,128)(2,1)} %kernel.1) | copy-start | bytes 4718596
  0.7 17.5 %copy-start.3 = (f32[4,384]{1,0:T(4,128)S(1)}, f32[4,384]{1,0:T(4,128)}, u32[]{:S(2)}) copy-start(f32[4,384]{1,0:T(4,128)} %param.18) | copy-start | bytes 18436
  1.7 12.1 %collective-permute-start.1 = (f32[24,128]{1,0:T(8,128)S(1)}, f32[24,128]{1,0:T(8,128)S(1)}, u32[]{:S(2)}, u32[]{:S(2)}) collective-permute-start(f32[24,128]{1,0:T(8,128)S(1)} %get-tuple-element.26), channel_id=1, source_target_pairs={{0,5},{1,4},{2,7},{3,6},{4,8},{5,9},{6,10},{7,11},{8,13},{9,12},{1... | collective-permute-start | bytes 36872 | tf_op jit(solution)/shard_map/ppermute | solution.py:659
  4.2 9.6 %collective-permute-start.2 = (f32[24,128]{1,0:T(8,128)S(1)}, f32[24,128]{1,0:T(8,128)S(1)}, u32[]{:S(2)}, u32[]{:S(2)}) collective-permute-start(f32[24,128]{1,0:T(8,128)S(1)} %get-tuple-element.26), channel_id=1, source_target_pairs={{0,9},{1,8},{2,11},{3,10},{4,13},{5,12},{6,15},{7,14},{8,1},{9,0},... | collective-permute-start | bytes 36872 | tf_op jit(solution)/shard_map/ppermute | solution.py:659
  7.1 6.8 %collective-permute-start.3 = (f32[24,128]{1,0:T(8,128)S(1)}, f32[24,128]{1,0:T(8,128)S(1)}, u32[]{:S(2)}, u32[]{:S(2)}) collective-permute-start(f32[24,128]{1,0:T(8,128)S(1)} %get-tuple-element.26), channel_id=1, source_target_pairs={{0,12},{1,13},{2,14},{3,15},{4,1},{5,0},{6,3},{7,2},{8,4},{9,5},{1... | collective-permute-start | bytes 36872 | tf_op jit(solution)/shard_map/ppermute | solution.py:659
  13.1 5.1 %collective-permute-start = (f32[24,56,128]{2,1,0:T(8,128)}, f32[24,56,128]{2,1,0:T(8,128)S(1)}, u32[]{:S(2)}, u32[]{:S(2)}) collective-permute-start(f32[24,56,128]{2,1,0:T(8,128)} %get-tuple-element.25), channel_id=1, source_target_pairs={{0,1},{1,0},{2,3},{3,2},{4,5},{5,4},{6,7},{7,6},{8,9},{9,8},{10,11... | collective-permute-start | bytes 2064392 | tf_op jit(solution)/shard_map/ppermute | solution.py:627
  13.9 4.2 %collective-permute-start.4 = (f32[112,128]{1,0:T(8,128)S(1)}, f32[112,128]{1,0:T(8,128)S(1)}, u32[]{:S(2)}, u32[]{:S(2)}) collective-permute-start(f32[112,128]{1,0:T(8,128)S(1)} %constant_dynamic-update-slice_fusion.near), channel_id=1, source_target_pairs={{0,2},{1,3},{2,0},{3,1},{4,6},{5,7},{6,4},{7,5},{8,10},{9,11},{10,... | collective-permute-start | bytes 172040 | tf_op jit(solution)/shard_map/ppermute | solution.py:627
  18.7 4.8 %collective-permute-start.5 = (bf16[416,128]{1,0:T(8,128)(2,1)S(1)}, bf16[416,128]{1,0:T(8,128)(2,1)S(1)}, u32[]{:S(2)}, u32[]{:S(2)}) collective-permute-start(bf16[416,128]{1,0:T(8,128)(2,1)S(1)} %get-tuple-element.31), channel_id=1, source_target_pairs={{0,2},{1,3},{2,0},{3,1},{4,6},{5,7},{6,4},{7,5},{8,10},{9,11},{10,... | collective-permute-start | bytes 319496 | tf_op jit(solution)/shard_map/ppermute | solution.py:627
  23.6 5.2 %collective-permute-start.6 = (bf16[128,128]{1,0:T(8,128)(2,1)S(1)}, bf16[128,128]{1,0:T(8,128)(2,1)S(1)}, u32[]{:S(2)}, u32[]{:S(2)}) collective-permute-start(bf16[128,128]{1,0:T(8,128)(2,1)S(1)} %get-tuple-element.35), channel_id=1, source_target_pairs={{0,9},{1,8},{2,11},{3,10},{4,13},{5,12},{6,15},{7,14},{8,1},{9,0},... | collective-permute-start | bytes 98312 | tf_op jit(solution)/shard_map/ppermute | solution.py:627
  23.7 5.8 %collective-permute-start.7 = (bf16[128,128]{1,0:T(8,128)(2,1)S(1)}, bf16[128,128]{1,0:T(8,128)(2,1)S(1)}, u32[]{:S(2)}, u32[]{:S(2)}) collective-permute-start(bf16[128,128]{1,0:T(8,128)(2,1)S(1)} %get-tuple-element.36), channel_id=1, source_target_pairs={{0,12},{1,13},{2,14},{3,15},{4,8},{5,9},{6,10},{7,11},{8,4},{9,5},... | collective-permute-start | bytes 98312 | tf_op jit(solution)/shard_map/ppermute | solution.py:627
  24.6 4.9 %collective-permute-start.8 = (bf16[128,128]{1,0:T(8,128)(2,1)S(1)}, bf16[128,128]{1,0:T(8,128)(2,1)S(1)}, u32[]{:S(2)}, u32[]{:S(2)}) collective-permute-start(bf16[128,128]{1,0:T(8,128)(2,1)S(1)} %get-tuple-element.37), channel_id=1, source_target_pairs={{0,5},{1,4},{2,7},{3,6},{4,1},{5,0},{6,3},{7,2},{8,13},{9,12},{10,... | collective-permute-start | bytes 98312 | tf_op jit(solution)/shard_map/ppermute | solution.py:627
  30.1 1.4 %collective-permute-start.9 = (f32[8,128]{1,0:T(8,128)S(1)}, f32[8,128]{1,0:T(8,128)S(1)}, u32[]{:S(2)}, u32[]{:S(2)}) collective-permute-start(f32[8,128]{1,0:T(8,128)S(1)} %get-tuple-element.42), channel_id=1, source_target_pairs={{0,1},{1,0},{2,3},{3,2},{4,5},{5,4},{6,7},{7,6},{8,9},{9,8},{10,11... | collective-permute-start | bytes 12296 | tf_op jit(solution)/shard_map/ppermute | solution.py:627

commit v9 on v8

--- a/solution.py
+++ b/solution.py
@@ -109,9 +109,10 @@
     for step in range(steps):
         last = jnp.where(spikes[step] > 0, step, last)
         given[step * trials : (step + 1) * trials] = spikes[step]
-    blank = jnp.zeros((6 - trials, last.shape[1]), F32)
-    rows = [last.astype(F32), leak[...].reshape(1, -1), population[...].astype(F32).reshape(1, -1)]
-    rows = jnp.concatenate(rows + [blank], axis=0)
+    high, low = both(leak[...].reshape(1, -1))
+    blank = jnp.zeros((5 - trials, last.shape[1]), F32)
+    rows = [last.astype(F32), high, low, population[...].astype(F32).reshape(1, -1), blank]
+    rows = jnp.concatenate(rows, axis=0)
     for block in range(plan.blocks):
         out[block * 8 : block * 8 + 8] = rows[:, block * 128 : block * 128 + 128]
     given[plan.width :] = jnp.zeros((given.shape[0] - plan.width, given.shape[1]), jnp.int32)
@@ -351,8 +352,8 @@
                 spot = pl.multiple_of((source * blocks + block) * 8, 8)
                 facts = (far if bit else near)[pl.ds(spot, 8)]
                 last = facts[0:trials]
-                leak = facts[trials : trials + 1]
-                population = facts[trials + 1 : trials + 2]
+                leak = facts[trials : trials + 1] + facts[trials + 1 : trials + 2]
+                population = facts[trials + 2 : trials + 3]
                 membrane = own * start[block]
                 for step in range(steps):
                     current = arriving[step * trials : (step + 1) * trials]
@@ -658,12 +659,12 @@
     size = facts.shape[0]
     facts = [facts] + [lax.ppermute(facts, "area", plan.ring(shift)) for shift in RING]
     mine, goes, token = payload_sums(plan, given, weights)
-    got = swap(goes, 1, area_count)
     blank = jnp.zeros((max(0, PAD - 4 * size - token.shape[0]), 128), F32)
     near = jnp.concatenate(facts + [token, blank])
+    near, goes = lax.optimization_barrier((near, goes))
     count, lane = 4 * size, quarter // 2
     while True:
-        more = swap(near, plan.mask(lane), area_count)
+        more = swap(near.astype(BF16), plan.mask(lane), area_count).astype(F32)
         if lane == 1:
             break
         near = jnp.stack(
@@ -671,6 +672,7 @@
         ).reshape(-1, 128)
         count, lane = 2 * count, lane // 2
 
+    got = swap(goes, 1, area_count)
     known, first = known_lfp(plan, given, population, history, lfp_kernel)
     known = known.reshape(area_count, share, 128)
     known = jnp.pad(known, ((0, 0), (0, plan.groups * 8 - share), (0, 0)))
@@ -693,10 +695,9 @@
     other, signal = finish_other(plan, keep, carried, gots)
     other = swap(other, 1, area_count)
     membrane, cycle_out, own = finish_own(plan, neurons, keep, carried, signal, gots)
-    lfp = own + other
     width = plan.width
-    lfp = [lfp[:, group * width : (group + 1) * width] for group in range(plan.groups)]
-    lfp = jnp.concatenate(lfp, axis=0)[:share]
+    lanes = [slice(group * width, (group + 1) * width) for group in range(plan.groups)]
+    lfp = jnp.concatenate([own[:, part] + other[:, part] for part in lanes])[:share]
     return membrane, cycle_out, lfp
 
 

time: 32.3 us -> 32 us (level)
  no operation moved by 1% of the time
where the time goes in v9:
time: 32 us; the launch traced here: 31.8 us
  starting transfers between devices  13.3 us (42%)
  Pallas kernels  10.7 us (33%)
  waiting for transfers between devices  6.24 us (20%)
  between operations  0.82 us (3%)
  other arithmetic  0.69 us (2%)
    ppermute x7, starting transfers between devices, swap(): lax.ppermute(values, 'area', [(i, i ^ bit) for i in range(area_count)])  7.08 us
    ppermute x7, waiting for transfers between devices, swap(): lax.ppermute(values, 'area', [(i, i ^ bit) for i in range(area_count)])  6.23 us
    ppermute x3, starting transfers between devices, body(): lax.ppermute(facts, 'area', plan.ring(shift))  6.18 us
    pallas_call x1, Pallas kernels, payload_sums(): pl.pallas_call(functools.partial(payload_kernel, plan), out_shape=(half,...  5.18 us
    pallas_call x1, Pallas kernels, known_lfp(): pl.pallas_call(functools.partial(known_kernel, plan), out_shape=(jax.Shap...  2.23 us
    pallas_call x1, Pallas kernels, facts_of(): pl.pallas_call(functools.partial(facts_kernel, plan), out_shape=(pltpu.VM...  1.01 us
    pallas_call x1, Pallas kernels, finish_own(): pl.pallas_call(functools.partial(own_kernel, plan), out_shape=(jax.ShapeD...  0.98 us
  transfers between devices with their start and end apart: 10, of which 4 were waited for; matrix products, arithmetic and copies ran while one was open for 0% of the time, Pallas kernels for 26%

profile of v9, /device:TPU:0, one launch (start us, length us, event | category | flops | bytes accessed | tf_op | source)
XLA Modules:
  0.0 31.8 jit_solution(9669960634303652465)
XLA Ops:
  0.6 0.0 copy-start.2
  0.6 0.0 copy-start.4
  0.7 0.0 copy-start.1
  0.7 0.0 copy-start
  0.7 0.0 copy-start.3
  0.7 1.0 %facts.1 = (f32[24,128]{1,0:T(8,128)S(1)}, s32[48,384]{1,0:T(8,128)S(1)}) custom-call(s32[10,4,384]{2,1,0:T(4,128)} %bitcast.13, f32[384]{0:T(512)} %leak.1, s32[384]{0:T(512)} %population.3, s32[96]{0:T(128)} %bitcast.15, s32[96]{0:T(128)} %target_block.1, s32[96]{0:T(128)} %delay_slot.1), custom_call_target="tpu_custom_call" | custom-call | tf_op jit(solution)/shard_map/facts/pallas_call | solution.py:126
  1.7 2.5 %collective-permute-start = (f32[24,128]{1,0:T(8,128)S(1)}, f32[24,128]{1,0:T(8,128)S(1)}, u32[]{:S(2)}, u32[]{:S(2)}) collective-permute-start(f32[24,128]{1,0:T(8,128)S(1)} %get-tuple-element.27), channel_id=1, source_target_pairs={{0,5},{1,4},{2,7},{3,6},{4,8},{5,9},{6,10},{7,11},{8,13},{9,12},{1... | collective-permute-start | bytes 36872 | tf_op jit(solution)/shard_map/ppermute | solution.py:660
  4.2 2.9 %collective-permute-start.1 = (f32[24,128]{1,0:T(8,128)S(1)}, f32[24,128]{1,0:T(8,128)S(1)}, u32[]{:S(2)}, u32[]{:S(2)}) collective-permute-start(f32[24,128]{1,0:T(8,128)S(1)} %get-tuple-element.27), channel_id=1, source_target_pairs={{0,9},{1,8},{2,11},{3,10},{4,13},{5,12},{6,15},{7,14},{8,1},{9,0},... | collective-permute-start | bytes 36872 | tf_op jit(solution)/shard_map/ppermute | solution.py:660
  7.1 0.8 %collective-permute-start.2 = (f32[24,128]{1,0:T(8,128)S(1)}, f32[24,128]{1,0:T(8,128)S(1)}, u32[]{:S(2)}, u32[]{:S(2)}) collective-permute-start(f32[24,128]{1,0:T(8,128)S(1)} %get-tuple-element.27), channel_id=1, source_target_pairs={{0,12},{1,13},{2,14},{3,15},{4,1},{5,0},{6,3},{7,2},{8,4},{9,5},{1... | collective-permute-start | bytes 36872 | tf_op jit(solution)/shard_map/ppermute | solution.py:660
  7.9 5.2 %payload.1 = (f32[24,56,128]{2,1,0:T(8,128)S(1)}, f32[24,56,128]{2,1,0:T(8,128)}, f32[8,128]{1,0:T(8,128)S(1)}) custom-call(s32[48,384]{1,0:T(8,128)S(1)} %get-tuple-element.25.given, bf16[96,384,128]{2,1,0:T(8,128)(2,1)} %weights.1), custom_call_target="tpu_custom_call" | custom-call | tf_op jit(solution)/shard_map/payload/pallas_call | solution.py:196
  13.1 0.0 collective-permute-done
  13.1 0.0 collective-permute-done.1
  13.1 0.0 collective-permute-done.2
  13.2 0.7 %collective-permute-start.3 = (f32[24,56,128]{2,1,0:T(8,128)}, f32[24,56,128]{2,1,0:T(8,128)S(1)}, u32[]{:S(2)}, u32[]{:S(2)}) collective-permute-start(f32[24,56,128]{2,1,0:T(8,128)} %get-tuple-element.30), channel_id=1, source_target_pairs={{0,1},{1,0},{2,3},{3,2},{4,5},{5,4},{6,7},{7,6},{8,9},{9,8},{10,11... | collective-permute-start | bytes 2064392 | tf_op jit(solution)/shard_map/ppermute | solution.py:628
  13.9 1.5 %collective-permute-start.4 = (bf16[112,128]{1,0:T(8,128)(2,1)S(1)}, bf16[112,128]{1,0:T(8,128)(2,1)S(1)}, u32[]{:S(2)}, u32[]{:S(2)}) collective-permute-start(bf16[112,128]{1,0:T(8,128)(2,1)S(1)} %convert_element_type.6), channel_id=1, source_target_pairs={{0,2},{1,3},{2,0},{3,1},{4,6},{5,7},{6,4},{7,5},{8,10},{9,11},{10,... | collective-permute-start | bytes 86024 | tf_op jit(solution)/shard_map/ppermute | solution.py:628
  15.4 0.0 copy-done.4
  15.5 0.0 copy-done.2
  15.5 0.0 copy-done.1
  15.5 0.0 copy-done
  15.5 2.2 %known_lfp.1 = (f32[384,128]{1,0:T(8,128)S(1)}, f32[16,8,128]{2,1,0:T(8,128)S(1)}) custom-call(s32[48,384]{1,0:T(8,128)S(1)} %get-tuple-element.25.given, s32[384]{0:T(512)S(1)} %copy-done.2, f32[4,2,4,256]{3,2,1,0:T(4,128)S(1)} %copy-done.1, bf16[384,4,2,256]{3,2,1,0:T(2,128)(2,1)S(1)} %copy-done), custom_call_target="tpu_custom_call" | custom-call | tf_op jit(solution)/shard_map/known_lfp/pallas_call | solution.py:289
  17.7 0.1 collective-permute-done.4
  17.8 0.0 collective-permute-done.3.got
  17.8 0.0 copy-done.3
  17.8 0.5 %compress.1 = (f32[360,128]{1,0:T(8,128)S(1)}, bf16[416,128]{1,0:T(8,128)(2,1)S(1)}, bf16[128,128]{1,0:T(8,128)(2,1)S(1)}) custom-call(f32[24,56,128]{2,1,0:T(8,128)S(1)} %get-tuple-element.26.mine, f32[24,56,128]{2,1,0:T(8,128)S(1)} %collective-permute-done.3.got, f32[112,128]{1,0:T(8,128)S(1)} %constant_dynamic-update-slice_fusion.near, ...), custom_call_target="tpu_custom_call" | custom-call | tf_op jit(solution)/shard_map/compress/pallas_call | solution.py:419
  18.3 1.5 %collective-permute-start.5 = (bf16[416,128]{1,0:T(8,128)(2,1)S(1)}, bf16[416,128]{1,0:T(8,128)(2,1)S(1)}, u32[]{:S(2)}, u32[]{:S(2)}) collective-permute-start(bf16[416,128]{1,0:T(8,128)(2,1)S(1)} %get-tuple-element.35), channel_id=1, source_target_pairs={{0,2},{1,3},{2,0},{3,1},{4,6},{5,7},{6,4},{7,5},{8,10},{9,11},{10,... | collective-permute-start | bytes 319496 | tf_op jit(solution)/shard_map/ppermute | solution.py:628
  19.9 3.2 %collective-permute-done.5.got = bf16[416,128]{1,0:T(8,128)(2,1)S(1)} collective-permute-done((bf16[416,128]{1,0:T(8,128)(2,1)S(1)}, bf16[416,128]{1,0:T(8,128)(2,1)S(1)}, u32[]{:S(2)}, u32[]{:S(2)}) %collective-permute-start.5) | collective-permute-done | bytes 106528 | tf_op jit(solution)/shard_map/ppermute | solution.py:628
  23.1 0.2 fold.1
  23.3 0.1 collective-permute-start.6
  23.3 1.2 %collective-permute-start.7 = (bf16[128,128]{1,0:T(8,128)(2,1)S(1)}, bf16[128,128]{1,0:T(8,128)(2,1)S(1)}, u32[]{:S(2)}, u32[]{:S(2)}) collective-permute-start(bf16[128,128]{1,0:T(8,128)(2,1)S(1)} %get-tuple-element.40), channel_id=1, source_target_pairs={{0,12},{1,13},{2,14},{3,15},{4,8},{5,9},{6,10},{7,11},{8,4},{9,5},... | collective-permute-start | bytes 98312 | tf_op jit(solution)/shard_map/ppermute | solution.py:628
  24.6 1.7 %collective-permute-start.8 = (bf16[128,128]{1,0:T(8,128)(2,1)S(1)}, bf16[128,128]{1,0:T(8,128)(2,1)S(1)}, u32[]{:S(2)}, u32[]{:S(2)}) collective-permute-start(bf16[128,128]{1,0:T(8,128)(2,1)S(1)} %get-tuple-element.41), channel_id=1, source_target_pairs={{0,5},{1,4},{2,7},{3,6},{4,1},{5,0},{6,3},{7,2},{8,13},{9,12},{10,... | collective-permute-start | bytes 98312 | tf_op jit(solution)/shard_map/ppermute | solution.py:628
  26.3 2.3 %collective-permute-done.6.refs_0_ = bf16[128,128]{1,0:T(8,128)(2,1)S(1)} collective-permute-done((bf16[128,128]{1,0:T(8,128)(2,1)S(1)}, bf16[128,128]{1,0:T(8,128)(2,1)S(1)}, u32[]{:S(2)}, u32[]{:S(2)}) %collective-permute-start.6) | collective-permute-done | bytes 32800 | tf_op jit(solution)/shard_map/ppermute | solution.py:628
  28.5 0.7 %collective-permute-done.7.refs_1_ = bf16[128,128]{1,0:T(8,128)(2,1)S(1)} collective-permute-done((bf16[128,128]{1,0:T(8,128)(2,1)S(1)}, bf16[128,128]{1,0:T(8,128)(2,1)S(1)}, u32[]{:S(2)}, u32[]{:S(2)}) %collective-permute-start.7) | collective-permute-done | bytes 32800 | tf_op jit(solution)/shard_map/ppermute | solution.py:628
  29.2 0.0 collective-permute-done.8.refs_2_
  29.2 0.6 %finish_other.1 = (f32[8,128]{1,0:T(8,128)S(1)}, f32[40,128]{1,0:T(8,128)S(1)}) custom-call(f32[120,128]{1,0:T(8,128)S(1)} %get-tuple-element.37.held, bf16[128,128]{1,0:T(8,128)(2,1)S(1)} %get-tuple-element.38.carried, bf16[128,128]{1,0:T(8,128)(2,1)S(1)} %collective-permute-done.6.refs_0_, bf16[128,128]{1,0:T(8,128)(2,1)S(1)} %collective-permute-done.7.refs_1_, ...), custom_call_target="tpu_custom_call" | custom-call | tf_op jit(solution)/shard_map/finish_other/pallas_call | solution.py:596
  29.8 0.3 %collective-permute-start.9 = (f32[8,128]{1,0:T(8,128)S(1)}, f32[8,128]{1,0:T(8,128)S(1)}, u32[]{:S(2)}, u32[]{:S(2)}) collective-permute-start(f32[8,128]{1,0:T(8,128)S(1)} %get-tuple-element.46), channel_id=1, source_target_pairs={{0,1},{1,0},{2,3},{3,2},{4,5},{5,4},{6,7},{7,6},{8,9},{9,8},{10,11... | collective-permute-start | bytes 12296 | tf_op jit(solution)/shard_map/ppermute | solution.py:628
  30.2 1.0 %finish_own.1 = (f32[4,384]{1,0:T(4,128)}, f32[4,4,384]{2,1,0:T(4,128)}, f32[8,128]{1,0:T(8,128)S(1)}) custom-call(f32[120,128]{1,0:T(8,128)S(1)} %get-tuple-element.37.held, bf16[128,128]{1,0:T(8,128)(2,1)S(1)} %get-tuple-element.38.carried, f32[40,128]{1,0:T(8,128)S(1)} %get-tuple-element.42.signal_in, ...), custom_call_target="tpu_custom_call" | custom-call | tf_op jit(solution)/shard_map/finish_own/pallas_call | solution.py:612
  31.1 0.0 collective-permute-done.9
  31.1 0.1 slice_add_fusion.2
  31.2 0.6 %pad_maximum_fusion = f32[24,40]{1,0:T(8,128)} fusion(f32[8,40]{1,0:T(8,128)S(1)} %get-tuple-element.48, f32[8,40]{1,0:T(8,128)S(1)} %get-tuple-element.49, f32[8,40]{1,0:T(8,128)S(1)} %get-tuple-element.47), kind=kLoop, calls=%fused_computation.7 | loop fusion | flops 1920 | bytes 7680 | tf_op jit(solution)/shard_map/concatenate | solution.py:700
  (11 shorter events, 0.1 us)
Async XLA Ops:
  0.6 14.8 %copy-start.2 = (s32[384]{0:T(512)S(1)}, s32[384]{0:T(512)}, u32[]{:S(2)}) copy-start(s32[384]{0:T(512)} %population.3) | copy-start | bytes 4612
  0.6 14.8 %copy-start.4 = (f32[4,4,384]{2,1,0:T(4,128)S(1)}, f32[4,4,384]{2,1,0:T(4,128)}, u32[]{:S(2)}) copy-start(f32[4,4,384]{2,1,0:T(4,128)} %param.19) | copy-start | bytes 73732
  0.7 14.8 %copy-start.1 = (f32[4,2,4,256]{3,2,1,0:T(4,128)S(1)}, f32[4,2,4,256]{3,2,1,0:T(4,128)}, u32[]{:S(2)}) copy-start(f32[4,2,4,256]{3,2,1,0:T(4,128)} %history.1) | copy-start | bytes 98308
  0.7 14.8 %copy-start = (bf16[384,4,2,256]{3,2,1,0:T(2,128)(2,1)S(1)}, bf16[384,4,2,256]{3,2,1,0:T(2,128)(2,1)}, u32[]{:S(2)}) copy-start(bf16[384,4,2,256]{3,2,1,0:T(2,128)(2,1)} %kernel.1) | copy-start | bytes 4718596
  0.7 17.1 %copy-start.3 = (f32[4,384]{1,0:T(4,128)S(1)}, f32[4,384]{1,0:T(4,128)}, u32[]{:S(2)}) copy-start(f32[4,384]{1,0:T(4,128)} %param.18) | copy-start | bytes 18436
  1.7 11.4 %collective-permute-start = (f32[24,128]{1,0:T(8,128)S(1)}, f32[24,128]{1,0:T(8,128)S(1)}, u32[]{:S(2)}, u32[]{:S(2)}) collective-permute-start(f32[24,128]{1,0:T(8,128)S(1)} %get-tuple-element.27), channel_id=1, source_target_pairs={{0,5},{1,4},{2,7},{3,6},{4,8},{5,9},{6,10},{7,11},{8,13},{9,12},{1... | collective-permute-start | bytes 36872 | tf_op jit(solution)/shard_map/ppermute | solution.py:660
  4.2 8.9 %collective-permute-start.1 = (f32[24,128]{1,0:T(8,128)S(1)}, f32[24,128]{1,0:T(8,128)S(1)}, u32[]{:S(2)}, u32[]{:S(2)}) collective-permute-start(f32[24,128]{1,0:T(8,128)S(1)} %get-tuple-element.27), channel_id=1, source_target_pairs={{0,9},{1,8},{2,11},{3,10},{4,13},{5,12},{6,15},{7,14},{8,1},{9,0},... | collective-permute-start | bytes 36872 | tf_op jit(solution)/shard_map/ppermute | solution.py:660
  7.1 6.0 %collective-permute-start.2 = (f32[24,128]{1,0:T(8,128)S(1)}, f32[24,128]{1,0:T(8,128)S(1)}, u32[]{:S(2)}, u32[]{:S(2)}) collective-permute-start(f32[24,128]{1,0:T(8,128)S(1)} %get-tuple-element.27), channel_id=1, source_target_pairs={{0,12},{1,13},{2,14},{3,15},{4,1},{5,0},{6,3},{7,2},{8,4},{9,5},{1... | collective-permute-start | bytes 36872 | tf_op jit(solution)/shard_map/ppermute | solution.py:660
  13.2 4.6 %collective-permute-start.3 = (f32[24,56,128]{2,1,0:T(8,128)}, f32[24,56,128]{2,1,0:T(8,128)S(1)}, u32[]{:S(2)}, u32[]{:S(2)}) collective-permute-start(f32[24,56,128]{2,1,0:T(8,128)} %get-tuple-element.30), channel_id=1, source_target_pairs={{0,1},{1,0},{2,3},{3,2},{4,5},{5,4},{6,7},{7,6},{8,9},{9,8},{10,11... | collective-permute-start | bytes 2064392 | tf_op jit(solution)/shard_map/ppermute | solution.py:628
  13.9 3.9 %collective-permute-start.4 = (bf16[112,128]{1,0:T(8,128)(2,1)S(1)}, bf16[112,128]{1,0:T(8,128)(2,1)S(1)}, u32[]{:S(2)}, u32[]{:S(2)}) collective-permute-start(bf16[112,128]{1,0:T(8,128)(2,1)S(1)} %convert_element_type.6), channel_id=1, source_target_pairs={{0,2},{1,3},{2,0},{3,1},{4,6},{5,7},{6,4},{7,5},{8,10},{9,11},{10,... | collective-permute-start | bytes 86024 | tf_op jit(solution)/shard_map/ppermute | solution.py:628
  18.3 4.8 %collective-permute-start.5 = (bf16[416,128]{1,0:T(8,128)(2,1)S(1)}, bf16[416,128]{1,0:T(8,128)(2,1)S(1)}, u32[]{:S(2)}, u32[]{:S(2)}) collective-permute-start(bf16[416,128]{1,0:T(8,128)(2,1)S(1)} %get-tuple-element.35), channel_id=1, source_target_pairs={{0,2},{1,3},{2,0},{3,1},{4,6},{5,7},{6,4},{7,5},{8,10},{9,11},{10,... | collective-permute-start | bytes 319496 | tf_op jit(solution)/shard_map/ppermute | solution.py:628
  23.3 5.2 %collective-permute-start.6 = (bf16[128,128]{1,0:T(8,128)(2,1)S(1)}, bf16[128,128]{1,0:T(8,128)(2,1)S(1)}, u32[]{:S(2)}, u32[]{:S(2)}) collective-permute-start(bf16[128,128]{1,0:T(8,128)(2,1)S(1)} %get-tuple-element.39), channel_id=1, source_target_pairs={{0,9},{1,8},{2,11},{3,10},{4,13},{5,12},{6,15},{7,14},{8,1},{9,0},... | collective-permute-start | bytes 98312 | tf_op jit(solution)/shard_map/ppermute | solution.py:628
  23.3 5.9 %collective-permute-start.7 = (bf16[128,128]{1,0:T(8,128)(2,1)S(1)}, bf16[128,128]{1,0:T(8,128)(2,1)S(1)}, u32[]{:S(2)}, u32[]{:S(2)}) collective-permute-start(bf16[128,128]{1,0:T(8,128)(2,1)S(1)} %get-tuple-element.40), channel_id=1, source_target_pairs={{0,12},{1,13},{2,14},{3,15},{4,8},{5,9},{6,10},{7,11},{8,4},{9,5},... | collective-permute-start | bytes 98312 | tf_op jit(solution)/shard_map/ppermute | solution.py:628
  24.6 4.6 %collective-permute-start.8 = (bf16[128,128]{1,0:T(8,128)(2,1)S(1)}, bf16[128,128]{1,0:T(8,128)(2,1)S(1)}, u32[]{:S(2)}, u32[]{:S(2)}) collective-permute-start(bf16[128,128]{1,0:T(8,128)(2,1)S(1)} %get-tuple-element.41), channel_id=1, source_target_pairs={{0,5},{1,4},{2,7},{3,6},{4,1},{5,0},{6,3},{7,2},{8,13},{9,12},{10,... | collective-permute-start | bytes 98312 | tf_op jit(solution)/shard_map/ppermute | solution.py:628
  29.8 1.3 %collective-permute-start.9 = (f32[8,128]{1,0:T(8,128)S(1)}, f32[8,128]{1,0:T(8,128)S(1)}, u32[]{:S(2)}, u32[]{:S(2)}) collective-permute-start(f32[8,128]{1,0:T(8,128)S(1)} %get-tuple-element.46), channel_id=1, source_target_pairs={{0,1},{1,0},{2,3},{3,2},{4,5},{5,4},{6,7},{7,6},{8,9},{9,8},{10,11... | collective-permute-start | bytes 12296 | tf_op jit(solution)/shard_map/ppermute | solution.py:628
